TPU v7x, 512 devices: a whole 4x8x8 slice. The times are simulated.
512 devices in a mesh: group: 16 (over y, core), sub: 32 (over z, x).
Axes of the slice: x: 4, y: 8, z: 8, core: 2. Of those that a mesh axis runs over, the one named last changes fastest.
Arguments:
- right_side: float32 [262144, 128], P(('group', 'sub')), may hold values from -6 to 6
- mass: float32 [512, 512], P(('group', 'sub')), may hold values from 0.05 to 0.5
- block_values: float32 [262144, 512], P(('group', 'sub')), may hold values from 0.000390625 to 0.005859375
- block_cols: int32 [4096, 8], P(('group', 'sub')), may hold values from 0 to 7, as said below
- face_rows: int32 [512, 256], P(('group', 'sub')), may hold values from 0 to 511, as said below
- land_rows: int32 [512, 256], P(('group', 'sub')), may hold values from 0 to 511, as said below
- face_counts: int32 [512, 32], P(('group', 'sub')), may hold values from 0 to 8, as said below
- face_weight: float32 [512, 256], P(('group', 'sub')), may hold values from 0.3 to 3
- local_factor: float32 [262144, 128], P(('group', 'sub')), may hold values from -0.25 to 0.25
- basis: float32 [32768, 512], P(('group', 'sub')), may hold values from -0.25 to 0.25
- coarse_inverse: float32 [2048, 2048], P('sub'), may hold values from -1 to 2.5, as said below
Outputs:
- solution_field: float32 [262144, 128], P(('group', 'sub'))
- residual: float32 [262144, 128], P(('group', 'sub'))
Inputs may be any that keep to these rules, and one draw needn't show every extreme that they name: `block_cols`: for each k, the column blocks of a subdomain's 8 block rows are a permutation of 0 to 7. `face_rows`: the 256 entries of a subdomain are distinct local rows. `land_rows`: the 256 entries of a subdomain are distinct local rows. `face_counts`: every subdomain has 8 live slots toward at least one peer. `coarse_inverse`: symmetric positive definite.
All inputs are finite; a program needn't handle non-finite values.
Results may differ from a plain program's by a relative error of at most 0.0003.
Values sent between devices are 32-bit elements; how exact they have to be, the bound alone decides.
No kernel may reach another device: no remote copies, remote signals or barrier semaphores. Data moves between devices by JAX's collectives and lax.ppermute only.
A program may use at most 64 MiB of HBM per device.

v0:
```python
import jax
import jax.numpy as jnp
from jax import lax
from jax.sharding import PartitionSpec as P

ITERS = 3


highest = lax.Precision.HIGHEST


def local(
    right_side,
    mass,
    block_values,
    block_cols,
    face_rows,
    land_rows,
    face_counts,
    face_weight,
    local_factor,
    basis,
    coarse_inverse,
):
    n_rows, n_rhs = right_side.shape
    n_peers = lax.axis_size("sub")
    n_slots = face_rows.shape[1]
    per_peer = n_slots // n_peers
    n_blocks, n_stored = block_cols.shape
    block_rows = n_rows // n_blocks
    n_coarse = basis.shape[0]
    factor_rows = local_factor.shape[1]
    faces = face_rows[0]
    lands = land_rows[0]
    slot_ids = jnp.arange(n_slots)
    live = slot_ids % per_peer < face_counts[0][slot_ids // per_peer]
    weights = jnp.where(live, face_weight[0], jnp.float32(0.0))
    received = lax.all_to_all(weights, "sub", split_axis=0, concat_axis=0, tiled=True)
    values_r = block_values.reshape(n_blocks, block_rows, n_stored * block_rows)
    flat_cols = block_cols.reshape(-1)
    row_total = jnp.sum(block_values, axis=1)
    col_part = jnp.sum(values_r, axis=1).reshape(n_blocks * n_stored, block_rows)
    col_total = (
        jnp.zeros((n_blocks, block_rows), jnp.float32).at[flat_cols].add(col_part).reshape(n_rows)
    )
    degree = (row_total + col_total).at[faces].add(weights).at[lands].add(received)
    diag_col = (mass[0] + degree)[:, None]
    factor_r = local_factor.reshape(n_rows // factor_rows, factor_rows, factor_rows)

    def precondition(resid):
        jacobi = resid / diag_col
        blocks = resid.reshape(n_rows // factor_rows, factor_rows, n_rhs)
        inner = jnp.einsum("bij,bjc->bic", factor_r, blocks, precision=highest)
        local_part = jnp.einsum("bji,bjc->bic", factor_r, inner, precision=highest).reshape(
            n_rows, n_rhs
        )
        coarse_part = jnp.dot(basis, resid, precision=highest)
        total_coarse = coarse_inverse.shape[1]
        start = lax.axis_index("sub") * n_coarse
        padded = lax.dynamic_update_slice_in_dim(
            jnp.zeros((total_coarse, n_rhs), jnp.float32), coarse_part, start, 0
        )
        whole = lax.psum(padded, ("group", "sub"))
        solved = jnp.dot(coarse_inverse, whole, precision=highest)
        coarse_term = jnp.einsum("nr,nc->rc", basis, solved, precision=highest)
        return jacobi + local_part + coarse_term

    def residual_product(resid, zvalue):
        return lax.psum(jnp.sum(resid * zvalue, axis=0), ("group", "sub"))

    resid = right_side
    solution = jnp.zeros_like(right_side)
    zvalue = precondition(resid)
    direction = zvalue
    gamma = residual_product(resid, zvalue)
    for iteration in range(ITERS):
        got_out = lax.all_to_all(
            weights[:, None] * direction[faces], "sub", split_axis=0, concat_axis=0, tiled=True
        )
        got_back = lax.all_to_all(direction[lands], "sub", split_axis=0, concat_axis=0, tiled=True)
        operate_blocks = direction.reshape(n_blocks, block_rows, n_rhs)
        picked = operate_blocks[block_cols].reshape(n_blocks, n_stored * block_rows, n_rhs)
        forward = jnp.einsum("rik,rkc->ric", values_r, picked, precision=highest).reshape(
            n_rows, n_rhs
        )
        back_terms = jnp.einsum(
            "rik,ric->rkc", values_r, operate_blocks, precision=highest
        ).reshape(n_blocks * n_stored, block_rows, n_rhs)
        backward = (
            jnp.zeros((n_blocks, block_rows, n_rhs), jnp.float32)
            .at[flat_cols]
            .add(back_terms)
            .reshape(n_rows, n_rhs)
        )
        coupled = jnp.zeros((n_rows, n_rhs), jnp.float32).at[lands].add(got_out)
        coupled = coupled.at[faces].add(weights[:, None] * got_back)
        image = diag_col * direction - forward - backward - coupled
        alpha = gamma / lax.psum(jnp.sum(direction * image, axis=0), ("group", "sub"))
        solution = solution + alpha * direction
        resid = resid - alpha * image
        if iteration + 1 < ITERS:
            zvalue = precondition(resid)
            gamma_new = residual_product(resid, zvalue)
            direction = zvalue + gamma_new / gamma * direction
            gamma = gamma_new
    return (solution, resid)


def solution(mesh):
    placed = (
        P(("group", "sub"), None),
        P(("group", "sub"), None),
        P(("group", "sub"), None),
        P(("group", "sub"), None),
        P(("group", "sub"), None),
        P(("group", "sub"), None),
        P(("group", "sub"), None),
        P(("group", "sub"), None),
        P(("group", "sub"), None),
        P(("group", "sub"), None),
        P("sub", None),
    )
    return jax.shard_map(
        local,
        mesh=mesh,
        in_specs=placed,
        out_specs=(P(("group", "sub"), None), P(("group", "sub"), None)),
        check_vma=False,
    )
```

profile of v0, /device:TPU:1, one launch (start us, length us, event | category | flops | bytes accessed | tf_op | source)
XLA Modules:
  0.0 1505.7 jit_solution(3155422974275814790)
XLA Ops:
  7.2 2.1 fusion.37
  9.3 1.8 fusion.38
  11.5 5.2 compare_select_fusion.3
  16.7 16.3 %compare_select_fusion.11 = (f32[256]{0:T(256)S(1)}, s32[256]{0:T(256)S(1)}) fusion(f32[256]{0:T(256)} %bitcast.231, pred[256]{0:T(512)(128)(4,1)S(1)} %get-tuple-element.59, pred[256]{0:T(512)(128)(4,1)S(1)} %get-tuple-element.60, pred[256]{0:T(512)(128)(4,1)S(1)} %get-tuple-element.61, pred[256]{0:T(512)(128)(4,1)S(1)} %get-tuple-element.62, ...), kind=kLoop, calls=%fused_computation.136 | loop fusion | flops 8448 | bytes 10596 | tf_op jit(solution)/shard_map/jit(_where)/select_n | solution.py:37
  35.7 13.7 all-to-all-start
  55.7 2.3 scatter_fusion
  58.8 2.3 scatter_fusion.1
  61.1 268.2 %all-reduce.5.cloned.1.call-done = f32[2048,128]{1,0:T(8,128)} async-done(((f32[2048,128]{1,0:T(8,128)}), f32[2048,128]{1,0:T(8,128)}) %all-reduce.5.cloned.1.call-update) | async-done | bytes 1048592 | tf_op jit(solution)/shard_map/psum | solution.py:63
  329.4 2.0 fusion.41
  333.5 6.8 all-to-all-start.1
  340.3 3.2 convolution_bitcast_fusion.2
  343.5 2.9 copy.84
  346.4 7.0 scatter_fusion.2
  353.6 2.0 gather_fusion
  357.1 9.2 all-to-all-start.2
  366.4 3.2 fusion.42
  369.7 1.6 scatter_custom_fusion.4
  371.3 4.4 all-to-all-done.2
  375.7 2.3 scatter_custom_fusion.5
  378.9 97.2 %all-reduce = (f32[128]{0:T(128)S(1)}, f32[128]{0:T(128)S(1)}) all-reduce(f32[128]{0:T(128)} %get-tuple-element.9, f32[128]{0:T(128)} %get-tuple-element.8), channel_id=1, replica_groups=mesh['group'=16,'sub'=32] {'group','sub'}, use_global_device_ids=true, to_apply=%region_7.8 | all-reduce | flops 256 | bytes 2048 | tf_op jit(solution)/shard_map/psum | solution.py:69
  479.7 265.4 %all-reduce.7.cloned.1.call-done = f32[2048,128]{1,0:T(8,128)} async-done(((f32[2048,128]{1,0:T(8,128)}), f32[2048,128]{1,0:T(8,128)}) %all-reduce.7.cloned.1.call-update) | async-done | bytes 1048592 | tf_op jit(solution)/shard_map/psum | solution.py:63
  745.2 2.0 fusion.44
  747.7 97.2 %psum.67 = f32[128]{0:T(128)S(1)} all-reduce(f32[128]{0:T(128)S(1)} %get-tuple-element.53), channel_id=1, replica_groups=mesh['group'=16,'sub'=32] {'group','sub'}, use_global_device_ids=true, to_apply=%region_15.16 | all-reduce | flops 128 | bytes 1024 | tf_op jit(solution)/shard_map/psum | solution.py:69
  847.3 2.0 gather_fusion.3
  850.1 5.9 all-to-all-start.3
  856.0 3.2 convolution_bitcast_fusion.1
  859.1 2.9 copy.95
  862.1 7.0 scatter_fusion.3
  869.3 9.5 all-to-all-start.4
  878.9 3.2 fusion.45
  882.1 1.9 scatter_custom_fusion.7
  884.0 4.1 all-to-all-done.4
  888.1 2.5 scatter_custom_fusion.8
  891.4 95.4 %psum.68 = f32[128]{0:T(128)S(1)} all-reduce(f32[128]{0:T(128)} %get-tuple-element.14), channel_id=1, replica_groups=mesh['group'=16,'sub'=32] {'group','sub'}, use_global_device_ids=true, to_apply=%region_20.21 | all-reduce | flops 128 | bytes 1024 | tf_op jit(solution)/shard_map/psum | solution.py:98
  991.0 265.4 %all-reduce.9.cloned.1.call-done = f32[2048,128]{1,0:T(8,128)} async-done(((f32[2048,128]{1,0:T(8,128)}), f32[2048,128]{1,0:T(8,128)}) %all-reduce.9.cloned.1.call-update) | async-done | bytes 1048592 | tf_op jit(solution)/shard_map/psum | solution.py:63
  1256.4 2.0 fusion.47
  1258.9 97.4 %psum.70 = f32[128]{0:T(128)S(1)} all-reduce(f32[128]{0:T(128)S(1)} %get-tuple-element.55), channel_id=1, replica_groups=mesh['group'=16,'sub'=32] {'group','sub'}, use_global_device_ids=true, to_apply=%region_23.24 | all-reduce | flops 128 | bytes 1024 | tf_op jit(solution)/shard_map/psum | solution.py:69
  1358.7 2.0 gather_fusion.6
  1361.5 5.7 all-to-all-start.5
  1367.3 3.2 convolution_bitcast_fusion
  1370.4 2.9 copy.105
  1373.4 7.0 scatter_fusion.4
  1380.6 9.2 all-to-all-start.6
  1389.8 3.2 fusion.48
  1393.1 1.6 scatter_custom_fusion.10
  1394.8 4.4 all-to-all-done.6
  1399.2 2.3 scatter_custom_fusion.11
  1401.7 95.4 %psum.71 = f32[128]{0:T(128)S(1)} all-reduce(f32[128]{0:T(128)S(1)} %get-tuple-element.12), channel_id=1, replica_groups=mesh['group'=16,'sub'=32] {'group','sub'}, use_global_device_ids=true, to_apply=%region_28.29 | all-reduce | flops 128 | bytes 1024 | tf_op jit(solution)/shard_map/psum | solution.py:98
  (167 shorter events, 33.3 us)
Async XLA Ops:
  7.2 322.2 %copy-start = (f32[64,2048]{1,0:T(8,128)S(1)}, f32[64,2048]{1,0:T(8,128)}, u32[]{:S(2)}) copy-start(f32[64,2048]{1,0:T(8,128)} %param.21) | copy-start | bytes 1572868
  7.2 45.0 %copy-start.17 = (f32[1,256]{1,0:T(1,128)S(1)}, f32[1,256]{1,0:T(1,128)}, u32[]{:S(2)}) copy-start(f32[1,256]{1,0:T(1,128)} %param.18) | copy-start | bytes 3076
  7.2 44.8 %copy-start.14 = (s32[8,8]{1,0:T(8,128)S(1)}, s32[8,8]{1,0:T(8,128)}, u32[]{:S(2)}) copy-start(s32[8,8]{1,0:T(8,128)} %param.14) | copy-start | bytes 772
  7.2 45.0 %copy-start.1 = (f32[512,512]{1,0:T(8,128)S(1)}, f32[512,512]{1,0:T(8,128)}, u32[]{:S(2)}) copy-start(f32[512,512]{1,0:T(8,128)} %param.13) | copy-start | bytes 3145732
  16.7 39.0 %copy-start.16 = (s32[256,1]{0,1:T(1,128)}, s32[256,1]{0,1:T(1,128)S(1)}, u32[]{:S(2)}) copy-start(s32[256,1]{0,1:T(1,128)S(1)} %get-tuple-element.57) | copy-start | bytes 3076
  35.7 22.3 %all-to-all-start = ((f32[32,8,1]{1,2,0:T(1,128)}), f32[32,8,1]{1,2,0:T(1,128)S(1)}, u32[]{:S(2)}, u32[]{:S(2)}) async-start(f32[32,8,1]{1,2,0:T(1,128)} %bitcast.41), calls=%async_computation | async-start | bytes 32768 | tf_op jit(solution)/shard_map/all_to_all | solution.py:38
  49.4 280.0 %all-reduce.5.cloned.1.call-start = ((), (), s32[]{:S(2)}) async-start(), calls=%async_computation.7 | async-start | bytes 2097152 | tf_op jit(solution)/shard_map/psum | solution.py:63
  49.5 4.1 copy-start.26
  49.5 4.2 copy-start.2
  49.5 4.2 copy-start.8
  50.9 1.0 copy-start.4
  50.9 3.2 copy-start.21
  52.3 294.1 %copy-start.18 = (s32[64]{0:T(128)}, s32[64]{0:T(128)S(1)}, u32[]{:S(2)}) copy-start(s32[64]{0:T(128)S(1)} %fusion.36) | copy-start | bytes 772
  53.6 5.2 copy-start.15
  54.1 278.6 %copy-start.11 = (f32[32,8]{1,0:T(8,128)}, f32[32,8]{1,0:T(8,128)S(1)}, u32[]{:S(2)}) copy-start(f32[32,8]{1,0:T(8,128)S(1)} %fusion.32) | copy-start | bytes 3076
  58.0 273.4 %copy-start.9 = (f32[64,512]{1,0:T(8,128)S(1)}, f32[64,512]{1,0:T(8,128)}, u32[]{:S(2)}) copy-start(f32[64,512]{1,0:T(8,128)} %param.20) | copy-start | bytes 393220
  331.8 513.0 %copy-start.6 = (f32[512,128]{0,1:T(8,128)}, f32[512,128]{0,1:T(8,128)S(1)}, u32[]{:S(2)}) copy-start(f32[512,128]{0,1:T(8,128)S(1)} %fusion.2) | copy-start | bytes 786436
  333.5 23.6 %all-to-all-start.1 = ((f32[32,8,128]{2,1,0:T(8,128)}), f32[32,8,128]{2,1,0:T(8,128)S(1)}, u32[]{:S(2)}, u32[]{:S(2)}) async-start(f32[32,8,128]{2,1,0:T(8,128)} %bitcast_multiply_fusion.8), calls=%async_computation.1 | async-start | bytes 262144 | tf_op jit(solution)/shard_map/all_to_all | solution.py:77
  357.1 18.6 %all-to-all-start.2 = ((f32[32,8,128]{2,1,0:T(8,128)}), f32[32,8,128]{2,1,0:T(8,128)S(1)}, u32[]{:S(2)}, u32[]{:S(2)}) async-start(f32[32,8,128]{2,1,0:T(8,128)} %bitcast.56), calls=%async_computation.2 | async-start | bytes 262144 | tf_op jit(solution)/shard_map/all_to_all | solution.py:80
  366.3 378.8 %all-reduce.7.cloned.1.call-start = ((), (), s32[]{:S(2)}) async-start(), calls=%async_computation.8 | async-start | bytes 2097152 | tf_op jit(solution)/shard_map/psum | solution.py:63
  476.1 0.5 copy-start.29
  476.1 0.6 copy-start.22
  477.2 1.0 copy-start.5
  479.0 365.9 %copy-start.30 = (f32[128]{0:T(128)S(1)}, f32[128]{0:T(128)}, u32[]{:S(2)}) copy-start(f32[128]{0:T(128)} %copy-done.29) | copy-start | bytes 1540
  844.8 4.5 copy-start.27
  847.3 2.0 copy-start.12
  850.1 19.2 %all-to-all-start.3 = ((f32[32,8,128]{2,1,0:T(8,128)}), f32[32,8,128]{2,1,0:T(8,128)S(1)}, u32[]{:S(2)}, u32[]{:S(2)}) async-start(f32[32,8,128]{2,1,0:T(8,128)} %bitcast_multiply_fusion.5), calls=%async_computation.3 | async-start | bytes 262144 | tf_op jit(solution)/shard_map/all_to_all | solution.py:77
  859.1 2.9 copy-start.19
  869.3 9.5 copy-start.10
  869.3 18.8 %all-to-all-start.4 = ((f32[32,8,128]{2,1,0:T(8,128)}), f32[32,8,128]{2,1,0:T(8,128)}, u32[]{:S(2)}, u32[]{:S(2)}) async-start(f32[32,8,128]{2,1,0:T(8,128)} %bitcast.71), calls=%async_computation.4 | async-start | bytes 262144 | tf_op jit(solution)/shard_map/all_to_all | solution.py:80
  878.8 377.6 %all-reduce.9.cloned.1.call-start = ((), (), s32[]{:S(2)}) async-start(), calls=%async_computation.9 | async-start | bytes 2097152 | tf_op jit(solution)/shard_map/psum | solution.py:63
  987.4 0.6 copy-start.24
  988.6 1.0 copy-start.3
  990.3 366.0 %copy-start.28 = (f32[128]{0:T(128)S(1)}, f32[128]{0:T(128)}, u32[]{:S(2)}) copy-start(f32[128]{0:T(128)} %copy-done.27) | copy-start | bytes 1540
  1358.7 2.0 copy-start.13
  1361.5 19.0 %all-to-all-start.5 = ((f32[32,8,128]{2,1,0:T(8,128)}), f32[32,8,128]{2,1,0:T(8,128)S(1)}, u32[]{:S(2)}, u32[]{:S(2)}) async-start(f32[32,8,128]{2,1,0:T(8,128)} %bitcast_multiply_fusion.2), calls=%async_computation.5 | async-start | bytes 262144 | tf_op jit(solution)/shard_map/all_to_all | solution.py:77
  1370.4 2.9 copy-start.20
  1380.6 18.6 %all-to-all-start.6 = ((f32[32,8,128]{2,1,0:T(8,128)}), f32[32,8,128]{2,1,0:T(8,128)S(1)}, u32[]{:S(2)}, u32[]{:S(2)}) async-start(f32[32,8,128]{2,1,0:T(8,128)} %bitcast.86), calls=%async_computation.6 | async-start | bytes 262144 | tf_op jit(solution)/shard_map/all_to_all | solution.py:80
  1393.0 104.2 %copy-start.7 = (f32[512,128]{0,1:T(8,128)S(1)}, f32[512,128]{0,1:T(8,128)}, u32[]{:S(2)}) copy-start(f32[512,128]{0,1:T(8,128)} %copy-done.6) | copy-start | bytes 786436
  1393.0 104.2 %copy-start.23 = (f32[128]{0:T(128)S(1)}, f32[128]{0:T(128)}, u32[]{:S(2)}) copy-start(f32[128]{0:T(128)} %copy-done.22) | copy-start | bytes 1540
  1393.0 104.1 %copy-start.25 = (f32[128]{0:T(128)S(1)}, f32[128]{0:T(128)}, u32[]{:S(2)}) copy-start(f32[128]{0:T(128)} %copy-done.24) | copy-start | bytes 1540
Sparse Core Ops, SparseCore 0:
  55.3 274.0 all-reduce.4
  478.4 266.6 all-reduce.6
  989.7 266.6 all-reduce.8
where the time goes:
time: 1520 us; the launch traced here: 1510 us
  waiting for transfers between devices  812 us (53%)
  blocking collectives  482 us (32%)
  other arithmetic  69.2 us (5%)
  starting transfers between devices  60.2 us (4%)
  local copies, waits for them, and re-layouts  34.9 us (2%)
  matrix products  32.1 us (2%)
    psum x3, waiting for transfers between devices, precondition(): whole = lax.psum(padded, ('group', 'sub'))  799 us
    psum x3, blocking collectives, residual_product(): return lax.psum(jnp.sum(resid * zvalue, axis=0), ('group', 'sub'))  292 us
    psum x2, blocking collectives, local(): lax.psum(jnp.sum(direction * image, axis=0), ('group', 'sub'))  191 us
  transfers between devices with their start and end apart: 10, of which 6 were waited for; matrix products, arithmetic and copies ran while one was open for 5% of the time, Pallas kernels for 0%

commit v1 on v0

v1 whole, which is shorter than its diff:
```python
import functools

import jax
import jax.numpy as jnp
from jax import lax
from jax.experimental import pallas as pl
from jax.experimental.pallas import tpu as pltpu
from jax.sharding import PartitionSpec as P

F32, BF16 = jnp.float32, jnp.bfloat16
ROWS, RHS, NC, SLOTS, BLK, NB = 512, 128, 64, 256, 64, 8
N_GROUP, N_SUB, LF = 16, 32, 128
VEC = (ROWS, RHS)
MSG_GROUP = (N_GROUP, 8, 128)
MSG_SUB = (N_SUB, 8, 128)
MSG_FACE = (N_SUB, 16, 128)


def split(x):
    high = x.astype(BF16)
    return high, (x - high.astype(F32)).astype(BF16)


def split3(x):
    high, rest = x.astype(BF16), None
    rest = x - high.astype(F32)
    mid = rest.astype(BF16)
    return high, mid, (rest - mid.astype(F32)).astype(BF16)


def dot(a, b):
    return jnp.dot(a, b, preferred_element_type=F32)


def dot_nt(a, b):
    return lax.dot_general(a, b, (((1,), (1,)), ((), ())), preferred_element_type=F32)


def exact(one_hot, x):
    n = x.shape[1]
    both = dot(one_hot, jnp.concatenate(split(x), axis=1))
    return both[:, :n] + both[:, n:]


def dot3(a_high, a_low, x):
    n = x.shape[1]
    x_high, x_low = split(x)
    both = dot(a_high, jnp.concatenate([x_high, x_low], axis=1))
    return both[:, :n] + (both[:, n:] + dot(a_low, x_high))


def rowdot(a, b):
    return jnp.sum(a * b, axis=0, keepdims=True)


def tile_of(*rows):
    index = lax.broadcasted_iota(jnp.int32, (8, RHS), 0)
    tile = jnp.zeros((8, RHS), F32)
    for at, row in enumerate(rows):
        tile = jnp.where(index == at, row, tile)
    return tile


def pack(coarse, aux):
    whole = jnp.concatenate([coarse, aux, jnp.zeros((56, RHS), F32)], axis=0)
    return whole.T.reshape(MSG_GROUP)


def send_faces(field, pick, weight, msg_ref):
    rows = exact(pick, field)
    msg_ref[:, :8, :] = (rows[:SLOTS] * weight).reshape(N_SUB, 8, RHS)
    msg_ref[:, 8:, :] = rows[SLOTS:].reshape(N_SUB, 8, RHS)


def coupled_of(recv_ref, place, weight):
    out = recv_ref[:, :8, :].reshape(SLOTS, RHS)
    back = recv_ref[:, 8:, :].reshape(SLOTS, RHS) * weight
    return exact(place, jnp.concatenate([out, back], axis=0))


def coarse_of(recv_ref, basis_t):
    turned = recv_ref[...].reshape(128, 128).T
    high, low = split(turned[:NC])
    high, low = high.astype(F32), low.astype(F32)
    stack = jnp.concatenate([high, high, low, jnp.zeros((NC, RHS), F32)], axis=0).astype(BF16)
    return dot(basis_t, stack), turned[NC : NC + 8]


def k_first(right_ref, basis_ref, msg_ref):
    high, low = split(basis_ref[...])
    msg_ref[...] = pack(dot3(high, low, right_ref[...]), jnp.zeros((8, RHS), F32))


def k_slots(faces_ref, lands_ref, counts_ref, weight_ref, pick_ref, place_ref, wcol_ref):
    peer = lax.broadcasted_iota(jnp.int32, (N_SUB, SLOTS), 0)
    slot = lax.broadcasted_iota(jnp.int32, (N_SUB, SLOTS), 1)
    spread = jnp.where(slot // 8 == peer, 1.0, 0.0).astype(BF16)
    counts = jnp.broadcast_to(counts_ref[...].astype(F32), (8, N_SUB)).astype(BF16)
    counts = dot(counts, spread)[:1]
    place_in = (lax.broadcasted_iota(jnp.int32, (1, SLOTS), 1) % 8).astype(F32)
    weights = jnp.where(place_in < counts, weight_ref[...], 0.0)
    wcol_ref[...] = jnp.broadcast_to(weights, (128, SLOTS)).T
    faces, lands = faces_ref[...], lands_ref[...]
    row = lax.broadcasted_iota(jnp.int32, (ROWS, SLOTS), 0)
    place_ref[:, :SLOTS] = jnp.where(row == lands, 1.0, 0.0).astype(BF16)
    place_ref[:, SLOTS:] = jnp.where(row == faces, 1.0, 0.0).astype(BF16)
    lane = lax.broadcasted_iota(jnp.int32, (SLOTS, 128), 1).astype(F32)
    for at, index in enumerate((faces, lands)):
        column = jnp.broadcast_to(index.astype(F32), (128, SLOTS)).T
        for t in range(ROWS // 128):
            pick_ref[at * SLOTS : (at + 1) * SLOTS, t * 128 : (t + 1) * 128] = jnp.where(
                column == lane + float(t * 128), 1.0, 0.0
            ).astype(BF16)


def k_setup(cols_ref, values_ref, mass_ref, bh_ref, bl_ref, base_ref, dense_ref):
    lane = lax.broadcasted_iota(jnp.int32, (1, 128), 1)
    upper = jnp.where(lane >= BLK, 1, 0)
    for b in range(NB):
        rows = slice(b * BLK, (b + 1) * BLK)
        parts = []
        for m in range(NB // 2):
            block = values_ref[rows, m * 128 : (m + 1) * 128]
            first, second = cols_ref[b, 2 * m], cols_ref[b, 2 * m + 1]
            parts.append((block, jnp.where(lane < BLK, first, second) - upper))
            parts.append(
                (pltpu.roll(block, BLK, axis=1), jnp.where(lane < BLK, second, first) - upper)
            )
        for t in range(NB // 2):
            total = None
            for block, column in parts:
                term = block * jnp.where(column == 2 * t, 1.0, 0.0)
                total = term if total is None else total + term
            dense_ref[rows, t * 128 : (t + 1) * 128] = total
    dense = dense_ref[...]
    both = dense + dense.T
    bh_ref[...], bl_ref[...] = split(both)
    mass = jnp.broadcast_to(mass_ref[...], (128, ROWS)).T
    base_ref[...] = mass + jnp.sum(both, axis=1, keepdims=True)


def k_factor(factor_ref, basis_ref, inverse_ref, gh_ref, gl_ref, sh_ref, sl_ref, st_ref, ch_ref, cl_ref):
    for b in range(ROWS // LF):
        rows = slice(b * LF, (b + 1) * LF)
        block = factor_ref[rows, :]
        high, low = split(block.T)
        gh_ref[rows, :], gl_ref[rows, :] = split(dot3(high, low, block))
    high, low = split(basis_ref[...])
    sh_ref[...], sl_ref[...] = high, low
    high, low = high.astype(F32), low.astype(F32)
    st_ref[...] = jnp.concatenate([high, low, high, jnp.zeros((NC, ROWS), F32)], axis=0).T.astype(BF16)
    high, low = split(inverse_ref[...])
    ch_ref[:NC, :], cl_ref[:NC, :] = high, low
    ch_ref[NC:, :] = jnp.zeros((128 - NC, N_SUB * NC), BF16)
    cl_ref[NC:, :] = jnp.zeros((128 - NC, N_SUB * NC), BF16)


def k_gather_first(recv_ref, wcol_ref, msg_ref):
    total = jnp.sum(recv_ref[...], axis=0)
    lane = lax.broadcasted_iota(jnp.int32, MSG_SUB, 2)
    msg_ref[...] = jnp.where(lane == 127, wcol_ref[...].reshape(MSG_SUB), total[None])


def k_gather(recv_ref, msg_ref):
    msg_ref[...] = jnp.broadcast_to(jnp.sum(recv_ref[...], axis=0)[None], MSG_SUB)


def k_solve(recv_ref, ch_ref, cl_ref, msg_ref):
    lane = lax.broadcasted_iota(jnp.int32, (8, 128), 1)
    tiles = []
    aux = jnp.zeros((8, 128), F32)
    for j in range(N_SUB // 2):
        even, odd = recv_ref[2 * j], recv_ref[2 * j + 1]
        tiles.append(jnp.where(lane < NC, even, pltpu.roll(odd, NC, axis=1)))
        aux = aux + (even + odd)
    whole = jnp.concatenate(tiles, axis=1)
    high = whole.astype(BF16).astype(F32)
    stack = jnp.concatenate([high, whole - high], axis=0).astype(BF16)
    first = dot_nt(stack, ch_ref[...])
    solved = first[:8] + (first[8:] + dot_nt(stack, cl_ref[...])[:8])
    tile = jnp.where(lane < NC, solved, aux)
    msg_ref[...] = jnp.broadcast_to(tile[None], MSG_GROUP)


def k_diag(recv_ref, place_ref, wcol_ref, base_ref, diag_ref, inv_ref):
    lane = lax.broadcasted_iota(jnp.int32, (SLOTS, 128), 1)
    got = jnp.where(lane == 127, recv_ref[...].reshape(SLOTS, 128), 0.0)
    got = jnp.broadcast_to(jnp.sum(got, axis=1, keepdims=True), (SLOTS, 128))
    both = jnp.concatenate([got, wcol_ref[...]], axis=0)
    diag = base_ref[...]
    for part in split3(both):
        diag = diag + dot(place_ref[...], part)
    diag_ref[...] = diag
    inv_ref[...] = 1.0 / diag


def k_smooth(field_ref, inv_ref, gh_ref, gl_ref, out_ref):
    for b in range(ROWS // LF):
        rows = slice(b * LF, (b + 1) * LF)
        field = field_ref[rows, :]
        out_ref[rows, :] = field * inv_ref[rows, :] + dot3(gh_ref[rows, :], gl_ref[rows, :], field)


def k_start(recv_ref, smooth_ref, st_ref, pick_ref, wcol_ref, z_ref, msg_ref):
    coarse, _ = coarse_of(recv_ref, st_ref[...])
    z = smooth_ref[...] + coarse
    z_ref[...] = z
    send_faces(z, pick_ref[...], wcol_ref[...], msg_ref)


def k_local0(z_ref, right_ref, diag_ref, bh_ref, bl_ref, out_ref, dots_ref):
    z = z_ref[...]
    out_ref[...] = diag_ref[...] * z - dot3(bh_ref[...], bl_ref[...], z)
    dots_ref[...] = tile_of(rowdot(right_ref[...], z))


def k_image(recv_ref, local_ref, z_ref, dots_ref, place_ref, wcol_ref, sh_ref, sl_ref, image_ref, msg_ref):
    image = local_ref[...] - coupled_of(recv_ref, place_ref[...], wcol_ref[...])
    image_ref[...] = image
    index = lax.broadcasted_iota(jnp.int32, (8, RHS), 0)
    aux = jnp.where(index == 2, rowdot(z_ref[...], image), dots_ref[...])
    msg_ref[...] = pack(dot3(sh_ref[...], sl_ref[...], image), aux)


def k_step0(recv_ref, smooth_ref, z_ref, st_ref, pick_ref, wcol_ref, u_ref, znew_ref, scal_ref, msg_ref):
    coarse, aux = coarse_of(recv_ref, st_ref[...])
    gamma, pap = aux[0:1], aux[2:3]
    alpha = gamma / pap
    u = smooth_ref[...] + coarse
    u_ref[...] = u
    znew = z_ref[...] - alpha * u
    znew_ref[...] = znew
    scal_ref[...] = tile_of(alpha, gamma, pap)
    send_faces(znew, pick_ref[...], wcol_ref[...], msg_ref)


def k_local1(z_ref, right_ref, q_ref, scal_ref, diag_ref, bh_ref, bl_ref, out_ref, resid_ref, dots_ref):
    z, q = z_ref[...], q_ref[...]
    out_ref[...] = diag_ref[...] * z - dot3(bh_ref[...], bl_ref[...], z)
    resid = right_ref[...] - scal_ref[0:1] * q
    resid_ref[...] = resid
    dots_ref[...] = tile_of(rowdot(resid, z), rowdot(z, q))


def k_step1(
    recv_ref, smooth_ref, u_ref, z_ref, scal_ref, st_ref, pick_ref, wcol_ref, znew_ref, scalnew_ref, msg_ref
):
    coarse, aux = coarse_of(recv_ref, st_ref[...])
    gamma, cross, zaz = aux[0:1], aux[1:2], aux[2:3]
    beta = gamma / scal_ref[1:2]
    pap = zaz + beta * (2.0 * cross + beta * scal_ref[2:3])
    alpha = gamma / pap
    u = smooth_ref[...] + coarse + beta * u_ref[...]
    znew = z_ref[...] - alpha * u
    znew_ref[...] = znew
    scalnew_ref[...] = tile_of(alpha, gamma, pap, beta)
    send_faces(znew, pick_ref[...], wcol_ref[...], msg_ref)


def k_local2(
    z_ref, z1_ref, z0_ref, v1_ref, q0_ref, resid_ref, scal0_ref, scal_ref, diag_ref, bh_ref, bl_ref,
    out_ref, direction_ref, image_ref, x_ref, residnew_ref, dots_ref,
):
    z, z0 = z_ref[...], z0_ref[...]
    out_ref[...] = diag_ref[...] * z - dot3(bh_ref[...], bl_ref[...], z)
    alpha, beta = scal_ref[0:1], scal_ref[3:4]
    direction = z1_ref[...] + beta * z0
    image = v1_ref[...] + beta * q0_ref[...]
    direction_ref[...], image_ref[...] = direction, image
    x_ref[...] = scal0_ref[0:1] * z0 + alpha * direction
    resid = resid_ref[...] - alpha * image
    residnew_ref[...] = resid
    dots_ref[...] = tile_of(rowdot(resid, z), rowdot(z, image))


def k_last_image(recv_ref, local_ref, z_ref, dots_ref, place_ref, wcol_ref, image_ref, msg_ref):
    image = local_ref[...] - coupled_of(recv_ref, place_ref[...], wcol_ref[...])
    image_ref[...] = image
    index = lax.broadcasted_iota(jnp.int32, (8, RHS), 0)
    aux = jnp.where(index == 2, rowdot(z_ref[...], image), dots_ref[...])
    msg_ref[...] = jnp.broadcast_to(aux[None], MSG_GROUP)


def k_end(recv_ref, scal_ref, z_ref, v_ref, direction_ref, image_ref, x_ref, resid_ref, xout_ref, rout_ref):
    aux = jnp.sum(recv_ref[...], axis=0)
    gamma, cross, zaz = aux[0:1], aux[1:2], aux[2:3]
    beta = gamma / scal_ref[1:2]
    pap = zaz + beta * (2.0 * cross + beta * scal_ref[2:3])
    alpha = gamma / pap
    xout_ref[...] = x_ref[...] + alpha * (z_ref[...] + beta * direction_ref[...])
    rout_ref[...] = resid_ref[...] - alpha * (v_ref[...] + beta * image_ref[...])


def call(kernel, outs, *args, smem=0, scratch=(), flops=1e6):
    specs = [pl.BlockSpec(memory_space=pltpu.SMEM)] * smem
    specs += [pl.BlockSpec(memory_space=pltpu.VMEM)] * (len(args) - smem)
    single = not isinstance(outs, list)
    shapes = [jax.ShapeDtypeStruct(s, d) for s, d in ([outs] if single else outs)]
    moved = sum(a.size * a.dtype.itemsize for a in [*args, *shapes])
    out = pl.pallas_call(
        kernel,
        out_shape=shapes,
        in_specs=specs,
        out_specs=[pl.BlockSpec(memory_space=pltpu.VMEM)] * len(shapes),
        scratch_shapes=list(scratch),
        compiler_params=pltpu.CompilerParams(vmem_limit_bytes=24 << 20),
        cost_estimate=pl.CostEstimate(flops=int(flops), bytes_accessed=int(moved), transcendentals=0),
    )(*args)
    return out[0] if single else out


def swap(x, axis):
    return lax.all_to_all(x, axis, split_axis=0, concat_axis=0, tiled=True)


def local(
    right_side,
    mass,
    block_values,
    block_cols,
    face_rows,
    land_rows,
    face_counts,
    face_weight,
    local_factor,
    basis,
    coarse_inverse,
):
    vec = (VEC, F32)
    tile = ((8, RHS), F32)
    to_group, to_sub, to_face = (MSG_GROUP, F32), (MSG_SUB, F32), (MSG_FACE, F32)
    square = ((ROWS, ROWS), BF16)

    part = swap(call(k_first, to_group, right_side, basis), "group")
    pick, place, wcol = call(
        k_slots, [square, square, ((SLOTS, 128), F32)], face_rows, land_rows, face_counts, face_weight
    )
    whole = swap(call(k_gather_first, to_sub, part, wcol), "sub")
    gh, gl, sh, sl, st, ch, cl = call(
        k_factor,
        [((ROWS, LF), BF16)] * 2
        + [((NC, ROWS), BF16)] * 2
        + [((ROWS, 256), BF16)]
        + [((128, N_SUB * NC), BF16)] * 2,
        local_factor,
        basis,
        coarse_inverse,
    )
    bh, bl, base = call(
        k_setup,
        [square, square, vec],
        block_cols,
        block_values,
        mass,
        smem=1,
        scratch=[pltpu.VMEM((ROWS, ROWS), F32)],
    )
    solved = swap(call(k_solve, to_group, whole, ch, cl), "group")
    diag, inv = call(k_diag, [vec, vec], whole, place, wcol, base)

    def smooth(field):
        return call(k_smooth, vec, field, inv, gh, gl)

    def coarse(msg):
        whole = swap(call(k_gather, to_sub, swap(msg, "group")), "sub")
        return swap(call(k_solve, to_group, whole, ch, cl), "group")

    def image(msg, near, z, dots):
        return call(k_image, [vec, to_group], swap(msg, "sub"), near, z, dots, place, wcol, sh, sl)

    z0, msg = call(k_start, [vec, to_face], solved, smooth(right_side), st, pick, wcol)
    near, dots = call(k_local0, [vec, tile], z0, right_side, diag, bh, bl)
    q0, msg = image(msg, near, z0, dots)

    solved = coarse(msg)
    u0, z1, scal0, msg = call(
        k_step0, [vec, vec, tile, to_face], solved, smooth(q0), z0, st, pick, wcol
    )
    near, resid1, dots = call(
        k_local1, [vec, vec, tile], z1, right_side, q0, scal0, diag, bh, bl
    )
    v1, msg = image(msg, near, z1, dots)

    solved = coarse(msg)
    z2, scal1, msg = call(
        k_step1, [vec, tile, to_face], solved, smooth(v1), u0, z1, scal0, st, pick, wcol
    )
    near, direction, im, x, resid2, dots = call(
        k_local2, [vec] * 5 + [tile], z2, z1, z0, v1, q0, resid1, scal0, scal1, diag, bh, bl
    )
    v2, msg = call(k_last_image, [vec, to_group], swap(msg, "sub"), near, z2, dots, place, wcol)
    whole = swap(call(k_gather, to_sub, swap(msg, "group")), "sub")
    return tuple(call(k_end, [vec, vec], whole, scal1, z2, v2, direction, im, x, resid2))


def solution(mesh):
    both = P(("group", "sub"), None)
    return jax.shard_map(
        local,
        mesh=mesh,
        in_specs=(both,) * 10 + (P("sub", None),),
        out_specs=(both, both),
        check_vma=False,
    )
```

time: 1520 us -> 246 us (0.16)
  waiting for transfers between devices: 812 us -> 47.1 us
  blocking collectives: 482 us -> 79.2 us
  other arithmetic: 69.2 us -> 0 us
  matrix products: 32.1 us -> 0 us
  Pallas kernels: 0 us -> 17.7 us
    psum x3 -> x0, waiting for transfers between devices: 799 us -> none  [precondition(): whole = lax.psum(padded, ('group', 'sub'))]
    psum x5 -> x0, blocking collectives: 482 us -> none  [the longest x3 292 us: residual_product(): return lax.psum(jnp.sum(resid * zvalue, axis=0), ('group', 'sub'))]
    all_to_all x0 -> x6, blocking collectives: none -> 79.2 us  [swap(): return lax.all_to_all(x, axis, split_axis=0, concat_axis=0, tiled=True)]
    unnamed x66 -> x170, local copies, waits for them, and re-layouts: 6.71 us -> 47.1 us
    scatter-add x12 -> x0, other arithmetic: 38.8 us -> none  [the longest x3 21.1 us: local(): backward = jnp.zeros((n_blocks, block_rows, n_rhs), jnp.float32).at[flat_...]
    all_to_all x7 -> x8, waiting for transfers between devices: 12.9 us -> 47.1 us  [swap(): return lax.all_to_all(x, axis, split_axis=0, concat_axis=0, tiled=True)]
    dot_general x21 -> x0, matrix products: 32.1 us -> none  [the longest x3 9.54 us: local(): jnp.einsum('rik,ric->rkc', values_r, operate_blocks, precision=highest)]
    select_n x7 -> x0, other arithmetic: 22.1 us -> none  [the longest x3 16.9 us: local(): weights = jnp.where(live, face_weight[0], jnp.float32(0.0))]
  transfers between devices with their start and end apart: 10 -> 8, of which waited for: 6 -> 8; matrix products, arithmetic and copies ran while one was open for 5% -> 0% of each run, Pallas kernels for 0% -> 2%
where the time goes in v1:
time: 246 us; the launch traced here: 244 us
  blocking collectives  79.2 us (32%)
  starting transfers between devices  51.5 us (21%)
  local copies, waits for them, and re-layouts  47.1 us (19%)
  waiting for transfers between devices  47.1 us (19%)
  Pallas kernels  17.7 us (7%)
    all_to_all x6, blocking collectives, swap(): return lax.all_to_all(x, axis, split_axis=0, concat_axis=0, tiled=True)  79.2 us
    all_to_all x8, starting transfers between devices, swap(): return lax.all_to_all(x, axis, split_axis=0, concat_axis=0, tiled=True)  51.5 us
    all_to_all x8, waiting for transfers between devices, swap(): return lax.all_to_all(x, axis, split_axis=0, concat_axis=0, tiled=True)  47.1 us
    unnamed x170, local copies, waits for them, and re-layouts  47.1 us
    pallas_call x25, Pallas kernels, call(): pl.pallas_call(kernel, out_shape=shapes, in_specs=specs, out_specs=[pl.Bl...  17.7 us
  transfers between devices with their start and end apart: 8, of which 8 were waited for; matrix products, arithmetic and copies ran while one was open for 0% of the time, Pallas kernels for 2%

profile of v1, /device:TPU:1, one launch (start us, length us, event | category | flops | bytes accessed | tf_op | source)
XLA Modules:
  0.0 243.8 jit_solution(10080875583179548764)
XLA Ops:
  3.4 10.3 %all-to-all-start = ((f32[16,8,128]{2,1,0:T(8,128)}), f32[16,8,128]{2,1,0:T(8,128)S(1)}, u32[]{:S(2)}, u32[]{:S(2)}) async-start(f32[16,8,128]{2,1,0:T(8,128)} %shard_map.122), calls=%async_computation | async-start | bytes 131072 | tf_op jit(solution)/shard_map/all_to_all | solution.py:313
  14.3 7.3 %all-to-all-done.recv_ref = f32[16,8,128]{2,1,0:T(8,128)S(1)} async-done(((f32[16,8,128]{2,1,0:T(8,128)}), f32[16,8,128]{2,1,0:T(8,128)S(1)}, u32[]{:S(2)}, u32[]{:S(2)}) %all-to-all-start) | async-done | bytes 65568 | tf_op jit(solution)/shard_map/all_to_all | solution.py:313
  22.3 11.4 %all-to-all-start.1 = ((f32[32,8,128]{2,1,0:T(8,128)}), f32[32,8,128]{2,1,0:T(8,128)S(1)}, u32[]{:S(2)}, u32[]{:S(2)}) async-start(f32[32,8,128]{2,1,0:T(8,128)} %shard_map.124), calls=%async_computation.1 | async-start | bytes 262144 | tf_op jit(solution)/shard_map/all_to_all | solution.py:313
  37.4 6.1 %all-to-all-done.1.recv_ref = f32[32,8,128]{2,1,0:T(8,128)S(1)} async-done(((f32[32,8,128]{2,1,0:T(8,128)}), f32[32,8,128]{2,1,0:T(8,128)S(1)}, u32[]{:S(2)}, u32[]{:S(2)}) %all-to-all-start.1) | async-done | bytes 131104 | tf_op jit(solution)/shard_map/all_to_all | solution.py:313
  43.5 1.0 shard_map.126
  44.6 5.6 %all-to-all-start.2 = ((f32[16,8,128]{2,1,0:T(8,128)}), f32[16,8,128]{2,1,0:T(8,128)}, u32[]{:S(2)}, u32[]{:S(2)}) async-start(f32[16,8,128]{2,1,0:T(8,128)} %shard_map.126), calls=%async_computation.2 | async-start | bytes 131072 | tf_op jit(solution)/shard_map/all_to_all | solution.py:313
  50.2 1.2 copy-done.36
  51.4 1.7 shard_map.127
  56.2 1.9 all-to-all-done.2.recv_ref
  58.1 0.9 copy-done.12
  59.1 0.9 copy-done.40
  60.0 1.5 shard_map.130
  62.9 4.6 %all-to-all-start.3 = ((f32[32,16,128]{2,1,0:T(8,128)}), f32[32,16,128]{2,1,0:T(8,128)}, u32[]{:S(2)}, u32[]{:S(2)}) async-start(f32[32,16,128]{2,1,0:T(8,128)} %copy-done.62), calls=%async_computation.3 | async-start | bytes 524288 | tf_op jit(solution)/shard_map/all_to_all | solution.py:313
  68.5 0.9 copy-done.19
  70.6 9.0 %all-to-all-done.3.recv_ref = f32[32,16,128]{2,1,0:T(8,128)} async-done(((f32[32,16,128]{2,1,0:T(8,128)}), f32[32,16,128]{2,1,0:T(8,128)}, u32[]{:S(2)}, u32[]{:S(2)}) %all-to-all-start.3) | async-done | bytes 262176 | tf_op jit(solution)/shard_map/all_to_all | solution.py:313
  79.6 0.9 copy-done.4
  82.2 0.9 copy-done.76
  83.2 1.5 shard_map.132
  84.7 14.4 %all_to_all.70.recv_ref = f32[16,8,128]{2,1,0:T(8,128)S(1)} all-to-all(f32[16,8,128]{2,1,0:T(8,128)S(1)} %get-tuple-element.62), channel_id=1, replica_groups=mesh['group'=16,'sub'=32] {'group'}, dimensions={0} | all-to-all | bytes 131072 | tf_op jit(solution)/shard_map/all_to_all | solution.py:313
  99.2 13.2 %all_to_all.71.recv_ref = f32[32,8,128]{2,1,0:T(8,128)S(1)} all-to-all(f32[32,8,128]{2,1,0:T(8,128)S(1)} %shard_map.133), channel_id=1, replica_groups=mesh['group'=16,'sub'=32] {'sub'}, dimensions={0} | all-to-all | bytes 262144 | tf_op jit(solution)/shard_map/all_to_all | solution.py:313
  113.4 5.4 %all-to-all-start.6 = ((f32[16,8,128]{2,1,0:T(8,128)}), f32[16,8,128]{2,1,0:T(8,128)}, u32[]{:S(2)}, u32[]{:S(2)}) async-start(f32[16,8,128]{2,1,0:T(8,128)} %copy-done.59), calls=%async_computation.6 | async-start | bytes 131072 | tf_op jit(solution)/shard_map/all_to_all | solution.py:313
  118.8 0.9 copy-done.16
  119.8 0.9 copy-done.23
  123.5 3.3 %all-to-all-done.6.recv_ref = f32[16,8,128]{2,1,0:T(8,128)} async-done(((f32[16,8,128]{2,1,0:T(8,128)}), f32[16,8,128]{2,1,0:T(8,128)}, u32[]{:S(2)}, u32[]{:S(2)}) %all-to-all-start.6) | async-done | bytes 65568 | tf_op jit(solution)/shard_map/all_to_all | solution.py:313
  126.8 0.9 copy-done.5
  127.7 0.9 copy-done.13
  128.7 0.9 copy-done.42
  129.6 1.5 shard_map.136
  133.2 4.6 %all-to-all-start.7 = ((f32[32,16,128]{2,1,0:T(8,128)}), f32[32,16,128]{2,1,0:T(8,128)}, u32[]{:S(2)}, u32[]{:S(2)}) async-start(f32[32,16,128]{2,1,0:T(8,128)} %copy-done.61), calls=%async_computation.7 | async-start | bytes 524288 | tf_op jit(solution)/shard_map/all_to_all | solution.py:313
  138.8 0.9 copy-done.20
  139.7 0.9 copy-done.24
  142.5 7.4 %all-to-all-done.7.recv_ref = f32[32,16,128]{2,1,0:T(8,128)} async-done(((f32[32,16,128]{2,1,0:T(8,128)}), f32[32,16,128]{2,1,0:T(8,128)}, u32[]{:S(2)}, u32[]{:S(2)}) %all-to-all-start.7) | async-done | bytes 262176 | tf_op jit(solution)/shard_map/all_to_all | solution.py:313
  149.9 0.9 copy-done.9
  152.5 0.9 copy-done.74
  153.5 1.5 shard_map.138
  155.0 13.0 %all_to_all.72.recv_ref = f32[16,8,128]{2,1,0:T(8,128)S(1)} all-to-all(f32[16,8,128]{2,1,0:T(8,128)S(1)} %get-tuple-element.69), channel_id=1, replica_groups=mesh['group'=16,'sub'=32] {'group'}, dimensions={0} | all-to-all | bytes 131072 | tf_op jit(solution)/shard_map/all_to_all | solution.py:313
  168.1 13.2 %all_to_all.73.recv_ref = f32[32,8,128]{2,1,0:T(8,128)S(1)} all-to-all(f32[32,8,128]{2,1,0:T(8,128)S(1)} %shard_map.139), channel_id=1, replica_groups=mesh['group'=16,'sub'=32] {'sub'}, dimensions={0} | all-to-all | bytes 262144 | tf_op jit(solution)/shard_map/all_to_all | solution.py:313
  182.3 5.6 %all-to-all-start.10 = ((f32[16,8,128]{2,1,0:T(8,128)}), f32[16,8,128]{2,1,0:T(8,128)}, u32[]{:S(2)}, u32[]{:S(2)}) async-start(f32[16,8,128]{2,1,0:T(8,128)} %copy-done.58), calls=%async_computation.10 | async-start | bytes 131072 | tf_op jit(solution)/shard_map/all_to_all | solution.py:313
  188.8 0.9 copy-done.44
  190.7 5.1 %all-to-all-done.10.recv_ref = f32[16,8,128]{2,1,0:T(8,128)} async-done(((f32[16,8,128]{2,1,0:T(8,128)}), f32[16,8,128]{2,1,0:T(8,128)}, u32[]{:S(2)}, u32[]{:S(2)}) %all-to-all-start.10) | async-done | bytes 65568 | tf_op jit(solution)/shard_map/all_to_all | solution.py:313
  195.8 0.9 copy-done.38
  196.8 0.9 copy-done.51
  197.7 1.5 shard_map.142
  200.0 4.0 %all-to-all-start.11 = ((f32[32,16,128]{2,1,0:T(8,128)}), f32[32,16,128]{2,1,0:T(8,128)S(1)}, u32[]{:S(2)}, u32[]{:S(2)}) async-start(f32[32,16,128]{2,1,0:T(8,128)} %copy-done.60), calls=%async_computation.11 | async-start | bytes 524288 | tf_op jit(solution)/shard_map/all_to_all | solution.py:313
  209.1 7.0 %all-to-all-done.11.recv_ref = f32[32,16,128]{2,1,0:T(8,128)S(1)} async-done(((f32[32,16,128]{2,1,0:T(8,128)}), f32[32,16,128]{2,1,0:T(8,128)S(1)}, u32[]{:S(2)}, u32[]{:S(2)}) %all-to-all-start.11) | async-done | bytes 262176 | tf_op jit(solution)/shard_map/all_to_all | solution.py:313
  216.1 0.9 copy-done.72
  217.4 12.2 %all_to_all.74.recv_ref = f32[16,8,128]{2,1,0:T(8,128)S(1)} all-to-all(f32[16,8,128]{2,1,0:T(8,128)S(1)} %get-tuple-element.78), channel_id=1, replica_groups=mesh['group'=16,'sub'=32] {'group'}, dimensions={0} | all-to-all | bytes 131072 | tf_op jit(solution)/shard_map/all_to_all | solution.py:313
  229.6 13.3 %all_to_all.75.recv_ref = f32[32,8,128]{2,1,0:T(8,128)S(1)} all-to-all(f32[32,8,128]{2,1,0:T(8,128)S(1)} %shard_map.145), channel_id=1, replica_groups=mesh['group'=16,'sub'=32] {'sub'}, dimensions={0} | all-to-all | bytes 262144 | tf_op jit(solution)/shard_map/all_to_all | solution.py:313
  (169 shorter events, 36.2 us)
Async XLA Ops:
  0.6 1.0 copy-start
  2.5 31.2 %copy-start.48 = (f32[64,2048]{1,0:T(8,128)S(1)}, f32[64,2048]{1,0:T(8,128)}, u32[]{:S(2)}) copy-start(f32[64,2048]{1,0:T(8,128)} %inverse_ref.1) | copy-start | bytes 1572868
  3.4 10.3 %copy-start.81 = (s32[1,256]{1,0:T(1,128)S(1)}, s32[1,256]{1,0:T(1,128)}, u32[]{:S(2)}) copy-start(s32[1,256]{1,0:T(1,128)} %faces_ref.1) | copy-start | bytes 3076
  3.4 10.3 %copy-start.82 = (s32[1,256]{1,0:T(1,128)S(1)}, s32[1,256]{1,0:T(1,128)}, u32[]{:S(2)}) copy-start(s32[1,256]{1,0:T(1,128)} %lands_ref.1) | copy-start | bytes 3076
  3.4 10.3 %copy-start.83 = (f32[1,256]{1,0:T(1,128)S(1)}, f32[1,256]{1,0:T(1,128)}, u32[]{:S(2)}) copy-start(f32[1,256]{1,0:T(1,128)} %weight_ref.1) | copy-start | bytes 3076
  3.4 10.3 %copy-start.84 = (s32[1,32]{1,0:T(1,128)S(1)}, s32[1,32]{1,0:T(1,128)}, u32[]{:S(2)}) copy-start(s32[1,32]{1,0:T(1,128)} %counts_ref.1) | copy-start | bytes 388
  3.4 18.2 %all-to-all-start = ((f32[16,8,128]{2,1,0:T(8,128)}), f32[16,8,128]{2,1,0:T(8,128)S(1)}, u32[]{:S(2)}, u32[]{:S(2)}) async-start(f32[16,8,128]{2,1,0:T(8,128)} %shard_map.122), calls=%async_computation | async-start | bytes 131072 | tf_op jit(solution)/shard_map/all_to_all | solution.py:313
  21.6 12.1 %copy-start.49 = (f32[512,128]{1,0:T(8,128)S(1)}, f32[512,128]{1,0:T(8,128)}, u32[]{:S(2)}) copy-start(f32[512,128]{1,0:T(8,128)} %factor_ref.1) | copy-start | bytes 786436
  22.3 11.5 %copy-start.47 = (f32[64,512]{1,0:T(8,128)S(1)}, f32[64,512]{1,0:T(8,128)}, u32[]{:S(2)}) copy-start(f32[64,512]{1,0:T(8,128)} %basis_ref.3) | copy-start | bytes 393220
  22.3 21.3 %all-to-all-start.1 = ((f32[32,8,128]{2,1,0:T(8,128)}), f32[32,8,128]{2,1,0:T(8,128)S(1)}, u32[]{:S(2)}, u32[]{:S(2)}) async-start(f32[32,8,128]{2,1,0:T(8,128)} %shard_map.124), calls=%async_computation.1 | async-start | bytes 262144 | tf_op jit(solution)/shard_map/all_to_all | solution.py:313
  43.5 1.1 copy-start.26
  44.6 5.6 %copy-start.79 = (s32[8,8]{1,0:T(8,128)S(1)}, s32[8,8]{1,0:T(8,128)}, u32[]{:S(2)}) copy-start(s32[8,8]{1,0:T(8,128)} %cols_ref.1) | copy-start | bytes 772
  44.6 5.6 %copy-start.80 = (f32[1,512]{1,0:T(1,128)S(1)}, f32[1,512]{1,0:T(1,128)}, u32[]{:S(2)}) copy-start(f32[1,512]{1,0:T(1,128)} %mass_ref.1) | copy-start | bytes 6148
  44.6 13.5 %all-to-all-start.2 = ((f32[16,8,128]{2,1,0:T(8,128)}), f32[16,8,128]{2,1,0:T(8,128)}, u32[]{:S(2)}, u32[]{:S(2)}) async-start(f32[16,8,128]{2,1,0:T(8,128)} %shard_map.126), calls=%async_computation.2 | async-start | bytes 131072 | tf_op jit(solution)/shard_map/all_to_all | solution.py:313
  50.2 1.2 copy-start.36
  51.4 1.7 copy-start.27
  53.1 1.4 copy-start.1
  53.1 1.4 copy-start.29
  53.1 1.4 copy-start.33
  58.1 1.0 copy-start.12
  59.1 0.9 copy-start.40
  62.9 16.7 %all-to-all-start.3 = ((f32[32,16,128]{2,1,0:T(8,128)}), f32[32,16,128]{2,1,0:T(8,128)}, u32[]{:S(2)}, u32[]{:S(2)}) async-start(f32[32,16,128]{2,1,0:T(8,128)} %copy-done.62), calls=%async_computation.3 | async-start | bytes 524288 | tf_op jit(solution)/shard_map/all_to_all | solution.py:313
  67.5 1.0 copy-start.3
  79.6 1.0 copy-start.4
  84.7 27.6 %copy-start.22 = (f32[512,128]{1,0:T(8,128)}, f32[512,128]{1,0:T(8,128)S(1)}, u32[]{:S(2)}) copy-start(f32[512,128]{1,0:T(8,128)S(1)} %get-tuple-element.63.field_ref.q_ref.q0_ref) | copy-start | bytes 786436
  113.4 13.4 %all-to-all-start.6 = ((f32[16,8,128]{2,1,0:T(8,128)}), f32[16,8,128]{2,1,0:T(8,128)}, u32[]{:S(2)}, u32[]{:S(2)}) async-start(f32[16,8,128]{2,1,0:T(8,128)} %copy-done.59), calls=%async_computation.6 | async-start | bytes 131072 | tf_op jit(solution)/shard_map/all_to_all | solution.py:313
  126.8 1.0 copy-start.5
  133.2 16.7 %all-to-all-start.7 = ((f32[32,16,128]{2,1,0:T(8,128)}), f32[32,16,128]{2,1,0:T(8,128)}, u32[]{:S(2)}, u32[]{:S(2)}) async-start(f32[32,16,128]{2,1,0:T(8,128)} %copy-done.61), calls=%async_computation.7 | async-start | bytes 524288 | tf_op jit(solution)/shard_map/all_to_all | solution.py:313
  137.8 1.0 copy-start.8
  149.9 1.0 copy-start.9
  155.0 26.2 %copy-start.43 = (f32[512,128]{1,0:T(8,128)}, f32[512,128]{1,0:T(8,128)S(1)}, u32[]{:S(2)}) copy-start(f32[512,128]{1,0:T(8,128)S(1)} %get-tuple-element.70.field_ref.v1_ref) | copy-start | bytes 786436
  181.3 6.6 %copy-start.17 = (f32[512,128]{1,0:T(8,128)S(1)}, f32[512,128]{1,0:T(8,128)}, u32[]{:S(2)}) copy-start(f32[512,128]{1,0:T(8,128)} %copy-done.15) | copy-start | bytes 786436
  182.3 5.6 %copy-start.31 = (bf16[512,128]{1,0:T(8,128)(2,1)S(1)}, bf16[512,128]{1,0:T(8,128)(2,1)}, u32[]{:S(2)}) copy-start(bf16[512,128]{1,0:T(8,128)(2,1)} %copy-done.28) | copy-start | bytes 393220
  182.3 13.5 %all-to-all-start.10 = ((f32[16,8,128]{2,1,0:T(8,128)}), f32[16,8,128]{2,1,0:T(8,128)}, u32[]{:S(2)}, u32[]{:S(2)}) async-start(f32[16,8,128]{2,1,0:T(8,128)} %copy-done.58), calls=%async_computation.10 | async-start | bytes 131072 | tf_op jit(solution)/shard_map/all_to_all | solution.py:313
  189.8 6.1 %copy-start.10 = (f32[512,128]{1,0:T(8,128)S(1)}, f32[512,128]{1,0:T(8,128)}, u32[]{:S(2)}) copy-start(f32[512,128]{1,0:T(8,128)} %copy-done.7) | copy-start | bytes 786436
  189.8 6.1 %copy-start.14 = (bf16[512,256]{1,0:T(8,128)(2,1)S(1)}, bf16[512,256]{1,0:T(8,128)(2,1)}, u32[]{:S(2)}) copy-start(bf16[512,256]{1,0:T(8,128)(2,1)} %copy-done.11) | copy-start | bytes 786436
  195.8 1.0 copy-start.38
  197.7 6.3 %copy-start.25 = (f32[512,128]{1,0:T(8,128)S(1)}, f32[512,128]{1,0:T(8,128)}, u32[]{:S(2)}) copy-start(f32[512,128]{1,0:T(8,128)} %copy-done.22) | copy-start | bytes 786436
  197.7 6.3 %copy-start.45 = (f32[512,128]{1,0:T(8,128)S(1)}, f32[512,128]{1,0:T(8,128)}, u32[]{:S(2)}) copy-start(f32[512,128]{1,0:T(8,128)} %copy-done.43) | copy-start | bytes 786436
  200.0 4.0 %copy-start.6 = (f32[512,128]{1,0:T(8,128)S(1)}, f32[512,128]{1,0:T(8,128)}, u32[]{:S(2)}) copy-start(f32[512,128]{1,0:T(8,128)} %copy-done.2) | copy-start | bytes 786436
  200.0 4.0 %copy-start.21 = (f32[512,128]{1,0:T(8,128)S(1)}, f32[512,128]{1,0:T(8,128)}, u32[]{:S(2)}) copy-start(f32[512,128]{1,0:T(8,128)} %copy-done.18) | copy-start | bytes 786436
  200.0 16.1 %all-to-all-start.11 = ((f32[32,16,128]{2,1,0:T(8,128)}), f32[32,16,128]{2,1,0:T(8,128)S(1)}, u32[]{:S(2)}, u32[]{:S(2)}) async-start(f32[32,16,128]{2,1,0:T(8,128)} %copy-done.60), calls=%async_computation.11 | async-start | bytes 524288 | tf_op jit(solution)/shard_map/all_to_all | solution.py:313
  204.0 1.0 copy-start.78
  216.1 1.0 copy-start.72
  217.1 25.8 %copy-start.68 = (f32[512,128]{1,0:T(8,128)S(1)}, f32[512,128]{1,0:T(8,128)}, u32[]{:S(2)}) copy-start(f32[512,128]{1,0:T(8,128)} %copy-done.67) | copy-start | bytes 786436
  217.1 25.8 %copy-start.70 = (f32[512,128]{1,0:T(8,128)S(1)}, f32[512,128]{1,0:T(8,128)}, u32[]{:S(2)}) copy-start(f32[512,128]{1,0:T(8,128)} %copy-done.69) | copy-start | bytes 786436
  217.4 25.5 %copy-start.66 = (f32[512,128]{1,0:T(8,128)S(1)}, f32[512,128]{1,0:T(8,128)}, u32[]{:S(2)}) copy-start(f32[512,128]{1,0:T(8,128)} %copy-done.65) | copy-start | bytes 786436
  229.6 13.3 %copy-start.64 = (f32[512,128]{1,0:T(8,128)S(1)}, f32[512,128]{1,0:T(8,128)}, u32[]{:S(2)}) copy-start(f32[512,128]{1,0:T(8,128)} %copy-done.63) | copy-start | bytes 786436
  (45 other events, 35.4 us)

commit v2 on v1

--- a/solution.py
+++ b/solution.py
@@ -66,16 +66,31 @@
     return whole.T.reshape(MSG_GROUP)
 
 
-def send_faces(field, pick, weight, msg_ref):
-    rows = exact(pick, field)
-    msg_ref[:, :8, :] = (rows[:SLOTS] * weight).reshape(N_SUB, 8, RHS)
+def one_hot(same):
+    return jnp.where(same, 1.0, 0.0).astype(BF16)
+
+
+def pick_of(columns):
+    lane = lax.broadcasted_iota(jnp.int32, (SLOTS, ROWS), 1).astype(F32)
+    return jnp.concatenate([one_hot(columns[:, i : i + 1] == lane) for i in range(2)], axis=0)
+
+
+def place_of(rows):
+    row = lax.broadcasted_iota(jnp.int32, (ROWS, SLOTS), 0).astype(F32)
+    return jnp.concatenate([one_hot(rows[i : i + 1] == row) for i in (1, 0)], axis=1)
+
+
+def send_faces(field, columns_ref, msg_ref):
+    columns = columns_ref[...]
+    rows = exact(pick_of(columns), field)
+    msg_ref[:, :8, :] = (rows[:SLOTS] * columns[:, 2:3]).reshape(N_SUB, 8, RHS)
     msg_ref[:, 8:, :] = rows[SLOTS:].reshape(N_SUB, 8, RHS)
 
 
-def coupled_of(recv_ref, place, weight):
+def coupled_of(recv_ref, rows_ref, columns_ref):
     out = recv_ref[:, :8, :].reshape(SLOTS, RHS)
-    back = recv_ref[:, 8:, :].reshape(SLOTS, RHS) * weight
-    return exact(place, jnp.concatenate([out, back], axis=0))
+    back = recv_ref[:, 8:, :].reshape(SLOTS, RHS) * columns_ref[:, 2:3]
+    return exact(place_of(rows_ref[...]), jnp.concatenate([out, back], axis=0))
 
 
 def coarse_of(recv_ref, basis_t):
@@ -91,26 +106,20 @@
     msg_ref[...] = pack(dot3(high, low, right_ref[...]), jnp.zeros((8, RHS), F32))
 
 
-def k_slots(faces_ref, lands_ref, counts_ref, weight_ref, pick_ref, place_ref, wcol_ref):
+def k_slots(faces_ref, lands_ref, counts_ref, weight_ref, rows_ref, columns_ref):
     peer = lax.broadcasted_iota(jnp.int32, (N_SUB, SLOTS), 0)
     slot = lax.broadcasted_iota(jnp.int32, (N_SUB, SLOTS), 1)
-    spread = jnp.where(slot // 8 == peer, 1.0, 0.0).astype(BF16)
+    spread = one_hot(slot // 8 == peer)
     counts = jnp.broadcast_to(counts_ref[...].astype(F32), (8, N_SUB)).astype(BF16)
     counts = dot(counts, spread)[:1]
     place_in = (lax.broadcasted_iota(jnp.int32, (1, SLOTS), 1) % 8).astype(F32)
     weights = jnp.where(place_in < counts, weight_ref[...], 0.0)
-    wcol_ref[...] = jnp.broadcast_to(weights, (128, SLOTS)).T
-    faces, lands = faces_ref[...], lands_ref[...]
-    row = lax.broadcasted_iota(jnp.int32, (ROWS, SLOTS), 0)
-    place_ref[:, :SLOTS] = jnp.where(row == lands, 1.0, 0.0).astype(BF16)
-    place_ref[:, SLOTS:] = jnp.where(row == faces, 1.0, 0.0).astype(BF16)
-    lane = lax.broadcasted_iota(jnp.int32, (SLOTS, 128), 1).astype(F32)
-    for at, index in enumerate((faces, lands)):
-        column = jnp.broadcast_to(index.astype(F32), (128, SLOTS)).T
-        for t in range(ROWS // 128):
-            pick_ref[at * SLOTS : (at + 1) * SLOTS, t * 128 : (t + 1) * 128] = jnp.where(
-                column == lane + float(t * 128), 1.0, 0.0
-            ).astype(BF16)
+    index = lax.broadcasted_iota(jnp.int32, (8, SLOTS), 0)
+    rows = jnp.where(index == 2, weights, 0.0)
+    rows = jnp.where(index == 0, faces_ref[...].astype(F32), rows)
+    rows = jnp.where(index == 1, lands_ref[...].astype(F32), rows)
+    rows_ref[...] = rows
+    columns_ref[...] = jnp.concatenate([rows, jnp.zeros((120, SLOTS), F32)], axis=0).T
 
 
 def k_setup(cols_ref, values_ref, mass_ref, bh_ref, bl_ref, base_ref, dense_ref):
@@ -139,26 +148,27 @@
     base_ref[...] = mass + jnp.sum(both, axis=1, keepdims=True)
 
 
-def k_factor(factor_ref, basis_ref, inverse_ref, gh_ref, gl_ref, sh_ref, sl_ref, st_ref, ch_ref, cl_ref):
+def k_factor(factor_ref, gh_ref, gl_ref):
     for b in range(ROWS // LF):
         rows = slice(b * LF, (b + 1) * LF)
         block = factor_ref[rows, :]
         high, low = split(block.T)
         gh_ref[rows, :], gl_ref[rows, :] = split(dot3(high, low, block))
+
+
+def k_coarse(basis_ref, inverse_ref, sh_ref, sl_ref, st_ref, ch_ref, cl_ref):
     high, low = split(basis_ref[...])
     sh_ref[...], sl_ref[...] = high, low
     high, low = high.astype(F32), low.astype(F32)
     st_ref[...] = jnp.concatenate([high, low, high, jnp.zeros((NC, ROWS), F32)], axis=0).T.astype(BF16)
-    high, low = split(inverse_ref[...])
-    ch_ref[:NC, :], cl_ref[:NC, :] = high, low
-    ch_ref[NC:, :] = jnp.zeros((128 - NC, N_SUB * NC), BF16)
-    cl_ref[NC:, :] = jnp.zeros((128 - NC, N_SUB * NC), BF16)
-
-
-def k_gather_first(recv_ref, wcol_ref, msg_ref):
+    ch_ref[...], cl_ref[...] = split(inverse_ref[...])
+
+
+def k_gather_first(recv_ref, columns_ref, msg_ref):
     total = jnp.sum(recv_ref[...], axis=0)
     lane = lax.broadcasted_iota(jnp.int32, MSG_SUB, 2)
-    msg_ref[...] = jnp.where(lane == 127, wcol_ref[...].reshape(MSG_SUB), total[None])
+    weight = jnp.broadcast_to(columns_ref[:, 2:3], (SLOTS, 128)).reshape(MSG_SUB)
+    msg_ref[...] = jnp.where(lane == 127, weight, total[None])
 
 
 def k_gather(recv_ref, msg_ref):
@@ -178,34 +188,33 @@
     stack = jnp.concatenate([high, whole - high], axis=0).astype(BF16)
     first = dot_nt(stack, ch_ref[...])
     solved = first[:8] + (first[8:] + dot_nt(stack, cl_ref[...])[:8])
-    tile = jnp.where(lane < NC, solved, aux)
+    tile = jnp.where(lane < NC, jnp.concatenate([solved, solved], axis=1), aux)
     msg_ref[...] = jnp.broadcast_to(tile[None], MSG_GROUP)
 
 
-def k_diag(recv_ref, place_ref, wcol_ref, base_ref, diag_ref, inv_ref):
+def k_diag(recv_ref, rows_ref, columns_ref, base_ref, diag_ref):
     lane = lax.broadcasted_iota(jnp.int32, (SLOTS, 128), 1)
     got = jnp.where(lane == 127, recv_ref[...].reshape(SLOTS, 128), 0.0)
     got = jnp.broadcast_to(jnp.sum(got, axis=1, keepdims=True), (SLOTS, 128))
-    both = jnp.concatenate([got, wcol_ref[...]], axis=0)
-    diag = base_ref[...]
+    both = jnp.concatenate([got, jnp.broadcast_to(columns_ref[:, 2:3], (SLOTS, 128))], axis=0)
+    diag, place = base_ref[...], place_of(rows_ref[...])
     for part in split3(both):
-        diag = diag + dot(place_ref[...], part)
+        diag = diag + dot(place, part)
     diag_ref[...] = diag
-    inv_ref[...] = 1.0 / diag
-
-
-def k_smooth(field_ref, inv_ref, gh_ref, gl_ref, out_ref):
+
+
+def k_smooth(field_ref, diag_ref, gh_ref, gl_ref, out_ref):
     for b in range(ROWS // LF):
         rows = slice(b * LF, (b + 1) * LF)
         field = field_ref[rows, :]
-        out_ref[rows, :] = field * inv_ref[rows, :] + dot3(gh_ref[rows, :], gl_ref[rows, :], field)
-
-
-def k_start(recv_ref, smooth_ref, st_ref, pick_ref, wcol_ref, z_ref, msg_ref):
+        out_ref[rows, :] = field / diag_ref[rows, :] + dot3(gh_ref[rows, :], gl_ref[rows, :], field)
+
+
+def k_start(recv_ref, smooth_ref, st_ref, columns_ref, z_ref, msg_ref):
     coarse, _ = coarse_of(recv_ref, st_ref[...])
     z = smooth_ref[...] + coarse
     z_ref[...] = z
-    send_faces(z, pick_ref[...], wcol_ref[...], msg_ref)
+    send_faces(z, columns_ref, msg_ref)
 
 
 def k_local0(z_ref, right_ref, diag_ref, bh_ref, bl_ref, out_ref, dots_ref):
@@ -214,15 +223,15 @@
     dots_ref[...] = tile_of(rowdot(right_ref[...], z))
 
 
-def k_image(recv_ref, local_ref, z_ref, dots_ref, place_ref, wcol_ref, sh_ref, sl_ref, image_ref, msg_ref):
-    image = local_ref[...] - coupled_of(recv_ref, place_ref[...], wcol_ref[...])
+def k_image(recv_ref, local_ref, z_ref, dots_ref, rows_ref, columns_ref, sh_ref, sl_ref, image_ref, msg_ref):
+    image = local_ref[...] - coupled_of(recv_ref, rows_ref, columns_ref)
     image_ref[...] = image
     index = lax.broadcasted_iota(jnp.int32, (8, RHS), 0)
     aux = jnp.where(index == 2, rowdot(z_ref[...], image), dots_ref[...])
     msg_ref[...] = pack(dot3(sh_ref[...], sl_ref[...], image), aux)
 
 
-def k_step0(recv_ref, smooth_ref, z_ref, st_ref, pick_ref, wcol_ref, u_ref, znew_ref, scal_ref, msg_ref):
+def k_step0(recv_ref, smooth_ref, z_ref, st_ref, columns_ref, u_ref, znew_ref, scal_ref, msg_ref):
     coarse, aux = coarse_of(recv_ref, st_ref[...])
     gamma, pap = aux[0:1], aux[2:3]
     alpha = gamma / pap
@@ -231,7 +240,7 @@
     znew = z_ref[...] - alpha * u
     znew_ref[...] = znew
     scal_ref[...] = tile_of(alpha, gamma, pap)
-    send_faces(znew, pick_ref[...], wcol_ref[...], msg_ref)
+    send_faces(znew, columns_ref, msg_ref)
 
 
 def k_local1(z_ref, right_ref, q_ref, scal_ref, diag_ref, bh_ref, bl_ref, out_ref, resid_ref, dots_ref):
@@ -243,7 +252,7 @@
 
 
 def k_step1(
-    recv_ref, smooth_ref, u_ref, z_ref, scal_ref, st_ref, pick_ref, wcol_ref, znew_ref, scalnew_ref, msg_ref
+    recv_ref, smooth_ref, u_ref, z_ref, scal_ref, st_ref, columns_ref, znew_ref, scalnew_ref, msg_ref
 ):
     coarse, aux = coarse_of(recv_ref, st_ref[...])
     gamma, cross, zaz = aux[0:1], aux[1:2], aux[2:3]
@@ -254,7 +263,7 @@
     znew = z_ref[...] - alpha * u
     znew_ref[...] = znew
     scalnew_ref[...] = tile_of(alpha, gamma, pap, beta)
-    send_faces(znew, pick_ref[...], wcol_ref[...], msg_ref)
+    send_faces(znew, columns_ref, msg_ref)
 
 
 def k_local2(
@@ -273,8 +282,8 @@
     dots_ref[...] = tile_of(rowdot(resid, z), rowdot(z, image))
 
 
-def k_last_image(recv_ref, local_ref, z_ref, dots_ref, place_ref, wcol_ref, image_ref, msg_ref):
-    image = local_ref[...] - coupled_of(recv_ref, place_ref[...], wcol_ref[...])
+def k_last_image(recv_ref, local_ref, z_ref, dots_ref, rows_ref, columns_ref, image_ref, msg_ref):
+    image = local_ref[...] - coupled_of(recv_ref, rows_ref, columns_ref)
     image_ref[...] = image
     index = lax.broadcasted_iota(jnp.int32, (8, RHS), 0)
     aux = jnp.where(index == 2, rowdot(z_ref[...], image), dots_ref[...])
@@ -291,17 +300,25 @@
     rout_ref[...] = resid_ref[...] - alpha * (v_ref[...] + beta * image_ref[...])
 
 
-def call(kernel, outs, *args, smem=0, scratch=(), flops=1e6):
+class Far:
+    def __init__(self, array):
+        self.array = array
+
+
+def call(kernel, outs, *args, smem=0, scratch=(), flops=1e6, far=False):
+    near = pl.BlockSpec(memory_space=pltpu.VMEM)
     specs = [pl.BlockSpec(memory_space=pltpu.SMEM)] * smem
-    specs += [pl.BlockSpec(memory_space=pltpu.VMEM)] * (len(args) - smem)
+    specs += [pl.BlockSpec() if isinstance(a, Far) else near for a in args[smem:]]
+    args = [pltpu.with_memory_space_constraint(a.array, pltpu.HBM) if isinstance(a, Far) else a for a in args]
     single = not isinstance(outs, list)
-    shapes = [jax.ShapeDtypeStruct(s, d) for s, d in ([outs] if single else outs)]
-    moved = sum(a.size * a.dtype.itemsize for a in [*args, *shapes])
+    sizes = [jax.ShapeDtypeStruct(s, d) for s, d in ([outs] if single else outs)]
+    shapes = [pltpu.HBM(a.shape, a.dtype) for a in sizes] if far else sizes
+    moved = sum(a.size * a.dtype.itemsize for a in [*args, *sizes])
     out = pl.pallas_call(
         kernel,
         out_shape=shapes,
         in_specs=specs,
-        out_specs=[pl.BlockSpec(memory_space=pltpu.VMEM)] * len(shapes),
+        out_specs=[pl.BlockSpec() if far else near] * len(shapes),
         scratch_shapes=list(scratch),
         compiler_params=pltpu.CompilerParams(vmem_limit_bytes=24 << 20),
         cost_estimate=pl.CostEstimate(flops=int(flops), bytes_accessed=int(moved), transcendentals=0),
@@ -331,64 +348,63 @@
     to_group, to_sub, to_face = (MSG_GROUP, F32), (MSG_SUB, F32), (MSG_FACE, F32)
     square = ((ROWS, ROWS), BF16)
 
-    part = swap(call(k_first, to_group, right_side, basis), "group")
-    pick, place, wcol = call(
-        k_slots, [square, square, ((SLOTS, 128), F32)], face_rows, land_rows, face_counts, face_weight
-    )
-    whole = swap(call(k_gather_first, to_sub, part, wcol), "sub")
-    gh, gl, sh, sl, st, ch, cl = call(
-        k_factor,
-        [((ROWS, LF), BF16)] * 2
-        + [((NC, ROWS), BF16)] * 2
-        + [((ROWS, 256), BF16)]
-        + [((128, N_SUB * NC), BF16)] * 2,
-        local_factor,
-        basis,
-        coarse_inverse,
-    )
+    part = swap(call(k_first, to_group, Far(right_side), Far(basis)), "group")
+    rows, columns = call(
+        k_slots, [((8, SLOTS), F32), ((SLOTS, 128), F32)], face_rows, land_rows, face_counts, face_weight
+    )
+    whole = swap(call(k_gather_first, to_sub, part, columns), "sub")
+    sh, sl, st, ch, cl = call(
+        k_coarse,
+        [((NC, ROWS), BF16)] * 2 + [((ROWS, 256), BF16)] + [((NC, N_SUB * NC), BF16)] * 2,
+        Far(basis),
+        Far(coarse_inverse),
+    )
+    gh, gl = call(k_factor, [((ROWS, LF), BF16)] * 2, Far(local_factor), far=True)
     bh, bl, base = call(
         k_setup,
         [square, square, vec],
         block_cols,
-        block_values,
-        mass,
+        Far(block_values),
+        Far(mass),
         smem=1,
         scratch=[pltpu.VMEM((ROWS, ROWS), F32)],
-    )
+        far=True,
+    )
+    gh, gl, bh, bl, base, right = (Far(a) for a in (gh, gl, bh, bl, base, right_side))
     solved = swap(call(k_solve, to_group, whole, ch, cl), "group")
-    diag, inv = call(k_diag, [vec, vec], whole, place, wcol, base)
+    diag = Far(call(k_diag, vec, whole, rows, columns, base, far=True))
 
     def smooth(field):
-        return call(k_smooth, vec, field, inv, gh, gl)
+        return call(k_smooth, vec, field, diag, gh, gl)
 
     def coarse(msg):
         whole = swap(call(k_gather, to_sub, swap(msg, "group")), "sub")
         return swap(call(k_solve, to_group, whole, ch, cl), "group")
 
     def image(msg, near, z, dots):
-        return call(k_image, [vec, to_group], swap(msg, "sub"), near, z, dots, place, wcol, sh, sl)
-
-    z0, msg = call(k_start, [vec, to_face], solved, smooth(right_side), st, pick, wcol)
-    near, dots = call(k_local0, [vec, tile], z0, right_side, diag, bh, bl)
+        return call(k_image, [vec, to_group], swap(msg, "sub"), near, z, dots, rows, columns, sh, sl)
+
+    z0, msg = call(k_start, [vec, to_face], solved, smooth(right), st, columns)
+    near, dots = call(k_local0, [vec, tile], z0, right, diag, bh, bl)
     q0, msg = image(msg, near, z0, dots)
 
     solved = coarse(msg)
     u0, z1, scal0, msg = call(
-        k_step0, [vec, vec, tile, to_face], solved, smooth(q0), z0, st, pick, wcol
+        k_step0, [vec, vec, tile, to_face], solved, smooth(q0), z0, st, columns
     )
     near, resid1, dots = call(
-        k_local1, [vec, vec, tile], z1, right_side, q0, scal0, diag, bh, bl
+        k_local1, [vec, vec, tile], z1, right, q0, scal0, diag, bh, bl
     )
     v1, msg = image(msg, near, z1, dots)
 
     solved = coarse(msg)
     z2, scal1, msg = call(
-        k_step1, [vec, tile, to_face], solved, smooth(v1), u0, z1, scal0, st, pick, wcol
+        k_step1, [vec, tile, to_face], solved, smooth(v1), u0, z1, scal0, st, columns
     )
     near, direction, im, x, resid2, dots = call(
         k_local2, [vec] * 5 + [tile], z2, z1, z0, v1, q0, resid1, scal0, scal1, diag, bh, bl
     )
-    v2, msg = call(k_last_image, [vec, to_group], swap(msg, "sub"), near, z2, dots, place, wcol)
+    v2, msg = call(k_last_image, [vec, to_group], swap(msg, "sub"), near, z2, dots, rows, columns)
     whole = swap(call(k_gather, to_sub, swap(msg, "group")), "sub")
     return tuple(call(k_end, [vec, vec], whole, scal1, z2, v2, direction, im, x, resid2))
 

time: 246 us -> 220 us (0.89)
  local copies, waits for them, and re-layouts: 47.1 us -> 0.02 us
  Pallas kernels: 17.7 us -> 30.8 us
  waiting for transfers between devices: 47.1 us -> 59.7 us
  starting transfers between devices: 51.5 us -> 47.8 us
    unnamed x170 -> x10, local copies, waits for them, and re-layouts: 47.1 us -> 0.02 us
    pallas_call x25 -> x26, Pallas kernels: 17.7 us -> 30.8 us  [call(): pl.pallas_call(kernel, out_shape=shapes, in_specs=specs, out_specs=[pl.Bl...]
    all_to_all x8, waiting for transfers between devices: 47.1 us -> 59.7 us  [swap(): return lax.all_to_all(x, axis, split_axis=0, concat_axis=0, tiled=True)]
    all_to_all x8, starting transfers between devices: 51.5 us -> 47.8 us  [swap(): return lax.all_to_all(x, axis, split_axis=0, concat_axis=0, tiled=True)]
  transfers between devices with their start and end apart: 8 -> 8, of which waited for: 8 -> 7; matrix products, arithmetic and copies ran while one was open for 0% -> 0% of each run, Pallas kernels for 2% -> 8%
where the time goes in v2:
time: 220 us; the launch traced here: 219 us
  blocking collectives  79.9 us (36%)
  waiting for transfers between devices  59.7 us (27%)
  starting transfers between devices  47.8 us (22%)
  Pallas kernels  30.8 us (14%)
    all_to_all x6, blocking collectives, swap(): return lax.all_to_all(x, axis, split_axis=0, concat_axis=0, tiled=True)  79.9 us
    all_to_all x8, waiting for transfers between devices, swap(): return lax.all_to_all(x, axis, split_axis=0, concat_axis=0, tiled=True)  59.7 us
    all_to_all x8, starting transfers between devices, swap(): return lax.all_to_all(x, axis, split_axis=0, concat_axis=0, tiled=True)  47.8 us
    pallas_call x26, Pallas kernels, call(): pl.pallas_call(kernel, out_shape=shapes, in_specs=specs, out_specs=[pl.Bl...  30.8 us
  transfers between devices with their start and end apart: 8, of which 7 were waited for; matrix products, arithmetic and copies ran while one was open for 0% of the time, Pallas kernels for 8%

profile of v2, /device:TPU:1, one launch (start us, length us, event | category | flops | bytes accessed | tf_op | source)
XLA Modules:
  0.0 219.1 jit_solution(8465966456882555746)
XLA Ops:
  0.6 1.9 shard_map.122
  2.6 10.3 %all-to-all-start = ((f32[16,8,128]{2,1,0:T(8,128)}), f32[16,8,128]{2,1,0:T(8,128)S(1)}, u32[]{:S(2)}, u32[]{:S(2)}) async-start(f32[16,8,128]{2,1,0:T(8,128)} %shard_map.122), calls=%async_computation | async-start | bytes 131072 | tf_op jit(solution)/shard_map/all_to_all | solution.py:330
  12.9 0.0 copy-done.1
  12.9 0.0 copy-done.2
  12.9 0.0 copy-done.3
  12.9 0.2 shard_map.123
  13.2 7.5 %all-to-all-done.recv_ref = f32[16,8,128]{2,1,0:T(8,128)S(1)} async-done(((f32[16,8,128]{2,1,0:T(8,128)}), f32[16,8,128]{2,1,0:T(8,128)S(1)}, u32[]{:S(2)}, u32[]{:S(2)}) %all-to-all-start) | async-done | bytes 65568 | tf_op jit(solution)/shard_map/all_to_all | solution.py:330
  20.7 0.8 shard_map.124
  21.5 11.3 %all-to-all-start.1 = ((f32[32,8,128]{2,1,0:T(8,128)}), f32[32,8,128]{2,1,0:T(8,128)S(1)}, u32[]{:S(2)}, u32[]{:S(2)}) async-start(f32[32,8,128]{2,1,0:T(8,128)} %shard_map.124), calls=%async_computation.1 | async-start | bytes 262144 | tf_op jit(solution)/shard_map/all_to_all | solution.py:330
  32.8 1.4 shard_map.125
  34.2 8.4 %all-to-all-done.1.recv_ref = f32[32,8,128]{2,1,0:T(8,128)S(1)} async-done(((f32[32,8,128]{2,1,0:T(8,128)}), f32[32,8,128]{2,1,0:T(8,128)S(1)}, u32[]{:S(2)}, u32[]{:S(2)}) %all-to-all-start.1) | async-done | bytes 131104 | tf_op jit(solution)/shard_map/all_to_all | solution.py:330
  42.6 1.0 shard_map.126
  43.6 4.8 %all-to-all-start.2 = ((f32[16,8,128]{2,1,0:T(8,128)}), f32[16,8,128]{2,1,0:T(8,128)S(1)}, u32[]{:S(2)}, u32[]{:S(2)}) async-start(f32[16,8,128]{2,1,0:T(8,128)} %shard_map.126), calls=%async_computation.2 | async-start | bytes 131072 | tf_op jit(solution)/shard_map/all_to_all | solution.py:330
  48.4 2.0 shard_map.129
  50.4 3.2 %shard_map.127 = (bf16[512,512]{1,0:T(8,128)(2,1)}, bf16[512,512]{1,0:T(8,128)(2,1)}, f32[512,128]{1,0:T(8,128)}) custom-call(s32[8,8]{1,0:T(8,128)S(1)} %copy-done, f32[512,512]{1,0:T(8,128)} %values_ref.1, f32[1,512]{1,0:T(1,128)} %mass_ref.1), custom_call_target="tpu_custom_call" | custom-call | flops 1000000 | bytes 2361600 | tf_op jit(solution)/shard_map/pallas_call | solution.py:317
  53.6 2.4 %shard_map.128.diag_ref = f32[512,128]{1,0:T(8,128)} custom-call(f32[32,8,128]{2,1,0:T(8,128)S(1)} %all-to-all-done.1.recv_ref, f32[8,256]{1,0:T(8,128)S(1)} %get-tuple-element.43.rows_ref, f32[256,128]{1,0:T(8,128)S(1)} %get-tuple-element.40.columns_ref, f32[512,128]{1,0:T(8,128)} %get-tuple-element.44.base_ref), custom_call_target="tpu_custom_call" | custom-call | flops 1000000 | bytes 794624 | tf_op jit(solution)/shard_map/pallas_call | solution.py:317
  55.9 1.4 shard_map.130.smooth_ref
  57.3 0.0 all-to-all-done.2.recv_ref
  57.3 1.3 shard_map.131
  58.7 3.9 %all-to-all-start.3 = ((f32[32,16,128]{2,1,0:T(8,128)}), f32[32,16,128]{2,1,0:T(8,128)S(1)}, u32[]{:S(2)}, u32[]{:S(2)}) async-start(f32[32,16,128]{2,1,0:T(8,128)} %get-tuple-element.48), calls=%async_computation.3 | async-start | bytes 524288 | tf_op jit(solution)/shard_map/all_to_all | solution.py:330
  62.5 1.8 shard_map.132
  64.3 10.2 %all-to-all-done.3.recv_ref = f32[32,16,128]{2,1,0:T(8,128)S(1)} async-done(((f32[32,16,128]{2,1,0:T(8,128)}), f32[32,16,128]{2,1,0:T(8,128)S(1)}, u32[]{:S(2)}, u32[]{:S(2)}) %all-to-all-start.3) | async-done | bytes 262176 | tf_op jit(solution)/shard_map/all_to_all | solution.py:330
  74.5 0.6 shard_map.133
  75.2 16.4 %all_to_all.70.recv_ref = f32[16,8,128]{2,1,0:T(8,128)S(1)} all-to-all(f32[16,8,128]{2,1,0:T(8,128)S(1)} %get-tuple-element.56), channel_id=1, replica_groups=mesh['group'=16,'sub'=32] {'group'}, dimensions={0} | all-to-all | bytes 131072 | tf_op jit(solution)/shard_map/all_to_all | solution.py:330
  91.6 13.2 %all_to_all.71.recv_ref = f32[32,8,128]{2,1,0:T(8,128)S(1)} all-to-all(f32[32,8,128]{2,1,0:T(8,128)S(1)} %shard_map.134), channel_id=1, replica_groups=mesh['group'=16,'sub'=32] {'sub'}, dimensions={0} | all-to-all | bytes 262144 | tf_op jit(solution)/shard_map/all_to_all | solution.py:330
  104.7 1.0 shard_map.135
  105.8 4.9 %all-to-all-start.6 = ((f32[16,8,128]{2,1,0:T(8,128)}), f32[16,8,128]{2,1,0:T(8,128)S(1)}, u32[]{:S(2)}, u32[]{:S(2)}) async-start(f32[16,8,128]{2,1,0:T(8,128)} %shard_map.135), calls=%async_computation.6 | async-start | bytes 131072 | tf_op jit(solution)/shard_map/all_to_all | solution.py:330
  110.6 1.3 shard_map.136.smooth_ref
  111.9 6.5 %all-to-all-done.6.recv_ref = f32[16,8,128]{2,1,0:T(8,128)S(1)} async-done(((f32[16,8,128]{2,1,0:T(8,128)}), f32[16,8,128]{2,1,0:T(8,128)S(1)}, u32[]{:S(2)}, u32[]{:S(2)}) %all-to-all-start.6) | async-done | bytes 65568 | tf_op jit(solution)/shard_map/all_to_all | solution.py:330
  118.5 1.3 shard_map.137
  119.8 3.9 %all-to-all-start.7 = ((f32[32,16,128]{2,1,0:T(8,128)}), f32[32,16,128]{2,1,0:T(8,128)S(1)}, u32[]{:S(2)}, u32[]{:S(2)}) async-start(f32[32,16,128]{2,1,0:T(8,128)} %get-tuple-element.58), calls=%async_computation.7 | async-start | bytes 524288 | tf_op jit(solution)/shard_map/all_to_all | solution.py:330
  123.7 1.8 shard_map.138
  125.5 10.3 %all-to-all-done.7.recv_ref = f32[32,16,128]{2,1,0:T(8,128)S(1)} async-done(((f32[32,16,128]{2,1,0:T(8,128)}), f32[32,16,128]{2,1,0:T(8,128)S(1)}, u32[]{:S(2)}, u32[]{:S(2)}) %all-to-all-start.7) | async-done | bytes 262176 | tf_op jit(solution)/shard_map/all_to_all | solution.py:330
  135.8 0.6 shard_map.139
  136.4 12.0 %all_to_all.72.recv_ref = f32[16,8,128]{2,1,0:T(8,128)S(1)} all-to-all(f32[16,8,128]{2,1,0:T(8,128)S(1)} %get-tuple-element.63), channel_id=1, replica_groups=mesh['group'=16,'sub'=32] {'group'}, dimensions={0} | all-to-all | bytes 131072 | tf_op jit(solution)/shard_map/all_to_all | solution.py:330
  148.5 13.2 %all_to_all.73.recv_ref = f32[32,8,128]{2,1,0:T(8,128)S(1)} all-to-all(f32[32,8,128]{2,1,0:T(8,128)S(1)} %shard_map.140), channel_id=1, replica_groups=mesh['group'=16,'sub'=32] {'sub'}, dimensions={0} | all-to-all | bytes 262144 | tf_op jit(solution)/shard_map/all_to_all | solution.py:330
  161.6 1.0 shard_map.141
  162.6 4.9 %all-to-all-start.10 = ((f32[16,8,128]{2,1,0:T(8,128)}), f32[16,8,128]{2,1,0:T(8,128)S(1)}, u32[]{:S(2)}, u32[]{:S(2)}) async-start(f32[16,8,128]{2,1,0:T(8,128)} %shard_map.141), calls=%async_computation.10 | async-start | bytes 131072 | tf_op jit(solution)/shard_map/all_to_all | solution.py:330
  167.5 1.3 shard_map.142.smooth_ref
  168.8 6.5 %all-to-all-done.10.recv_ref = f32[16,8,128]{2,1,0:T(8,128)S(1)} async-done(((f32[16,8,128]{2,1,0:T(8,128)}), f32[16,8,128]{2,1,0:T(8,128)S(1)}, u32[]{:S(2)}, u32[]{:S(2)}) %all-to-all-start.10) | async-done | bytes 65568 | tf_op jit(solution)/shard_map/all_to_all | solution.py:330
  175.3 1.3 shard_map.143
  176.7 3.9 %all-to-all-start.11 = ((f32[32,16,128]{2,1,0:T(8,128)}), f32[32,16,128]{2,1,0:T(8,128)S(1)}, u32[]{:S(2)}, u32[]{:S(2)}) async-start(f32[32,16,128]{2,1,0:T(8,128)} %get-tuple-element.66), calls=%async_computation.11 | async-start | bytes 524288 | tf_op jit(solution)/shard_map/all_to_all | solution.py:330
  180.5 1.8 shard_map.144
  182.4 10.2 %all-to-all-done.11.recv_ref = f32[32,16,128]{2,1,0:T(8,128)S(1)} async-done(((f32[32,16,128]{2,1,0:T(8,128)}), f32[32,16,128]{2,1,0:T(8,128)S(1)}, u32[]{:S(2)}, u32[]{:S(2)}) %all-to-all-start.11) | async-done | bytes 262176 | tf_op jit(solution)/shard_map/all_to_all | solution.py:330
  192.6 0.4 shard_map.145
  193.0 12.0 %all_to_all.74.recv_ref = f32[16,8,128]{2,1,0:T(8,128)S(1)} all-to-all(f32[16,8,128]{2,1,0:T(8,128)S(1)} %get-tuple-element.72), channel_id=1, replica_groups=mesh['group'=16,'sub'=32] {'group'}, dimensions={0} | all-to-all | bytes 131072 | tf_op jit(solution)/shard_map/all_to_all | solution.py:330
  205.1 13.2 %all_to_all.75.recv_ref = f32[32,8,128]{2,1,0:T(8,128)S(1)} all-to-all(f32[32,8,128]{2,1,0:T(8,128)S(1)} %shard_map.146), channel_id=1, replica_groups=mesh['group'=16,'sub'=32] {'sub'}, dimensions={0} | all-to-all | bytes 262144 | tf_op jit(solution)/shard_map/all_to_all | solution.py:330
  218.2 0.9 shard_map.147
  (10 shorter events, 0.1 us)
Async XLA Ops:
  2.5 10.3 %copy-start.1 = (s32[1,256]{1,0:T(1,128)S(1)}, s32[1,256]{1,0:T(1,128)}, u32[]{:S(2)}) copy-start(s32[1,256]{1,0:T(1,128)} %faces_ref.1) | copy-start | bytes 3076
  2.5 10.3 %copy-start.2 = (s32[1,256]{1,0:T(1,128)S(1)}, s32[1,256]{1,0:T(1,128)}, u32[]{:S(2)}) copy-start(s32[1,256]{1,0:T(1,128)} %lands_ref.1) | copy-start | bytes 3076
  2.5 10.3 %copy-start.3 = (f32[1,256]{1,0:T(1,128)S(1)}, f32[1,256]{1,0:T(1,128)}, u32[]{:S(2)}) copy-start(f32[1,256]{1,0:T(1,128)} %weight_ref.1) | copy-start | bytes 3076
  2.5 10.3 %copy-start.4 = (s32[1,32]{1,0:T(1,128)S(1)}, s32[1,32]{1,0:T(1,128)}, u32[]{:S(2)}) copy-start(s32[1,32]{1,0:T(1,128)} %counts_ref.1) | copy-start | bytes 388
  2.6 18.2 %all-to-all-start = ((f32[16,8,128]{2,1,0:T(8,128)}), f32[16,8,128]{2,1,0:T(8,128)S(1)}, u32[]{:S(2)}, u32[]{:S(2)}) async-start(f32[16,8,128]{2,1,0:T(8,128)} %shard_map.122), calls=%async_computation | async-start | bytes 131072 | tf_op jit(solution)/shard_map/all_to_all | solution.py:330
  21.5 21.1 %all-to-all-start.1 = ((f32[32,8,128]{2,1,0:T(8,128)}), f32[32,8,128]{2,1,0:T(8,128)S(1)}, u32[]{:S(2)}, u32[]{:S(2)}) async-start(f32[32,8,128]{2,1,0:T(8,128)} %shard_map.124), calls=%async_computation.1 | async-start | bytes 262144 | tf_op jit(solution)/shard_map/all_to_all | solution.py:330
  43.6 13.7 %all-to-all-start.2 = ((f32[16,8,128]{2,1,0:T(8,128)}), f32[16,8,128]{2,1,0:T(8,128)S(1)}, u32[]{:S(2)}, u32[]{:S(2)}) async-start(f32[16,8,128]{2,1,0:T(8,128)} %shard_map.126), calls=%async_computation.2 | async-start | bytes 131072 | tf_op jit(solution)/shard_map/all_to_all | solution.py:330
  48.4 2.0 copy-start
  58.7 15.9 %all-to-all-start.3 = ((f32[32,16,128]{2,1,0:T(8,128)}), f32[32,16,128]{2,1,0:T(8,128)S(1)}, u32[]{:S(2)}, u32[]{:S(2)}) async-start(f32[32,16,128]{2,1,0:T(8,128)} %get-tuple-element.48), calls=%async_computation.3 | async-start | bytes 524288 | tf_op jit(solution)/shard_map/all_to_all | solution.py:330
  105.8 12.7 %all-to-all-start.6 = ((f32[16,8,128]{2,1,0:T(8,128)}), f32[16,8,128]{2,1,0:T(8,128)S(1)}, u32[]{:S(2)}, u32[]{:S(2)}) async-start(f32[16,8,128]{2,1,0:T(8,128)} %shard_map.135), calls=%async_computation.6 | async-start | bytes 131072 | tf_op jit(solution)/shard_map/all_to_all | solution.py:330
  119.8 16.0 %all-to-all-start.7 = ((f32[32,16,128]{2,1,0:T(8,128)}), f32[32,16,128]{2,1,0:T(8,128)S(1)}, u32[]{:S(2)}, u32[]{:S(2)}) async-start(f32[32,16,128]{2,1,0:T(8,128)} %get-tuple-element.58), calls=%async_computation.7 | async-start | bytes 524288 | tf_op jit(solution)/shard_map/all_to_all | solution.py:330
  162.6 12.7 %all-to-all-start.10 = ((f32[16,8,128]{2,1,0:T(8,128)}), f32[16,8,128]{2,1,0:T(8,128)S(1)}, u32[]{:S(2)}, u32[]{:S(2)}) async-start(f32[16,8,128]{2,1,0:T(8,128)} %shard_map.141), calls=%async_computation.10 | async-start | bytes 131072 | tf_op jit(solution)/shard_map/all_to_all | solution.py:330
  176.7 16.0 %all-to-all-start.11 = ((f32[32,16,128]{2,1,0:T(8,128)}), f32[32,16,128]{2,1,0:T(8,128)S(1)}, u32[]{:S(2)}, u32[]{:S(2)}) async-start(f32[32,16,128]{2,1,0:T(8,128)} %get-tuple-element.66), calls=%async_computation.11 | async-start | bytes 524288 | tf_op jit(solution)/shard_map/all_to_all | solution.py:330

commit v3 on v2

v3 whole, which is shorter than its diff:
```python
import jax
import jax.numpy as jnp
from jax import lax
from jax.experimental import pallas as pl
from jax.experimental.pallas import tpu as pltpu
from jax.sharding import PartitionSpec as P

F32, BF16 = jnp.float32, jnp.bfloat16
ROWS, RHS, NC, SLOTS, BLK, NB = 512, 128, 64, 256, 64, 8
N_GROUP, N_SUB, LF = 16, 32, 128
VEC = (ROWS, RHS)
MSG_GROUP = (N_GROUP, 8, 128)
MSG_SUB = (N_SUB, 8, 128)
MSG_FACE = (N_SUB, 16, 128)
LAST_GROUP, LAST_SUB = (N_GROUP, 4, 128), (N_SUB, 4, 128)


def split(x):
    high = x.astype(BF16)
    rest = x - high.astype(F32)
    mid = rest.astype(BF16)
    return high, mid, (rest - mid.astype(F32)).astype(BF16)


def dot(a, b):
    return jnp.dot(a, b, preferred_element_type=F32)


def dot_nt(a, b):
    return lax.dot_general(a, b, (((1,), (1,)), ((), ())), preferred_element_type=F32)


def folded(products, n):
    total = None
    for at in reversed(range(products.shape[1] // n)):
        part = products[:, at * n : (at + 1) * n]
        total = part if total is None else total + part
    return total


def exact(one_hot, x):
    return folded(dot(one_hot, jnp.concatenate(split(x), axis=1)), x.shape[1])


def times(a, x):
    parts = split(x)
    total = None
    for order, part in reversed(list(enumerate(split(a)))):
        right = jnp.concatenate(parts[: len(parts) - order], axis=1)
        term = folded(dot(part, right), x.shape[1])
        total = term if total is None else total + term
    return total


def rowdot(a, b):
    return jnp.sum(a * b, axis=0, keepdims=True)


def tile_of(*rows):
    index = lax.broadcasted_iota(jnp.int32, (8, RHS), 0)
    tile = jnp.zeros((8, RHS), F32)
    for at, row in enumerate(rows):
        tile = jnp.where(index == at, row, tile)
    return tile


def pack(coarse, aux):
    whole = jnp.concatenate([coarse, aux, jnp.zeros((56, RHS), F32)], axis=0)
    return whole.T.reshape(MSG_GROUP)


def one_hot(same):
    return jnp.where(same, 1.0, 0.0).astype(BF16)


def pick_of(columns):
    lane = lax.broadcasted_iota(jnp.int32, (SLOTS, ROWS), 1).astype(F32)
    return jnp.concatenate([one_hot(columns[:, i : i + 1] == lane) for i in range(2)], axis=0)


def place_of(rows):
    row = lax.broadcasted_iota(jnp.int32, (ROWS, SLOTS), 0).astype(F32)
    return jnp.concatenate([one_hot(rows[i : i + 1] == row) for i in (1, 0)], axis=1)


def send_faces(field, columns_ref, msg_ref):
    columns = columns_ref[...]
    rows = exact(pick_of(columns), field)
    msg_ref[:, :8, :] = (rows[:SLOTS] * columns[:, 2:3]).reshape(N_SUB, 8, RHS)
    msg_ref[:, 8:, :] = rows[SLOTS:].reshape(N_SUB, 8, RHS)


def coupled_of(recv_ref, rows_ref, columns_ref):
    out = recv_ref[:, :8, :].reshape(SLOTS, RHS)
    back = recv_ref[:, 8:, :].reshape(SLOTS, RHS) * columns_ref[:, 2:3]
    return exact(place_of(rows_ref[...]), jnp.concatenate([out, back], axis=0))


def coarse_of(recv_ref, turned_ref):
    turned = recv_ref[...].reshape(128, 128).T
    return times(turned_ref[...], turned[:NC]), turned[NC : NC + 8]


def smooth_of(field_ref, diag_ref, gram_ref):
    parts = []
    for b in range(ROWS // LF):
        rows = slice(b * LF, (b + 1) * LF)
        field = field_ref[rows, :]
        parts.append(field / diag_ref[rows, :] + times(gram_ref[rows, :], field))
    return jnp.concatenate(parts, axis=0)


def k_first(right_ref, basis_ref, msg_ref):
    msg_ref[...] = pack(times(basis_ref[...], right_ref[...]), jnp.zeros((8, RHS), F32))


def k_slots(faces_ref, lands_ref, counts_ref, weight_ref, factor_ref, rows_ref, columns_ref, gram_ref):
    peer = lax.broadcasted_iota(jnp.int32, (N_SUB, SLOTS), 0)
    slot = lax.broadcasted_iota(jnp.int32, (N_SUB, SLOTS), 1)
    spread = one_hot(slot // 8 == peer)
    counts = jnp.broadcast_to(counts_ref[...].astype(F32), (8, N_SUB)).astype(BF16)
    counts = dot(counts, spread)[:1]
    place_in = (lax.broadcasted_iota(jnp.int32, (1, SLOTS), 1) % 8).astype(F32)
    weights = jnp.where(place_in < counts, weight_ref[...], 0.0)
    index = lax.broadcasted_iota(jnp.int32, (8, SLOTS), 0)
    rows = jnp.where(index == 2, weights, 0.0)
    rows = jnp.where(index == 0, faces_ref[...].astype(F32), rows)
    rows = jnp.where(index == 1, lands_ref[...].astype(F32), rows)
    rows_ref[...] = rows
    columns_ref[...] = jnp.concatenate([rows, jnp.zeros((120, SLOTS), F32)], axis=0).T
    for b in range(ROWS // LF):
        at = slice(b * LF, (b + 1) * LF)
        block = factor_ref[at, :]
        gram_ref[at, :] = times(block.T, block)


def k_setup(cols_ref, values_ref, mass_ref, basis_ref, blocks_ref, base_ref, turned_ref, dense_ref):
    lane = lax.broadcasted_iota(jnp.int32, (1, 128), 1)
    upper = jnp.where(lane >= BLK, 1, 0)
    for b in range(NB):
        rows = slice(b * BLK, (b + 1) * BLK)
        parts = []
        for m in range(NB // 2):
            block = values_ref[rows, m * 128 : (m + 1) * 128]
            first, second = cols_ref[b, 2 * m], cols_ref[b, 2 * m + 1]
            parts.append((block, jnp.where(lane < BLK, first, second) - upper))
            parts.append(
                (pltpu.roll(block, BLK, axis=1), jnp.where(lane < BLK, second, first) - upper)
            )
        for t in range(NB // 2):
            total = None
            for block, column in parts:
                term = block * jnp.where(column == 2 * t, 1.0, 0.0)
                total = term if total is None else total + term
            dense_ref[rows, t * 128 : (t + 1) * 128] = total
    dense = dense_ref[...]
    both = dense + dense.T
    blocks_ref[...] = both
    turned_ref[...] = basis_ref[...].T
    mass = jnp.broadcast_to(mass_ref[...], (128, ROWS)).T
    base_ref[...] = mass + jnp.sum(both, axis=1, keepdims=True)


def k_gather_first(recv_ref, columns_ref, msg_ref):
    total = jnp.sum(recv_ref[...], axis=0)
    lane = lax.broadcasted_iota(jnp.int32, MSG_SUB, 2)
    weight = jnp.broadcast_to(columns_ref[:, 2:3], (SLOTS, 128)).reshape(MSG_SUB)
    msg_ref[...] = jnp.where(lane == 127, weight, total[None])


def k_gather(recv_ref, msg_ref):
    msg_ref[...] = jnp.broadcast_to(jnp.sum(recv_ref[...], axis=0)[None], msg_ref.shape)


def k_solve(recv_ref, inverse_ref, msg_ref):
    lane = lax.broadcasted_iota(jnp.int32, (8, 128), 1)
    tiles = []
    aux = jnp.zeros((8, 128), F32)
    for j in range(N_SUB // 2):
        even, odd = recv_ref[2 * j], recv_ref[2 * j + 1]
        tiles.append(jnp.where(lane < NC, even, pltpu.roll(odd, NC, axis=1)))
        aux = aux + (even + odd)
    parts = [part.astype(F32) for part in split(jnp.concatenate(tiles, axis=1))]
    n = len(parts)
    stack = jnp.concatenate(parts + parts[: n % 2], axis=0).astype(BF16)
    solved = None
    for order, part in reversed(list(enumerate(split(inverse_ref[...])))):
        product = dot_nt(stack, part)
        for at in reversed(range(n - order)):
            term = product[at * 8 : (at + 1) * 8]
            solved = term if solved is None else solved + term
    tile = jnp.where(lane < NC, jnp.concatenate([solved, solved], axis=1), aux)
    msg_ref[...] = jnp.broadcast_to(tile[None], MSG_GROUP)


def k_diag(recv_ref, rows_ref, columns_ref, base_ref, diag_ref):
    lane = lax.broadcasted_iota(jnp.int32, (SLOTS, 128), 1)
    got = jnp.where(lane == 127, recv_ref[...].reshape(SLOTS, 128), 0.0)
    got = jnp.broadcast_to(jnp.sum(got, axis=1, keepdims=True), (SLOTS, 128))
    both = jnp.concatenate([got, jnp.broadcast_to(columns_ref[:, 2:3], (SLOTS, 128))], axis=0)
    diag, place = base_ref[...], place_of(rows_ref[...])
    for part in split(both):
        diag = diag + dot(place, part)
    diag_ref[...] = diag


def k_start(recv_ref, right_ref, diag_ref, gram_ref, turned_ref, columns_ref, z_ref, msg_ref):
    coarse, _ = coarse_of(recv_ref, turned_ref)
    z = smooth_of(right_ref, diag_ref, gram_ref) + coarse
    z_ref[...] = z
    send_faces(z, columns_ref, msg_ref)


def k_local0(z_ref, right_ref, diag_ref, blocks_ref, out_ref, dots_ref):
    z = z_ref[...]
    out_ref[...] = diag_ref[...] * z - times(blocks_ref[...], z)
    dots_ref[...] = tile_of(rowdot(right_ref[...], z))


def k_image(recv_ref, local_ref, z_ref, dots_ref, rows_ref, columns_ref, basis_ref, image_ref, msg_ref):
    image = local_ref[...] - coupled_of(recv_ref, rows_ref, columns_ref)
    image_ref[...] = image
    index = lax.broadcasted_iota(jnp.int32, (8, RHS), 0)
    aux = jnp.where(index == 2, rowdot(z_ref[...], image), dots_ref[...])
    msg_ref[...] = pack(times(basis_ref[...], image), aux)


def k_step0(recv_ref, q_ref, diag_ref, gram_ref, z_ref, turned_ref, columns_ref, u_ref, znew_ref, scal_ref, msg_ref):
    coarse, aux = coarse_of(recv_ref, turned_ref)
    gamma, pap = aux[0:1], aux[2:3]
    alpha = gamma / pap
    u = smooth_of(q_ref, diag_ref, gram_ref) + coarse
    u_ref[...] = u
    znew = z_ref[...] - alpha * u
    znew_ref[...] = znew
    scal_ref[...] = tile_of(alpha, gamma, pap)
    send_faces(znew, columns_ref, msg_ref)


def k_local1(z_ref, right_ref, q_ref, scal_ref, diag_ref, blocks_ref, out_ref, resid_ref, dots_ref):
    z, q = z_ref[...], q_ref[...]
    out_ref[...] = diag_ref[...] * z - times(blocks_ref[...], z)
    resid = right_ref[...] - scal_ref[0:1] * q
    resid_ref[...] = resid
    dots_ref[...] = tile_of(rowdot(resid, z), rowdot(z, q))


def k_step1(
    recv_ref, q_ref, diag_ref, gram_ref, u_ref, z_ref, scal_ref, turned_ref, columns_ref, znew_ref, scalnew_ref, msg_ref
):
    coarse, aux = coarse_of(recv_ref, turned_ref)
    gamma, cross, zaz = aux[0:1], aux[1:2], aux[2:3]
    beta = gamma / scal_ref[1:2]
    pap = zaz + beta * (2.0 * cross + beta * scal_ref[2:3])
    alpha = gamma / pap
    u = smooth_of(q_ref, diag_ref, gram_ref) + coarse + beta * u_ref[...]
    znew = z_ref[...] - alpha * u
    znew_ref[...] = znew
    scalnew_ref[...] = tile_of(alpha, gamma, pap, beta)
    send_faces(znew, columns_ref, msg_ref)


def k_local2(
    z_ref, z1_ref, z0_ref, v1_ref, q0_ref, resid_ref, scal0_ref, scal_ref, diag_ref, blocks_ref,
    out_ref, direction_ref, image_ref, x_ref, residnew_ref, dots_ref,
):
    z, z0 = z_ref[...], z0_ref[...]
    out_ref[...] = diag_ref[...] * z - times(blocks_ref[...], z)
    alpha, beta = scal_ref[0:1], scal_ref[3:4]
    direction = z1_ref[...] + beta * z0
    image = v1_ref[...] + beta * q0_ref[...]
    direction_ref[...], image_ref[...] = direction, image
    x_ref[...] = scal0_ref[0:1] * z0 + alpha * direction
    resid = resid_ref[...] - alpha * image
    residnew_ref[...] = resid
    dots_ref[...] = tile_of(rowdot(resid, z), rowdot(z, image))


def k_last_image(recv_ref, local_ref, z_ref, dots_ref, rows_ref, columns_ref, image_ref, msg_ref):
    image = local_ref[...] - coupled_of(recv_ref, rows_ref, columns_ref)
    image_ref[...] = image
    index = lax.broadcasted_iota(jnp.int32, (8, RHS), 0)
    aux = jnp.where(index == 2, rowdot(z_ref[...], image), dots_ref[...])
    msg_ref[...] = jnp.broadcast_to(aux[None, :4], LAST_GROUP)


def k_end(recv_ref, scal_ref, z_ref, v_ref, direction_ref, image_ref, x_ref, resid_ref, xout_ref, rout_ref):
    aux = jnp.sum(recv_ref[...], axis=0)
    gamma, cross, zaz = aux[0:1], aux[1:2], aux[2:3]
    beta = gamma / scal_ref[1:2]
    pap = zaz + beta * (2.0 * cross + beta * scal_ref[2:3])
    alpha = gamma / pap
    xout_ref[...] = x_ref[...] + alpha * (z_ref[...] + beta * direction_ref[...])
    rout_ref[...] = resid_ref[...] - alpha * (v_ref[...] + beta * image_ref[...])


class Far:
    def __init__(self, array):
        self.array = array


def call(kernel, outs, *args, smem=0, scratch=(), flops=1e6, far=()):
    near = pl.BlockSpec(memory_space=pltpu.VMEM)
    specs = [pl.BlockSpec(memory_space=pltpu.SMEM)] * smem
    specs += [pl.BlockSpec() if isinstance(a, Far) else near for a in args[smem:]]
    args = [pltpu.with_memory_space_constraint(a.array, pltpu.HBM) if isinstance(a, Far) else a for a in args]
    single = not isinstance(outs, list)
    sizes = [jax.ShapeDtypeStruct(s, d) for s, d in ([outs] if single else outs)]
    shapes = [pltpu.HBM(a.shape, a.dtype) if i in far else a for i, a in enumerate(sizes)]
    moved = sum(a.size * a.dtype.itemsize for a in [*args, *sizes])
    out = pl.pallas_call(
        kernel,
        out_shape=shapes,
        in_specs=specs,
        out_specs=[pl.BlockSpec() if i in far else near for i in range(len(shapes))],
        scratch_shapes=list(scratch),
        compiler_params=pltpu.CompilerParams(vmem_limit_bytes=24 << 20),
        cost_estimate=pl.CostEstimate(flops=int(flops), bytes_accessed=int(moved), transcendentals=0),
    )(*args)
    return out[0] if single else out


def swap(x, axis):
    return lax.all_to_all(x, axis, split_axis=0, concat_axis=0, tiled=True)


def local(
    right_side,
    mass,
    block_values,
    block_cols,
    face_rows,
    land_rows,
    face_counts,
    face_weight,
    local_factor,
    basis,
    coarse_inverse,
):
    vec = (VEC, F32)
    tile = ((8, RHS), F32)
    to_group, to_sub, to_face = (MSG_GROUP, F32), (MSG_SUB, F32), (MSG_FACE, F32)

    part = swap(call(k_first, to_group, Far(right_side), Far(basis)), "group")
    rows, columns, gram = call(
        k_slots,
        [((8, SLOTS), F32), ((SLOTS, 128), F32), vec],
        face_rows,
        land_rows,
        face_counts,
        face_weight,
        Far(local_factor),
    )
    whole = swap(call(k_gather_first, to_sub, part, columns), "sub")
    blocks, base, turned = call(
        k_setup,
        [((ROWS, ROWS), F32), vec, ((ROWS, NC), F32)],
        block_cols,
        Far(block_values),
        Far(mass),
        Far(basis),
        smem=1,
        scratch=[pltpu.VMEM((ROWS, ROWS), F32)],
        far=(0, 1),
    )
    blocks, right = Far(blocks), Far(right_side)
    first_inverse, turned = lax.optimization_barrier((coarse_inverse, turned))
    solved = swap(call(k_solve, to_group, whole, first_inverse), "group")
    diag = call(k_diag, vec, whole, rows, columns, Far(base))

    def coarse(msg):
        whole = swap(call(k_gather, to_sub, swap(msg, "group")), "sub")
        return swap(call(k_solve, to_group, whole, coarse_inverse), "group")

    def image(msg, near, z, dots):
        return call(k_image, [vec, to_group], swap(msg, "sub"), near, z, dots, rows, columns, basis)

    z0, msg = call(k_start, [vec, to_face], solved, right, diag, gram, turned, columns)
    near, dots = call(k_local0, [vec, tile], z0, right, diag, blocks)
    q0, msg = image(msg, near, z0, dots)

    solved = coarse(msg)
    u0, z1, scal0, msg = call(
        k_step0, [vec, vec, tile, to_face], solved, q0, diag, gram, z0, turned, columns
    )
    near, resid1, dots = call(
        k_local1, [vec, vec, tile], z1, right, q0, scal0, diag, blocks, far=(1,)
    )
    v1, msg = image(msg, near, z1, dots)

    solved = coarse(msg)
    z2, scal1, msg = call(
        k_step1, [vec, tile, to_face], solved, v1, diag, gram, u0, z1, scal0, turned, columns
    )
    near, direction, im, x, resid2, dots = call(
        k_local2, [vec] * 5 + [tile], z2, z1, z0, v1, q0, Far(resid1), scal0, scal1, diag, blocks
    )
    v2, msg = call(
        k_last_image, [vec, (LAST_GROUP, F32)], swap(msg, "sub"), near, z2, dots, rows, columns
    )
    whole = swap(call(k_gather, (LAST_SUB, F32), swap(msg, "group")), "sub")
    return tuple(call(k_end, [vec, vec], whole, scal1, z2, v2, direction, im, x, resid2))


def solution(mesh):
    both = P(("group", "sub"), None)
    return jax.shard_map(
        local,
        mesh=mesh,
        in_specs=(both,) * 10 + (P("sub", None),),
        out_specs=(both, both),
        check_vma=False,
    )
```

time: 220 us -> 213 us (0.968)
  blocking collectives: 79.9 us -> 97.8 us
  waiting for transfers between devices: 59.7 us -> 49 us
  starting transfers between devices: 47.8 us -> 38.2 us
  Pallas kernels: 30.8 us -> 26.4 us
    all_to_all x6 -> x8, blocking collectives: 79.9 us -> 97.8 us  [swap(): return lax.all_to_all(x, axis, split_axis=0, concat_axis=0, tiled=True)]
    all_to_all x8 -> x6, waiting for transfers between devices: 59.7 us -> 49 us  [swap(): return lax.all_to_all(x, axis, split_axis=0, concat_axis=0, tiled=True)]
    all_to_all x8 -> x6, starting transfers between devices: 47.8 us -> 38.2 us  [swap(): return lax.all_to_all(x, axis, split_axis=0, concat_axis=0, tiled=True)]
    pallas_call x26 -> x21, Pallas kernels: 30.8 us -> 26.4 us  [call(): pl.pallas_call(kernel, out_shape=shapes, in_specs=specs, out_specs=[pl.Bl...]
  transfers between devices with their start and end apart: 8 -> 6, of which waited for: 7 -> 6; matrix products, arithmetic and copies ran while one was open for 0% -> 0% of each run, Pallas kernels for 8% -> 6%
where the time goes in v3:
time: 213 us; the launch traced here: 212 us
  blocking collectives  97.8 us (46%)
  waiting for transfers between devices  49 us (23%)
  starting transfers between devices  38.2 us (18%)
  Pallas kernels  26.4 us (12%)
    all_to_all x8, blocking collectives, swap(): return lax.all_to_all(x, axis, split_axis=0, concat_axis=0, tiled=True)  97.8 us
    all_to_all x6, waiting for transfers between devices, swap(): return lax.all_to_all(x, axis, split_axis=0, concat_axis=0, tiled=True)  49 us
    all_to_all x6, starting transfers between devices, swap(): return lax.all_to_all(x, axis, split_axis=0, concat_axis=0, tiled=True)  38.2 us
    pallas_call x21, Pallas kernels, call(): pl.pallas_call(kernel, out_shape=shapes, in_specs=specs, out_specs=[pl.Bl...  26.4 us
  transfers between devices with their start and end apart: 6, of which 6 were waited for; matrix products, arithmetic and copies ran while one was open for 0% of the time, Pallas kernels for 6%

profile of v3, /device:TPU:1, one launch (start us, length us, event | category | flops | bytes accessed | tf_op | source)
XLA Modules:
  0.0 212.2 jit_solution(18353663447884199013)
XLA Ops:
  0.6 2.0 shard_map.122
  2.6 0.0 copy-start.3
  2.6 10.3 %all-to-all-start = ((f32[16,8,128]{2,1,0:T(8,128)}), f32[16,8,128]{2,1,0:T(8,128)S(1)}, u32[]{:S(2)}, u32[]{:S(2)}) async-start(f32[16,8,128]{2,1,0:T(8,128)} %shard_map.122), calls=%async_computation | async-start | bytes 131072 | tf_op jit(solution)/shard_map/all_to_all | solution.py:324
  12.9 0.0 copy-done.3
  12.9 0.0 copy-done.4
  12.9 0.0 copy-done.5
  12.9 0.0 copy-done.6
  13.0 1.4 shard_map.123
  14.3 6.4 %all-to-all-done.recv_ref = f32[16,8,128]{2,1,0:T(8,128)S(1)} async-done(((f32[16,8,128]{2,1,0:T(8,128)}), f32[16,8,128]{2,1,0:T(8,128)S(1)}, u32[]{:S(2)}, u32[]{:S(2)}) %all-to-all-start) | async-done | bytes 65568 | tf_op jit(solution)/shard_map/all_to_all | solution.py:324
  20.8 0.8 shard_map.124
  21.5 11.4 %all-to-all-start.1 = ((f32[32,8,128]{2,1,0:T(8,128)}), f32[32,8,128]{2,1,0:T(8,128)S(1)}, u32[]{:S(2)}, u32[]{:S(2)}) async-start(f32[32,8,128]{2,1,0:T(8,128)} %shard_map.124), calls=%async_computation.1 | async-start | bytes 262144 | tf_op jit(solution)/shard_map/all_to_all | solution.py:324
  33.0 0.0 copy-done.2
  33.0 0.0 copy-start
  33.0 3.3 %shard_map.125 = (f32[512,512]{1,0:T(8,128)}, f32[512,128]{1,0:T(8,128)}, f32[512,64]{1,0:T(8,128)S(1)}) custom-call(s32[8,8]{1,0:T(8,128)S(1)} %copy-done.2, f32[512,512]{1,0:T(8,128)} %values_ref.1, f32[1,512]{1,0:T(1,128)} %mass_ref.1, f32[64,512]{1,0:T(8,128)} %basis_ref.7), custom_call_target="tpu_custom_call" | custom-call | flops 1000000 | bytes 2623744 | tf_op jit(solution)/shard_map/pallas_call | solution.py:311
  36.2 6.5 %all-to-all-done.1.recv_ref = f32[32,8,128]{2,1,0:T(8,128)S(1)} async-done(((f32[32,8,128]{2,1,0:T(8,128)}), f32[32,8,128]{2,1,0:T(8,128)S(1)}, u32[]{:S(2)}, u32[]{:S(2)}) %all-to-all-start.1) | async-done | bytes 131104 | tf_op jit(solution)/shard_map/all_to_all | solution.py:324
  42.8 0.0 copy-done
  42.8 1.1 shard_map.126
  43.9 4.9 %all-to-all-start.2 = ((f32[16,8,128]{2,1,0:T(8,128)}), f32[16,8,128]{2,1,0:T(8,128)S(1)}, u32[]{:S(2)}, u32[]{:S(2)}) async-start(f32[16,8,128]{2,1,0:T(8,128)} %shard_map.126), calls=%async_computation.2 | async-start | bytes 131072 | tf_op jit(solution)/shard_map/all_to_all | solution.py:324
  48.8 1.6 shard_map.127.diag_ref
  50.4 6.2 %all-to-all-done.2.recv_ref = f32[16,8,128]{2,1,0:T(8,128)S(1)} async-done(((f32[16,8,128]{2,1,0:T(8,128)}), f32[16,8,128]{2,1,0:T(8,128)S(1)}, u32[]{:S(2)}, u32[]{:S(2)}) %all-to-all-start.2) | async-done | bytes 65568 | tf_op jit(solution)/shard_map/all_to_all | solution.py:324
  56.6 2.6 %shard_map.128 = (f32[512,128]{1,0:T(8,128)S(1)}, f32[32,16,128]{2,1,0:T(8,128)}) custom-call(f32[16,8,128]{2,1,0:T(8,128)S(1)} %all-to-all-done.2.recv_ref, f32[512,128]{1,0:T(8,128)} %right_ref.7, f32[512,128]{1,0:T(8,128)S(1)} %shard_map.127.diag_ref, f32[512,128]{1,0:T(8,128)S(1)} %get-tuple-element.41.gram_ref, ...), custom_call_target="tpu_custom_call" | custom-call | flops 1000000 | bytes 1638400 | tf_op jit(solution)/shard_map/pallas_call | solution.py:311
  59.2 3.9 %all-to-all-start.3 = ((f32[32,16,128]{2,1,0:T(8,128)}), f32[32,16,128]{2,1,0:T(8,128)S(1)}, u32[]{:S(2)}, u32[]{:S(2)}) async-start(f32[32,16,128]{2,1,0:T(8,128)} %get-tuple-element.43), calls=%async_computation.3 | async-start | bytes 524288 | tf_op jit(solution)/shard_map/all_to_all | solution.py:324
  63.1 0.0 copy-start.1
  63.1 2.1 shard_map.129
  65.2 10.0 %all-to-all-done.3.recv_ref = f32[32,16,128]{2,1,0:T(8,128)S(1)} async-done(((f32[32,16,128]{2,1,0:T(8,128)}), f32[32,16,128]{2,1,0:T(8,128)S(1)}, u32[]{:S(2)}, u32[]{:S(2)}) %all-to-all-start.3) | async-done | bytes 262176 | tf_op jit(solution)/shard_map/all_to_all | solution.py:324
  75.2 0.0 copy-done.1
  75.2 0.8 shard_map.130
  76.0 12.0 %all_to_all.70.recv_ref = f32[16,8,128]{2,1,0:T(8,128)S(1)} all-to-all(f32[16,8,128]{2,1,0:T(8,128)S(1)} %get-tuple-element.48), channel_id=1, replica_groups=mesh['group'=16,'sub'=32] {'group'}, dimensions={0} | all-to-all | bytes 131072 | tf_op jit(solution)/shard_map/all_to_all | solution.py:324
  88.0 13.2 %all_to_all.71.recv_ref = f32[32,8,128]{2,1,0:T(8,128)S(1)} all-to-all(f32[32,8,128]{2,1,0:T(8,128)S(1)} %shard_map.131), channel_id=1, replica_groups=mesh['group'=16,'sub'=32] {'sub'}, dimensions={0} | all-to-all | bytes 262144 | tf_op jit(solution)/shard_map/all_to_all | solution.py:324
  101.2 0.5 shard_map.132
  101.6 11.8 %all_to_all.72.recv_ref = f32[16,8,128]{2,1,0:T(8,128)S(1)} all-to-all(f32[16,8,128]{2,1,0:T(8,128)S(1)} %shard_map.132), channel_id=1, replica_groups=mesh['group'=16,'sub'=32] {'group'}, dimensions={0} | all-to-all | bytes 131072 | tf_op jit(solution)/shard_map/all_to_all | solution.py:324
  113.5 1.7 shard_map.133
  115.1 3.9 %all-to-all-start.7 = ((f32[32,16,128]{2,1,0:T(8,128)}), f32[32,16,128]{2,1,0:T(8,128)S(1)}, u32[]{:S(2)}, u32[]{:S(2)}) async-start(f32[32,16,128]{2,1,0:T(8,128)} %get-tuple-element.50), calls=%async_computation.7 | async-start | bytes 524288 | tf_op jit(solution)/shard_map/all_to_all | solution.py:324
  119.0 2.2 %shard_map.134 = (f32[512,128]{1,0:T(8,128)S(1)}, f32[512,128]{1,0:T(8,128)}, f32[8,128]{1,0:T(8,128)S(1)}) custom-call(f32[512,128]{1,0:T(8,128)S(1)} %get-tuple-element.51.z_ref.z1_ref, f32[512,128]{1,0:T(8,128)} %right_ref.7, f32[512,128]{1,0:T(8,128)S(1)} %get-tuple-element.49.q_ref.q0_ref, f32[8,128]{1,0:T(8,128)S(1)} %get-tuple-element.52.scal_ref.scal0_ref, ...), custom_call_target="tpu_custom_call" | custom-call | flops 1000000 | bytes 2629632 | tf_op jit(solution)/shard_map/pallas_call | solution.py:311
  121.2 9.9 %all-to-all-done.7.recv_ref = f32[32,16,128]{2,1,0:T(8,128)S(1)} async-done(((f32[32,16,128]{2,1,0:T(8,128)}), f32[32,16,128]{2,1,0:T(8,128)S(1)}, u32[]{:S(2)}, u32[]{:S(2)}) %all-to-all-start.7) | async-done | bytes 262176 | tf_op jit(solution)/shard_map/all_to_all | solution.py:324
  131.1 0.8 shard_map.135
  131.9 12.0 %all_to_all.73.recv_ref = f32[16,8,128]{2,1,0:T(8,128)S(1)} all-to-all(f32[16,8,128]{2,1,0:T(8,128)S(1)} %get-tuple-element.55), channel_id=1, replica_groups=mesh['group'=16,'sub'=32] {'group'}, dimensions={0} | all-to-all | bytes 131072 | tf_op jit(solution)/shard_map/all_to_all | solution.py:324
  143.9 13.1 %all_to_all.74.recv_ref = f32[32,8,128]{2,1,0:T(8,128)S(1)} all-to-all(f32[32,8,128]{2,1,0:T(8,128)S(1)} %shard_map.136), channel_id=1, replica_groups=mesh['group'=16,'sub'=32] {'sub'}, dimensions={0} | all-to-all | bytes 262144 | tf_op jit(solution)/shard_map/all_to_all | solution.py:324
  157.1 0.5 shard_map.137
  157.6 11.8 %all_to_all.75.recv_ref = f32[16,8,128]{2,1,0:T(8,128)S(1)} all-to-all(f32[16,8,128]{2,1,0:T(8,128)S(1)} %shard_map.137), channel_id=1, replica_groups=mesh['group'=16,'sub'=32] {'group'}, dimensions={0} | all-to-all | bytes 131072 | tf_op jit(solution)/shard_map/all_to_all | solution.py:324
  169.4 1.7 shard_map.138
  171.1 3.9 %all-to-all-start.11 = ((f32[32,16,128]{2,1,0:T(8,128)}), f32[32,16,128]{2,1,0:T(8,128)S(1)}, u32[]{:S(2)}, u32[]{:S(2)}) async-start(f32[32,16,128]{2,1,0:T(8,128)} %get-tuple-element.58), calls=%async_computation.11 | async-start | bytes 524288 | tf_op jit(solution)/shard_map/all_to_all | solution.py:324
  174.9 2.2 %shard_map.139 = (f32[512,128]{1,0:T(8,128)S(1)}, f32[512,128]{1,0:T(8,128)S(1)}, f32[512,128]{1,0:T(8,128)S(1)}, f32[512,128]{1,0:T(8,128)S(1)}, f32[512,128]{1,0:T(8,128)S(1)}, /*index=5*/f32[8,128]{1,0:T(8,128)S(1)}) custom-call(f32[512,128]{1,0:T(8,128)S(1)} %get-tuple-element.59.z_ref, f32[512,128]{1,0:T(8,128)S(1)} %get-tuple-element.51.z_ref.z1_ref, ...), custom_call_target="tpu_custom_call" | custom-call | flops 1000000 | bytes 4206592 | tf_op jit(solution)/shard_map/pallas_call | solution.py:311
  177.1 9.9 %all-to-all-done.11.recv_ref = f32[32,16,128]{2,1,0:T(8,128)S(1)} async-done(((f32[32,16,128]{2,1,0:T(8,128)}), f32[32,16,128]{2,1,0:T(8,128)S(1)}, u32[]{:S(2)}, u32[]{:S(2)}) %all-to-all-start.11) | async-done | bytes 262176 | tf_op jit(solution)/shard_map/all_to_all | solution.py:324
  187.0 0.5 shard_map.140
  187.5 11.7 %all_to_all.76.recv_ref = f32[16,4,128]{2,1,0:T(4,128)S(1)} all-to-all(f32[16,4,128]{2,1,0:T(4,128)S(1)} %get-tuple-element.64), channel_id=1, replica_groups=mesh['group'=16,'sub'=32] {'group'}, dimensions={0} | all-to-all | bytes 65536 | tf_op jit(solution)/shard_map/all_to_all | solution.py:324
  199.2 12.1 %all_to_all.77.recv_ref = f32[32,4,128]{2,1,0:T(4,128)S(1)} all-to-all(f32[32,4,128]{2,1,0:T(4,128)S(1)} %shard_map.141), channel_id=1, replica_groups=mesh['group'=16,'sub'=32] {'sub'}, dimensions={0} | all-to-all | bytes 131072 | tf_op jit(solution)/shard_map/all_to_all | solution.py:324
  211.3 0.9 shard_map.142
  (7 shorter events, 0.1 us)
Async XLA Ops:
  2.6 10.3 %copy-start.3 = (s32[1,256]{1,0:T(1,128)S(1)}, s32[1,256]{1,0:T(1,128)}, u32[]{:S(2)}) copy-start(s32[1,256]{1,0:T(1,128)} %faces_ref.1) | copy-start | bytes 3076
  2.6 10.3 %copy-start.4 = (s32[1,256]{1,0:T(1,128)S(1)}, s32[1,256]{1,0:T(1,128)}, u32[]{:S(2)}) copy-start(s32[1,256]{1,0:T(1,128)} %lands_ref.1) | copy-start | bytes 3076
  2.6 10.3 %copy-start.5 = (f32[1,256]{1,0:T(1,128)S(1)}, f32[1,256]{1,0:T(1,128)}, u32[]{:S(2)}) copy-start(f32[1,256]{1,0:T(1,128)} %weight_ref.1) | copy-start | bytes 3076
  2.6 10.3 %copy-start.6 = (s32[1,32]{1,0:T(1,128)S(1)}, s32[1,32]{1,0:T(1,128)}, u32[]{:S(2)}) copy-start(s32[1,32]{1,0:T(1,128)} %counts_ref.1) | copy-start | bytes 388
  2.6 18.2 %all-to-all-start = ((f32[16,8,128]{2,1,0:T(8,128)}), f32[16,8,128]{2,1,0:T(8,128)S(1)}, u32[]{:S(2)}, u32[]{:S(2)}) async-start(f32[16,8,128]{2,1,0:T(8,128)} %shard_map.122), calls=%async_computation | async-start | bytes 131072 | tf_op jit(solution)/shard_map/all_to_all | solution.py:324
  21.5 11.4 %copy-start.2 = (s32[8,8]{1,0:T(8,128)S(1)}, s32[8,8]{1,0:T(8,128)}, u32[]{:S(2)}) copy-start(s32[8,8]{1,0:T(8,128)} %cols_ref.1) | copy-start | bytes 772
  21.5 21.3 %all-to-all-start.1 = ((f32[32,8,128]{2,1,0:T(8,128)}), f32[32,8,128]{2,1,0:T(8,128)S(1)}, u32[]{:S(2)}, u32[]{:S(2)}) async-start(f32[32,8,128]{2,1,0:T(8,128)} %shard_map.124), calls=%async_computation.1 | async-start | bytes 262144 | tf_op jit(solution)/shard_map/all_to_all | solution.py:324
  33.0 9.8 %copy-start = (f32[64,2048]{1,0:T(8,128)S(1)}, f32[64,2048]{1,0:T(8,128)}, u32[]{:S(2)}) copy-start(f32[64,2048]{1,0:T(8,128)} %inverse_ref.4) | copy-start | bytes 1572868
  43.9 12.7 %all-to-all-start.2 = ((f32[16,8,128]{2,1,0:T(8,128)}), f32[16,8,128]{2,1,0:T(8,128)S(1)}, u32[]{:S(2)}, u32[]{:S(2)}) async-start(f32[16,8,128]{2,1,0:T(8,128)} %shard_map.126), calls=%async_computation.2 | async-start | bytes 131072 | tf_op jit(solution)/shard_map/all_to_all | solution.py:324
  59.2 16.0 %all-to-all-start.3 = ((f32[32,16,128]{2,1,0:T(8,128)}), f32[32,16,128]{2,1,0:T(8,128)S(1)}, u32[]{:S(2)}, u32[]{:S(2)}) async-start(f32[32,16,128]{2,1,0:T(8,128)} %get-tuple-element.43), calls=%async_computation.3 | async-start | bytes 524288 | tf_op jit(solution)/shard_map/all_to_all | solution.py:324
  63.1 12.1 %copy-start.1 = (f32[64,512]{1,0:T(8,128)S(1)}, f32[64,512]{1,0:T(8,128)}, u32[]{:S(2)}) copy-start(f32[64,512]{1,0:T(8,128)} %basis_ref.7) | copy-start | bytes 393220
  115.1 16.0 %all-to-all-start.7 = ((f32[32,16,128]{2,1,0:T(8,128)}), f32[32,16,128]{2,1,0:T(8,128)S(1)}, u32[]{:S(2)}, u32[]{:S(2)}) async-start(f32[32,16,128]{2,1,0:T(8,128)} %get-tuple-element.50), calls=%async_computation.7 | async-start | bytes 524288 | tf_op jit(solution)/shard_map/all_to_all | solution.py:324
  171.1 16.0 %all-to-all-start.11 = ((f32[32,16,128]{2,1,0:T(8,128)}), f32[32,16,128]{2,1,0:T(8,128)S(1)}, u32[]{:S(2)}, u32[]{:S(2)}) async-start(f32[32,16,128]{2,1,0:T(8,128)} %get-tuple-element.58), calls=%async_computation.11 | async-start | bytes 524288 | tf_op jit(solution)/shard_map/all_to_all | solution.py:324

commit v4 on v3

--- a/solution.py
+++ b/solution.py
@@ -8,6 +8,8 @@
 F32, BF16 = jnp.float32, jnp.bfloat16
 ROWS, RHS, NC, SLOTS, BLK, NB = 512, 128, 64, 256, 64, 8
 N_GROUP, N_SUB, LF = 16, 32, 128
+ORDER = [4 * z + x for x in range(4) for z in range(8)]
+PLACE = [ORDER.index(peer) for peer in range(N_SUB)]
 VEC = (ROWS, RHS)
 MSG_GROUP = (N_GROUP, 8, 128)
 MSG_SUB = (N_SUB, 8, 128)
@@ -86,28 +88,26 @@
 def send_faces(field, columns_ref, msg_ref):
     columns = columns_ref[...]
     rows = exact(pick_of(columns), field)
-    msg_ref[:, :8, :] = (rows[:SLOTS] * columns[:, 2:3]).reshape(N_SUB, 8, RHS)
-    msg_ref[:, 8:, :] = rows[SLOTS:].reshape(N_SUB, 8, RHS)
+    faces, lands = rows[:SLOTS] * columns[:, 2:3], rows[SLOTS:]
+    for at, peer in enumerate(ORDER):
+        msg_ref[at, :8, :] = faces[peer * 8 : (peer + 1) * 8]
+        msg_ref[at, 8:, :] = lands[peer * 8 : (peer + 1) * 8]
 
 
 def coupled_of(recv_ref, rows_ref, columns_ref):
-    out = recv_ref[:, :8, :].reshape(SLOTS, RHS)
-    back = recv_ref[:, 8:, :].reshape(SLOTS, RHS) * columns_ref[:, 2:3]
+    out = jnp.concatenate([recv_ref[at, :8, :] for at in PLACE], axis=0)
+    back = jnp.concatenate([recv_ref[at, 8:, :] for at in PLACE], axis=0) * columns_ref[:, 2:3]
     return exact(place_of(rows_ref[...]), jnp.concatenate([out, back], axis=0))
 
 
-def coarse_of(recv_ref, turned_ref):
-    turned = recv_ref[...].reshape(128, 128).T
-    return times(turned_ref[...], turned[:NC]), turned[NC : NC + 8]
-
-
-def smooth_of(field_ref, diag_ref, gram_ref):
-    parts = []
-    for b in range(ROWS // LF):
-        rows = slice(b * LF, (b + 1) * LF)
-        field = field_ref[rows, :]
-        parts.append(field / diag_ref[rows, :] + times(gram_ref[rows, :], field))
-    return jnp.concatenate(parts, axis=0)
+def coarse_of(recv_ref, basis_ref):
+    turned = recv_ref[...].reshape(RHS, 128)
+    return times(turned[:, :NC], basis_ref[...]).T, turned.T[NC : NC + 8]
+
+
+def smooth_of(field_ref, smoother_ref):
+    blocks = [slice(b * LF, (b + 1) * LF) for b in range(ROWS // LF)]
+    return jnp.concatenate([times(smoother_ref[b, :], field_ref[b, :]) for b in blocks], axis=0)
 
 
 def k_first(right_ref, basis_ref, msg_ref):
@@ -134,7 +134,7 @@
         gram_ref[at, :] = times(block.T, block)
 
 
-def k_setup(cols_ref, values_ref, mass_ref, basis_ref, blocks_ref, base_ref, turned_ref, dense_ref):
+def k_setup(cols_ref, values_ref, mass_ref, blocks_ref, base_ref, dense_ref):
     lane = lax.broadcasted_iota(jnp.int32, (1, 128), 1)
     upper = jnp.where(lane >= BLK, 1, 0)
     for b in range(NB):
@@ -156,16 +156,15 @@
     dense = dense_ref[...]
     both = dense + dense.T
     blocks_ref[...] = both
-    turned_ref[...] = basis_ref[...].T
     mass = jnp.broadcast_to(mass_ref[...], (128, ROWS)).T
     base_ref[...] = mass + jnp.sum(both, axis=1, keepdims=True)
 
 
 def k_gather_first(recv_ref, columns_ref, msg_ref):
     total = jnp.sum(recv_ref[...], axis=0)
-    lane = lax.broadcasted_iota(jnp.int32, MSG_SUB, 2)
-    weight = jnp.broadcast_to(columns_ref[:, 2:3], (SLOTS, 128)).reshape(MSG_SUB)
-    msg_ref[...] = jnp.where(lane == 127, weight, total[None])
+    lane = lax.broadcasted_iota(jnp.int32, (8, 128), 1)
+    for at, peer in enumerate(ORDER):
+        msg_ref[at] = jnp.where(lane == 127, columns_ref[peer * 8 : (peer + 1) * 8, 2:3], total)
 
 
 def k_gather(recv_ref, msg_ref):
@@ -177,7 +176,7 @@
     tiles = []
     aux = jnp.zeros((8, 128), F32)
     for j in range(N_SUB // 2):
-        even, odd = recv_ref[2 * j], recv_ref[2 * j + 1]
+        even, odd = recv_ref[PLACE[2 * j]], recv_ref[PLACE[2 * j + 1]]
         tiles.append(jnp.where(lane < NC, even, pltpu.roll(odd, NC, axis=1)))
         aux = aux + (even + odd)
     parts = [part.astype(F32) for part in split(jnp.concatenate(tiles, axis=1))]
@@ -193,43 +192,49 @@
     msg_ref[...] = jnp.broadcast_to(tile[None], MSG_GROUP)
 
 
-def k_diag(recv_ref, rows_ref, columns_ref, base_ref, diag_ref):
+def k_finish(recv_ref, rows_ref, columns_ref, base_ref, blocks_ref, gram_ref, matrix_ref, smoother_ref):
     lane = lax.broadcasted_iota(jnp.int32, (SLOTS, 128), 1)
-    got = jnp.where(lane == 127, recv_ref[...].reshape(SLOTS, 128), 0.0)
+    got = jnp.concatenate([recv_ref[at] for at in PLACE], axis=0)
+    got = jnp.where(lane == 127, got, 0.0)
     got = jnp.broadcast_to(jnp.sum(got, axis=1, keepdims=True), (SLOTS, 128))
     both = jnp.concatenate([got, jnp.broadcast_to(columns_ref[:, 2:3], (SLOTS, 128))], axis=0)
     diag, place = base_ref[...], place_of(rows_ref[...])
     for part in split(both):
         diag = diag + dot(place, part)
-    diag_ref[...] = diag
-
-
-def k_start(recv_ref, right_ref, diag_ref, gram_ref, turned_ref, columns_ref, z_ref, msg_ref):
-    coarse, _ = coarse_of(recv_ref, turned_ref)
-    z = smooth_of(right_ref, diag_ref, gram_ref) + coarse
+    index = lax.broadcasted_iota(jnp.int32, (LF, LF), 0) == lax.broadcasted_iota(jnp.int32, (LF, LF), 1)
+    matrix_ref[...] = -blocks_ref[...]
+    for b in range(ROWS // LF):
+        at = slice(b * LF, (b + 1) * LF)
+        matrix_ref[at, at] = jnp.where(index, diag[at], 0.0) - blocks_ref[at, at]
+        smoother_ref[at, :] = gram_ref[at, :] + jnp.where(index, 1.0 / diag[at], 0.0)
+
+
+def k_start(recv_ref, right_ref, smoother_ref, basis_ref, columns_ref, z_ref, msg_ref):
+    coarse, _ = coarse_of(recv_ref, basis_ref)
+    z = smooth_of(right_ref, smoother_ref) + coarse
     z_ref[...] = z
     send_faces(z, columns_ref, msg_ref)
 
 
-def k_local0(z_ref, right_ref, diag_ref, blocks_ref, out_ref, dots_ref):
+def image_of(recv_ref, z_ref, matrix_ref, rows_ref, columns_ref):
+    return times(matrix_ref[...], z_ref[...]) - coupled_of(recv_ref, rows_ref, columns_ref)
+
+
+def k_image0(
+    recv_ref, z_ref, right_ref, matrix_ref, rows_ref, columns_ref, basis_ref, image_ref, msg_ref
+):
+    image = image_of(recv_ref, z_ref, matrix_ref, rows_ref, columns_ref)
+    image_ref[...] = image
     z = z_ref[...]
-    out_ref[...] = diag_ref[...] * z - times(blocks_ref[...], z)
-    dots_ref[...] = tile_of(rowdot(right_ref[...], z))
-
-
-def k_image(recv_ref, local_ref, z_ref, dots_ref, rows_ref, columns_ref, basis_ref, image_ref, msg_ref):
-    image = local_ref[...] - coupled_of(recv_ref, rows_ref, columns_ref)
-    image_ref[...] = image
-    index = lax.broadcasted_iota(jnp.int32, (8, RHS), 0)
-    aux = jnp.where(index == 2, rowdot(z_ref[...], image), dots_ref[...])
+    aux = tile_of(rowdot(right_ref[...], z), jnp.zeros((1, RHS), F32), rowdot(z, image))
     msg_ref[...] = pack(times(basis_ref[...], image), aux)
 
 
-def k_step0(recv_ref, q_ref, diag_ref, gram_ref, z_ref, turned_ref, columns_ref, u_ref, znew_ref, scal_ref, msg_ref):
-    coarse, aux = coarse_of(recv_ref, turned_ref)
+def k_step0(recv_ref, q_ref, smoother_ref, z_ref, basis_ref, columns_ref, u_ref, znew_ref, scal_ref, msg_ref):
+    coarse, aux = coarse_of(recv_ref, basis_ref)
     gamma, pap = aux[0:1], aux[2:3]
     alpha = gamma / pap
-    u = smooth_of(q_ref, diag_ref, gram_ref) + coarse
+    u = smooth_of(q_ref, smoother_ref) + coarse
     u_ref[...] = u
     znew = z_ref[...] - alpha * u
     znew_ref[...] = znew
@@ -237,61 +242,63 @@
     send_faces(znew, columns_ref, msg_ref)
 
 
-def k_local1(z_ref, right_ref, q_ref, scal_ref, diag_ref, blocks_ref, out_ref, resid_ref, dots_ref):
+def k_image1(
+    recv_ref, z_ref, right_ref, q_ref, scal_ref, matrix_ref, rows_ref, columns_ref, basis_ref, image_ref, msg_ref
+):
+    image = image_of(recv_ref, z_ref, matrix_ref, rows_ref, columns_ref)
+    image_ref[...] = image
     z, q = z_ref[...], q_ref[...]
-    out_ref[...] = diag_ref[...] * z - times(blocks_ref[...], z)
     resid = right_ref[...] - scal_ref[0:1] * q
-    resid_ref[...] = resid
-    dots_ref[...] = tile_of(rowdot(resid, z), rowdot(z, q))
+    aux = tile_of(rowdot(resid, z), rowdot(z, q), rowdot(z, image))
+    msg_ref[...] = pack(times(basis_ref[...], image), aux)
 
 
 def k_step1(
-    recv_ref, q_ref, diag_ref, gram_ref, u_ref, z_ref, scal_ref, turned_ref, columns_ref, znew_ref, scalnew_ref, msg_ref
-):
-    coarse, aux = coarse_of(recv_ref, turned_ref)
+    recv_ref, v_ref, smoother_ref, u_ref, z_ref, scal_ref, basis_ref, columns_ref, znew_ref, scalnew_ref, msg_ref
+):
+    coarse, aux = coarse_of(recv_ref, basis_ref)
     gamma, cross, zaz = aux[0:1], aux[1:2], aux[2:3]
     beta = gamma / scal_ref[1:2]
     pap = zaz + beta * (2.0 * cross + beta * scal_ref[2:3])
     alpha = gamma / pap
-    u = smooth_of(q_ref, diag_ref, gram_ref) + coarse + beta * u_ref[...]
+    u = smooth_of(v_ref, smoother_ref) + coarse + beta * u_ref[...]
     znew = z_ref[...] - alpha * u
     znew_ref[...] = znew
     scalnew_ref[...] = tile_of(alpha, gamma, pap, beta)
     send_faces(znew, columns_ref, msg_ref)
 
 
-def k_local2(
-    z_ref, z1_ref, z0_ref, v1_ref, q0_ref, resid_ref, scal0_ref, scal_ref, diag_ref, blocks_ref,
-    out_ref, direction_ref, image_ref, x_ref, residnew_ref, dots_ref,
-):
-    z, z0 = z_ref[...], z0_ref[...]
-    out_ref[...] = diag_ref[...] * z - times(blocks_ref[...], z)
-    alpha, beta = scal_ref[0:1], scal_ref[3:4]
-    direction = z1_ref[...] + beta * z0
-    image = v1_ref[...] + beta * q0_ref[...]
-    direction_ref[...], image_ref[...] = direction, image
-    x_ref[...] = scal0_ref[0:1] * z0 + alpha * direction
-    resid = resid_ref[...] - alpha * image
-    residnew_ref[...] = resid
-    dots_ref[...] = tile_of(rowdot(resid, z), rowdot(z, image))
-
-
-def k_last_image(recv_ref, local_ref, z_ref, dots_ref, rows_ref, columns_ref, image_ref, msg_ref):
-    image = local_ref[...] - coupled_of(recv_ref, rows_ref, columns_ref)
+def second_of(right_ref, q_ref, v_ref, scal0_ref, scal_ref):
+    image = v_ref[...] + scal_ref[3:4] * q_ref[...]
+    return image, right_ref[...] - scal0_ref[0:1] * q_ref[...] - scal_ref[0:1] * image
+
+
+def k_image2(
+    recv_ref, z_ref, right_ref, q_ref, v_ref, scal0_ref, scal_ref, matrix_ref, rows_ref, columns_ref,
+    image_ref, msg_ref,
+):
+    image = image_of(recv_ref, z_ref, matrix_ref, rows_ref, columns_ref)
     image_ref[...] = image
-    index = lax.broadcasted_iota(jnp.int32, (8, RHS), 0)
-    aux = jnp.where(index == 2, rowdot(z_ref[...], image), dots_ref[...])
+    z = z_ref[...]
+    before, resid = second_of(right_ref, q_ref, v_ref, scal0_ref, scal_ref)
+    aux = tile_of(rowdot(resid, z), rowdot(z, before), rowdot(z, image))
     msg_ref[...] = jnp.broadcast_to(aux[None, :4], LAST_GROUP)
 
 
-def k_end(recv_ref, scal_ref, z_ref, v_ref, direction_ref, image_ref, x_ref, resid_ref, xout_ref, rout_ref):
+def k_end(
+    recv_ref, scal0_ref, scal_ref, z0_ref, z1_ref, z2_ref, right_ref, q_ref, v_ref, last_ref, xout_ref, rout_ref
+):
     aux = jnp.sum(recv_ref[...], axis=0)
     gamma, cross, zaz = aux[0:1], aux[1:2], aux[2:3]
     beta = gamma / scal_ref[1:2]
     pap = zaz + beta * (2.0 * cross + beta * scal_ref[2:3])
     alpha = gamma / pap
-    xout_ref[...] = x_ref[...] + alpha * (z_ref[...] + beta * direction_ref[...])
-    rout_ref[...] = resid_ref[...] - alpha * (v_ref[...] + beta * image_ref[...])
+    z0 = z0_ref[...]
+    direction = z1_ref[...] + scal_ref[3:4] * z0
+    x = scal0_ref[0:1] * z0 + scal_ref[0:1] * direction
+    xout_ref[...] = x + alpha * (z2_ref[...] + beta * direction)
+    image, resid = second_of(right_ref, q_ref, v_ref, scal0_ref, scal_ref)
+    rout_ref[...] = resid - alpha * (last_ref[...] + beta * image)
 
 
 class Far:
@@ -321,7 +328,8 @@
 
 
 def swap(x, axis):
-    return lax.all_to_all(x, axis, split_axis=0, concat_axis=0, tiled=True)
+    order = [ORDER] if axis == "sub" else None
+    return lax.all_to_all(x, axis, split_axis=0, concat_axis=0, tiled=True, axis_index_groups=order)
 
 
 def local(
@@ -350,56 +358,77 @@
         face_counts,
         face_weight,
         Far(local_factor),
+        far=(2,),
     )
     whole = swap(call(k_gather_first, to_sub, part, columns), "sub")
-    blocks, base, turned = call(
+    blocks, base = call(
         k_setup,
-        [((ROWS, ROWS), F32), vec, ((ROWS, NC), F32)],
+        [((ROWS, ROWS), F32), vec],
         block_cols,
         Far(block_values),
         Far(mass),
-        Far(basis),
         smem=1,
         scratch=[pltpu.VMEM((ROWS, ROWS), F32)],
         far=(0, 1),
     )
-    blocks, right = Far(blocks), Far(right_side)
-    first_inverse, turned = lax.optimization_barrier((coarse_inverse, turned))
+    first_inverse, base = lax.optimization_barrier((coarse_inverse, base))
     solved = swap(call(k_solve, to_group, whole, first_inverse), "group")
-    diag = call(k_diag, vec, whole, rows, columns, Far(base))
+    matrix, smoother = call(
+        k_finish,
+        [((ROWS, ROWS), F32), vec],
+        whole,
+        rows,
+        columns,
+        Far(base),
+        Far(blocks),
+        Far(gram),
+    )
 
     def coarse(msg):
         whole = swap(call(k_gather, to_sub, swap(msg, "group")), "sub")
         return swap(call(k_solve, to_group, whole, coarse_inverse), "group")
 
-    def image(msg, near, z, dots):
-        return call(k_image, [vec, to_group], swap(msg, "sub"), near, z, dots, rows, columns, basis)
-
-    z0, msg = call(k_start, [vec, to_face], solved, right, diag, gram, turned, columns)
-    near, dots = call(k_local0, [vec, tile], z0, right, diag, blocks)
-    q0, msg = image(msg, near, z0, dots)
-
-    solved = coarse(msg)
+    z0, msg = call(k_start, [vec, to_face], solved, right_side, smoother, basis, columns)
+    q0, msg = call(
+        k_image0, [vec, to_group], swap(msg, "sub"), z0, right_side, matrix, rows, columns, basis
+    )
     u0, z1, scal0, msg = call(
-        k_step0, [vec, vec, tile, to_face], solved, q0, diag, gram, z0, turned, columns
-    )
-    near, resid1, dots = call(
-        k_local1, [vec, vec, tile], z1, right, q0, scal0, diag, blocks, far=(1,)
-    )
-    v1, msg = image(msg, near, z1, dots)
-
-    solved = coarse(msg)
+        k_step0, [vec, vec, tile, to_face], coarse(msg), q0, smoother, z0, basis, columns
+    )
+    v1, msg = call(
+        k_image1,
+        [vec, to_group],
+        swap(msg, "sub"),
+        z1,
+        right_side,
+        q0,
+        scal0,
+        matrix,
+        rows,
+        columns,
+        basis,
+    )
     z2, scal1, msg = call(
-        k_step1, [vec, tile, to_face], solved, v1, diag, gram, u0, z1, scal0, turned, columns
-    )
-    near, direction, im, x, resid2, dots = call(
-        k_local2, [vec] * 5 + [tile], z2, z1, z0, v1, q0, Far(resid1), scal0, scal1, diag, blocks
+        k_step1, [vec, tile, to_face], coarse(msg), v1, smoother, u0, z1, scal0, basis, columns
     )
     v2, msg = call(
-        k_last_image, [vec, (LAST_GROUP, F32)], swap(msg, "sub"), near, z2, dots, rows, columns
+        k_image2,
+        [vec, (LAST_GROUP, F32)],
+        swap(msg, "sub"),
+        z2,
+        right_side,
+        q0,
+        v1,
+        scal0,
+        scal1,
+        matrix,
+        rows,
+        columns,
     )
     whole = swap(call(k_gather, (LAST_SUB, F32), swap(msg, "group")), "sub")
-    return tuple(call(k_end, [vec, vec], whole, scal1, z2, v2, direction, im, x, resid2))
+    return tuple(
+        call(k_end, [vec, vec], whole, scal0, scal1, z0, z1, z2, right_side, q0, v1, v2)
+    )
 
 
 def solution(mesh):

time: 213 us -> 210 us (0.986)
  blocking collectives: 97.8 us -> 144 us
  waiting for transfers between devices: 49 us -> 17.3 us
  starting transfers between devices: 38.2 us -> 27.1 us
  Pallas kernels: 26.4 us -> 19.5 us
    all_to_all x8 -> x11, blocking collectives: 97.8 us -> 144 us  [swap(): lax.all_to_all(x, axis, split_axis=0, concat_axis=0, tiled=True, axis_ind...]
    all_to_all x6 -> x3, waiting for transfers between devices: 49 us -> 17.3 us  [swap(): lax.all_to_all(x, axis, split_axis=0, concat_axis=0, tiled=True, axis_ind...]
    all_to_all x6 -> x3, starting transfers between devices: 38.2 us -> 27.1 us  [swap(): lax.all_to_all(x, axis, split_axis=0, concat_axis=0, tiled=True, axis_ind...]
    pallas_call x21 -> x18, Pallas kernels: 26.4 us -> 19.5 us  [call(): pl.pallas_call(kernel, out_shape=shapes, in_specs=specs, out_specs=[pl.Bl...]
  transfers between devices with their start and end apart: 6 -> 3, of which waited for: 6 -> 3; matrix products, arithmetic and copies ran while one was open for 0% -> 0% of each run, Pallas kernels for 6% -> 4%
where the time goes in v4:
time: 210 us; the launch traced here: 209 us
  blocking collectives  144 us (69%)
  starting transfers between devices  27.1 us (13%)
  Pallas kernels  19.5 us (9%)
  waiting for transfers between devices  17.3 us (8%)
    all_to_all x11, blocking collectives, swap(): lax.all_to_all(x, axis, split_axis=0, concat_axis=0, tiled=True, axis_ind...  144 us
    all_to_all x3, starting transfers between devices, swap(): lax.all_to_all(x, axis, split_axis=0, concat_axis=0, tiled=True, axis_ind...  27.1 us
    pallas_call x18, Pallas kernels, call(): pl.pallas_call(kernel, out_shape=shapes, in_specs=specs, out_specs=[pl.Bl...  19.5 us
    all_to_all x3, waiting for transfers between devices, swap(): lax.all_to_all(x, axis, split_axis=0, concat_axis=0, tiled=True, axis_ind...  17.3 us
  transfers between devices with their start and end apart: 3, of which 3 were waited for; matrix products, arithmetic and copies ran while one was open for 0% of the time, Pallas kernels for 4%

profile of v4, /device:TPU:1, one launch (start us, length us, event | category | flops | bytes accessed | tf_op | source)
XLA Modules:
  0.0 208.7 jit_solution(16977816430658616691)
XLA Ops:
  0.6 2.0 shard_map.122
  2.6 0.0 copy-start.4
  2.6 0.0 copy-start.5
  2.6 0.0 copy-start.6
  2.6 0.0 copy-start.7
  2.6 10.3 %all-to-all-start = ((f32[16,8,128]{2,1,0:T(8,128)}), f32[16,8,128]{2,1,0:T(8,128)S(1)}, u32[]{:S(2)}, u32[]{:S(2)}) async-start(f32[16,8,128]{2,1,0:T(8,128)} %shard_map.122), calls=%async_computation | async-start | bytes 131072 | tf_op jit(solution)/shard_map/all_to_all | solution.py:332
  12.9 0.0 copy-done.4
  12.9 0.0 copy-done.5
  12.9 0.0 copy-done.6
  12.9 0.0 copy-done.7
  13.0 2.1 shard_map.123
  15.0 5.7 %all-to-all-done.recv_ref = f32[16,8,128]{2,1,0:T(8,128)S(1)} async-done(((f32[16,8,128]{2,1,0:T(8,128)}), f32[16,8,128]{2,1,0:T(8,128)S(1)}, u32[]{:S(2)}, u32[]{:S(2)}) %all-to-all-start) | async-done | bytes 65568 | tf_op jit(solution)/shard_map/all_to_all | solution.py:332
  20.8 0.8 shard_map.124
  21.5 0.0 copy-start.3
  21.5 11.4 %all-to-all-start.1 = ((f32[32,8,128]{2,1,0:T(8,128)}), f32[32,8,128]{2,1,0:T(8,128)S(1)}, u32[]{:S(2)}, u32[]{:S(2)}) async-start(f32[32,8,128]{2,1,0:T(8,128)} %shard_map.124), calls=%async_computation.1 | async-start | bytes 262144 | tf_op jit(solution)/shard_map/all_to_all | solution.py:332
  33.0 0.0 copy-done.3
  33.0 0.0 copy-start.1
  33.0 3.2 %shard_map.125 = (f32[512,512]{1,0:T(8,128)}, f32[512,128]{1,0:T(8,128)}) custom-call(s32[8,8]{1,0:T(8,128)S(1)} %copy-done.3, f32[512,512]{1,0:T(8,128)} %values_ref.1, f32[1,512]{1,0:T(1,128)} %mass_ref.1), custom_call_target="tpu_custom_call" | custom-call | flops 1000000 | bytes 2361600 | tf_op jit(solution)/shard_map/pallas_call | solution.py:318
  36.2 6.0 %all-to-all-done.1.recv_ref = f32[32,8,128]{2,1,0:T(8,128)S(1)} async-done(((f32[32,8,128]{2,1,0:T(8,128)}), f32[32,8,128]{2,1,0:T(8,128)S(1)}, u32[]{:S(2)}, u32[]{:S(2)}) %all-to-all-start.1) | async-done | bytes 131104 | tf_op jit(solution)/shard_map/all_to_all | solution.py:332
  42.1 0.0 copy-done.1
  42.1 1.1 shard_map.126
  43.2 5.4 %all-to-all-start.2 = ((f32[16,8,128]{2,1,0:T(8,128)}), f32[16,8,128]{2,1,0:T(8,128)S(1)}, u32[]{:S(2)}, u32[]{:S(2)}) async-start(f32[16,8,128]{2,1,0:T(8,128)} %shard_map.126), calls=%async_computation.2 | async-start | bytes 131072 | tf_op jit(solution)/shard_map/all_to_all | solution.py:332
  48.6 0.0 copy-start
  48.6 0.0 copy-start.2
  48.6 2.2 %shard_map.127 = (f32[512,512]{1,0:T(8,128)S(1)}, f32[512,128]{1,0:T(8,128)S(1)}) custom-call(f32[32,8,128]{2,1,0:T(8,128)S(1)} %all-to-all-done.1.recv_ref, f32[8,256]{1,0:T(8,128)S(1)} %get-tuple-element.29.rows_ref, f32[256,128]{1,0:T(8,128)S(1)} %get-tuple-element.26.columns_ref, f32[512,128]{1,0:T(8,128)} %get-tuple-element.30.base_ref, ...), custom_call_target="tpu_custom_call" | custom-call | flops 1000000 | bytes 3153920 | tf_op jit(solution)/shard_map/pallas_call | solution.py:318
  50.8 5.6 %all-to-all-done.2.recv_ref = f32[16,8,128]{2,1,0:T(8,128)S(1)} async-done(((f32[16,8,128]{2,1,0:T(8,128)}), f32[16,8,128]{2,1,0:T(8,128)S(1)}, u32[]{:S(2)}, u32[]{:S(2)}) %all-to-all-start.2) | async-done | bytes 65568 | tf_op jit(solution)/shard_map/all_to_all | solution.py:332
  56.4 0.0 copy-done
  56.4 0.0 copy-done.2
  56.4 0.9 shard_map.128
  57.3 13.4 %all_to_all.70.recv_ref = f32[32,16,128]{2,1,0:T(8,128)S(1)} all-to-all(f32[32,16,128]{2,1,0:T(8,128)S(1)} %get-tuple-element.34), channel_id=1, replica_groups={{0,4,8,12,16,20,24,28,1,5,9,13,17,21,25,29,2,6,10,14,18,22,26,30,3,7,11..., dimensions={0} | all-to-all | bytes 524288 | tf_op jit(solution)/shard_map/all_to_all | solution.py:332
  70.7 1.3 shard_map.129
  72.0 13.2 %all_to_all.71.recv_ref = f32[16,8,128]{2,1,0:T(8,128)S(1)} all-to-all(f32[16,8,128]{2,1,0:T(8,128)S(1)} %get-tuple-element.37), channel_id=1, replica_groups=mesh['group'=16,'sub'=32] {'group'}, dimensions={0} | all-to-all | bytes 131072 | tf_op jit(solution)/shard_map/all_to_all | solution.py:332
  85.3 13.4 %all_to_all.72.recv_ref = f32[32,8,128]{2,1,0:T(8,128)S(1)} all-to-all(f32[32,8,128]{2,1,0:T(8,128)S(1)} %shard_map.130), channel_id=1, replica_groups={{0,4,8,12,16,20,24,28,1,5,9,13,17,21,25,29,2,6,10,14,18,22,26,30,3,7,11..., dimensions={0} | all-to-all | bytes 262144 | tf_op jit(solution)/shard_map/all_to_all | solution.py:332
  98.7 0.5 shard_map.131
  99.1 12.3 %all_to_all.73.recv_ref = f32[16,8,128]{2,1,0:T(8,128)S(1)} all-to-all(f32[16,8,128]{2,1,0:T(8,128)S(1)} %shard_map.131), channel_id=1, replica_groups=mesh['group'=16,'sub'=32] {'group'}, dimensions={0} | all-to-all | bytes 131072 | tf_op jit(solution)/shard_map/all_to_all | solution.py:332
  111.5 0.9 shard_map.132
  112.4 13.4 %all_to_all.74.recv_ref = f32[32,16,128]{2,1,0:T(8,128)S(1)} all-to-all(f32[32,16,128]{2,1,0:T(8,128)S(1)} %get-tuple-element.39), channel_id=1, replica_groups={{0,4,8,12,16,20,24,28,1,5,9,13,17,21,25,29,2,6,10,14,18,22,26,30,3,7,11..., dimensions={0} | all-to-all | bytes 524288 | tf_op jit(solution)/shard_map/all_to_all | solution.py:332
  125.7 1.3 shard_map.133
  127.1 13.2 %all_to_all.75.recv_ref = f32[16,8,128]{2,1,0:T(8,128)S(1)} all-to-all(f32[16,8,128]{2,1,0:T(8,128)S(1)} %get-tuple-element.42), channel_id=1, replica_groups=mesh['group'=16,'sub'=32] {'group'}, dimensions={0} | all-to-all | bytes 131072 | tf_op jit(solution)/shard_map/all_to_all | solution.py:332
  140.3 13.4 %all_to_all.76.recv_ref = f32[32,8,128]{2,1,0:T(8,128)S(1)} all-to-all(f32[32,8,128]{2,1,0:T(8,128)S(1)} %shard_map.134), channel_id=1, replica_groups={{0,4,8,12,16,20,24,28,1,5,9,13,17,21,25,29,2,6,10,14,18,22,26,30,3,7,11..., dimensions={0} | all-to-all | bytes 262144 | tf_op jit(solution)/shard_map/all_to_all | solution.py:332
  153.7 0.5 shard_map.135
  154.2 12.3 %all_to_all.77.recv_ref = f32[16,8,128]{2,1,0:T(8,128)S(1)} all-to-all(f32[16,8,128]{2,1,0:T(8,128)S(1)} %shard_map.135), channel_id=1, replica_groups=mesh['group'=16,'sub'=32] {'group'}, dimensions={0} | all-to-all | bytes 131072 | tf_op jit(solution)/shard_map/all_to_all | solution.py:332
  166.5 0.9 shard_map.136
  167.4 13.4 %all_to_all.78.recv_ref = f32[32,16,128]{2,1,0:T(8,128)S(1)} all-to-all(f32[32,16,128]{2,1,0:T(8,128)S(1)} %get-tuple-element.45), channel_id=1, replica_groups={{0,4,8,12,16,20,24,28,1,5,9,13,17,21,25,29,2,6,10,14,18,22,26,30,3,7,11..., dimensions={0} | all-to-all | bytes 524288 | tf_op jit(solution)/shard_map/all_to_all | solution.py:332
  180.8 1.0 shard_map.137
  181.8 12.9 %all_to_all.79.recv_ref = f32[16,4,128]{2,1,0:T(4,128)S(1)} all-to-all(f32[16,4,128]{2,1,0:T(4,128)S(1)} %get-tuple-element.48), channel_id=1, replica_groups=mesh['group'=16,'sub'=32] {'group'}, dimensions={0} | all-to-all | bytes 65536 | tf_op jit(solution)/shard_map/all_to_all | solution.py:332
  194.7 13.1 %all_to_all.80.recv_ref = f32[32,4,128]{2,1,0:T(4,128)S(1)} all-to-all(f32[32,4,128]{2,1,0:T(4,128)S(1)} %shard_map.138), channel_id=1, replica_groups={{0,4,8,12,16,20,24,28,1,5,9,13,17,21,25,29,2,6,10,14,18,22,26,30,3,7,11..., dimensions={0} | all-to-all | bytes 131072 | tf_op jit(solution)/shard_map/all_to_all | solution.py:332
  207.8 0.9 shard_map.139
  (3 shorter events, 0.1 us)
Async XLA Ops:
  2.6 10.3 %copy-start.4 = (s32[1,256]{1,0:T(1,128)S(1)}, s32[1,256]{1,0:T(1,128)}, u32[]{:S(2)}) copy-start(s32[1,256]{1,0:T(1,128)} %faces_ref.1) | copy-start | bytes 3076
  2.6 10.3 %copy-start.5 = (s32[1,256]{1,0:T(1,128)S(1)}, s32[1,256]{1,0:T(1,128)}, u32[]{:S(2)}) copy-start(s32[1,256]{1,0:T(1,128)} %lands_ref.1) | copy-start | bytes 3076
  2.6 10.3 %copy-start.6 = (f32[1,256]{1,0:T(1,128)S(1)}, f32[1,256]{1,0:T(1,128)}, u32[]{:S(2)}) copy-start(f32[1,256]{1,0:T(1,128)} %weight_ref.1) | copy-start | bytes 3076
  2.6 10.3 %copy-start.7 = (s32[1,32]{1,0:T(1,128)S(1)}, s32[1,32]{1,0:T(1,128)}, u32[]{:S(2)}) copy-start(s32[1,32]{1,0:T(1,128)} %counts_ref.1) | copy-start | bytes 388
  2.6 18.2 %all-to-all-start = ((f32[16,8,128]{2,1,0:T(8,128)}), f32[16,8,128]{2,1,0:T(8,128)S(1)}, u32[]{:S(2)}, u32[]{:S(2)}) async-start(f32[16,8,128]{2,1,0:T(8,128)} %shard_map.122), calls=%async_computation | async-start | bytes 131072 | tf_op jit(solution)/shard_map/all_to_all | solution.py:332
  21.5 11.4 %copy-start.3 = (s32[8,8]{1,0:T(8,128)S(1)}, s32[8,8]{1,0:T(8,128)}, u32[]{:S(2)}) copy-start(s32[8,8]{1,0:T(8,128)} %cols_ref.1) | copy-start | bytes 772
  21.5 20.6 %all-to-all-start.1 = ((f32[32,8,128]{2,1,0:T(8,128)}), f32[32,8,128]{2,1,0:T(8,128)S(1)}, u32[]{:S(2)}, u32[]{:S(2)}) async-start(f32[32,8,128]{2,1,0:T(8,128)} %shard_map.124), calls=%async_computation.1 | async-start | bytes 262144 | tf_op jit(solution)/shard_map/all_to_all | solution.py:332
  33.0 9.1 %copy-start.1 = (f32[64,2048]{1,0:T(8,128)S(1)}, f32[64,2048]{1,0:T(8,128)}, u32[]{:S(2)}) copy-start(f32[64,2048]{1,0:T(8,128)} %inverse_ref.4) | copy-start | bytes 1572868
  43.2 13.2 %all-to-all-start.2 = ((f32[16,8,128]{2,1,0:T(8,128)}), f32[16,8,128]{2,1,0:T(8,128)S(1)}, u32[]{:S(2)}, u32[]{:S(2)}) async-start(f32[16,8,128]{2,1,0:T(8,128)} %shard_map.126), calls=%async_computation.2 | async-start | bytes 131072 | tf_op jit(solution)/shard_map/all_to_all | solution.py:332
  48.6 7.8 %copy-start = (f32[512,128]{1,0:T(8,128)S(1)}, f32[512,128]{1,0:T(8,128)}, u32[]{:S(2)}) copy-start(f32[512,128]{1,0:T(8,128)} %right_ref.11) | copy-start | bytes 786436
  48.6 7.8 %copy-start.2 = (f32[64,512]{1,0:T(8,128)S(1)}, f32[64,512]{1,0:T(8,128)}, u32[]{:S(2)}) copy-start(f32[64,512]{1,0:T(8,128)} %basis_ref.11) | copy-start | bytes 393220

commit v5 on v4

--- a/solution.py
+++ b/solution.py
@@ -110,11 +110,10 @@
     return jnp.concatenate([times(smoother_ref[b, :], field_ref[b, :]) for b in blocks], axis=0)
 
 
-def k_first(right_ref, basis_ref, msg_ref):
+def k_first(
+    right_ref, basis_ref, faces_ref, lands_ref, counts_ref, weight_ref, msg_ref, rows_ref, columns_ref
+):
     msg_ref[...] = pack(times(basis_ref[...], right_ref[...]), jnp.zeros((8, RHS), F32))
-
-
-def k_slots(faces_ref, lands_ref, counts_ref, weight_ref, factor_ref, rows_ref, columns_ref, gram_ref):
     peer = lax.broadcasted_iota(jnp.int32, (N_SUB, SLOTS), 0)
     slot = lax.broadcasted_iota(jnp.int32, (N_SUB, SLOTS), 1)
     spread = one_hot(slot // 8 == peer)
@@ -128,10 +127,6 @@
     rows = jnp.where(index == 1, lands_ref[...].astype(F32), rows)
     rows_ref[...] = rows
     columns_ref[...] = jnp.concatenate([rows, jnp.zeros((120, SLOTS), F32)], axis=0).T
-    for b in range(ROWS // LF):
-        at = slice(b * LF, (b + 1) * LF)
-        block = factor_ref[at, :]
-        gram_ref[at, :] = times(block.T, block)
 
 
 def k_setup(cols_ref, values_ref, mass_ref, blocks_ref, base_ref, dense_ref):
@@ -192,7 +187,7 @@
     msg_ref[...] = jnp.broadcast_to(tile[None], MSG_GROUP)
 
 
-def k_finish(recv_ref, rows_ref, columns_ref, base_ref, blocks_ref, gram_ref, matrix_ref, smoother_ref):
+def k_finish(recv_ref, rows_ref, columns_ref, base_ref, blocks_ref, factor_ref, matrix_ref, smoother_ref):
     lane = lax.broadcasted_iota(jnp.int32, (SLOTS, 128), 1)
     got = jnp.concatenate([recv_ref[at] for at in PLACE], axis=0)
     got = jnp.where(lane == 127, got, 0.0)
@@ -206,7 +201,8 @@
     for b in range(ROWS // LF):
         at = slice(b * LF, (b + 1) * LF)
         matrix_ref[at, at] = jnp.where(index, diag[at], 0.0) - blocks_ref[at, at]
-        smoother_ref[at, :] = gram_ref[at, :] + jnp.where(index, 1.0 / diag[at], 0.0)
+        factor = factor_ref[at, :]
+        smoother_ref[at, :] = times(factor.T, factor) + jnp.where(index, 1.0 / diag[at], 0.0)
 
 
 def k_start(recv_ref, right_ref, smoother_ref, basis_ref, columns_ref, z_ref, msg_ref):
@@ -349,17 +345,17 @@
     tile = ((8, RHS), F32)
     to_group, to_sub, to_face = (MSG_GROUP, F32), (MSG_SUB, F32), (MSG_FACE, F32)
 
-    part = swap(call(k_first, to_group, Far(right_side), Far(basis)), "group")
-    rows, columns, gram = call(
-        k_slots,
-        [((8, SLOTS), F32), ((SLOTS, 128), F32), vec],
-        face_rows,
-        land_rows,
-        face_counts,
-        face_weight,
-        Far(local_factor),
-        far=(2,),
-    )
+    part, rows, columns = call(
+        k_first,
+        [to_group, ((8, SLOTS), F32), ((SLOTS, 128), F32)],
+        Far(right_side),
+        Far(basis),
+        Far(face_rows),
+        Far(land_rows),
+        Far(face_counts),
+        Far(face_weight),
+    )
+    part = swap(part, "group")
     whole = swap(call(k_gather_first, to_sub, part, columns), "sub")
     blocks, base = call(
         k_setup,
@@ -381,7 +377,7 @@
         columns,
         Far(base),
         Far(blocks),
-        Far(gram),
+        Far(local_factor),
     )
 
     def coarse(msg):

time: 210 us -> 209 us (level)
  blocking collectives: 144 us -> 161 us
  starting transfers between devices: 27.1 us -> 17.5 us
  waiting for transfers between devices: 17.3 us -> 11.4 us
  Pallas kernels: 19.5 us -> 17.1 us
    all_to_all x11 -> x12, blocking collectives: 144 us -> 161 us  [swap(): lax.all_to_all(x, axis, split_axis=0, concat_axis=0, tiled=True, axis_ind...]
    all_to_all x3 -> x2, starting transfers between devices: 27.1 us -> 17.5 us  [swap(): lax.all_to_all(x, axis, split_axis=0, concat_axis=0, tiled=True, axis_ind...]
    all_to_all x3 -> x2, waiting for transfers between devices: 17.3 us -> 11.4 us  [swap(): lax.all_to_all(x, axis, split_axis=0, concat_axis=0, tiled=True, axis_ind...]
    pallas_call x18 -> x17, Pallas kernels: 19.5 us -> 17.1 us  [call(): pl.pallas_call(kernel, out_shape=shapes, in_specs=specs, out_specs=[pl.Bl...]
  transfers between devices with their start and end apart: 3 -> 2, of which waited for: 3 -> 2; matrix products, arithmetic and copies ran while one was open for 0% -> 0% of each run, Pallas kernels for 4% -> 3%
where the time goes in v5:
time: 209 us; the launch traced here: 208 us
  blocking collectives  161 us (77%)
  starting transfers between devices  17.5 us (8%)
  Pallas kernels  17.1 us (8%)
  waiting for transfers between devices  11.4 us (5%)
    all_to_all x12, blocking collectives, swap(): lax.all_to_all(x, axis, split_axis=0, concat_axis=0, tiled=True, axis_ind...  161 us
    all_to_all x2, starting transfers between devices, swap(): lax.all_to_all(x, axis, split_axis=0, concat_axis=0, tiled=True, axis_ind...  17.5 us
    pallas_call x17, Pallas kernels, call(): pl.pallas_call(kernel, out_shape=shapes, in_specs=specs, out_specs=[pl.Bl...  17.1 us
    all_to_all x2, waiting for transfers between devices, swap(): lax.all_to_all(x, axis, split_axis=0, concat_axis=0, tiled=True, axis_ind...  11.4 us
  transfers between devices with their start and end apart: 2, of which 2 were waited for; matrix products, arithmetic and copies ran while one was open for 0% of the time, Pallas kernels for 3%

profile of v5, /device:TPU:1, one launch (start us, length us, event | category | flops | bytes accessed | tf_op | source)
XLA Modules:
  0.0 207.8 jit_solution(10787372077615562806)
XLA Ops:
  0.6 1.4 shard_map.122
  2.1 17.1 %all_to_all.70.recv_ref = f32[16,8,128]{2,1,0:T(8,128)S(1)} all-to-all(f32[16,8,128]{2,1,0:T(8,128)S(1)} %get-tuple-element.26), channel_id=1, replica_groups=mesh['group'=16,'sub'=32] {'group'}, dimensions={0} | all-to-all | bytes 131072 | tf_op jit(solution)/shard_map/all_to_all | solution.py:328
  19.2 0.8 shard_map.123
  19.9 0.0 copy-start.3
  19.9 12.1 %all-to-all-start.1 = ((f32[32,8,128]{2,1,0:T(8,128)}), f32[32,8,128]{2,1,0:T(8,128)S(1)}, u32[]{:S(2)}, u32[]{:S(2)}) async-start(f32[32,8,128]{2,1,0:T(8,128)} %shard_map.123), calls=%async_computation.1 | async-start | bytes 262144 | tf_op jit(solution)/shard_map/all_to_all | solution.py:328
  32.1 0.0 copy-done.3
  32.1 0.0 copy-start.1
  32.1 3.2 %shard_map.124 = (f32[512,512]{1,0:T(8,128)}, f32[512,128]{1,0:T(8,128)}) custom-call(s32[8,8]{1,0:T(8,128)S(1)} %copy-done.3, f32[512,512]{1,0:T(8,128)} %values_ref.1, f32[1,512]{1,0:T(1,128)} %mass_ref.1), custom_call_target="tpu_custom_call" | custom-call | flops 1000000 | bytes 2361600 | tf_op jit(solution)/shard_map/pallas_call | solution.py:314
  35.3 6.0 %all-to-all-done.1.recv_ref = f32[32,8,128]{2,1,0:T(8,128)S(1)} async-done(((f32[32,8,128]{2,1,0:T(8,128)}), f32[32,8,128]{2,1,0:T(8,128)S(1)}, u32[]{:S(2)}, u32[]{:S(2)}) %all-to-all-start.1) | async-done | bytes 131104 | tf_op jit(solution)/shard_map/all_to_all | solution.py:328
  41.2 0.0 copy-done.1
  41.2 1.1 shard_map.125
  42.3 5.4 %all-to-all-start.2 = ((f32[16,8,128]{2,1,0:T(8,128)}), f32[16,8,128]{2,1,0:T(8,128)S(1)}, u32[]{:S(2)}, u32[]{:S(2)}) async-start(f32[16,8,128]{2,1,0:T(8,128)} %shard_map.125), calls=%async_computation.2 | async-start | bytes 131072 | tf_op jit(solution)/shard_map/all_to_all | solution.py:328
  47.7 0.0 copy-start
  47.7 0.0 copy-start.2
  47.7 2.4 %shard_map.126 = (f32[512,512]{1,0:T(8,128)S(1)}, f32[512,128]{1,0:T(8,128)S(1)}) custom-call(f32[32,8,128]{2,1,0:T(8,128)S(1)} %all-to-all-done.1.recv_ref, f32[8,256]{1,0:T(8,128)S(1)} %get-tuple-element.30.rows_ref, f32[256,128]{1,0:T(8,128)S(1)} %get-tuple-element.27.columns_ref, f32[512,128]{1,0:T(8,128)} %get-tuple-element.31.base_ref, ...), custom_call_target="tpu_custom_call" | custom-call | flops 1000000 | bytes 3153920 | tf_op jit(solution)/shard_map/pallas_call | solution.py:314
  50.1 5.4 %all-to-all-done.2.recv_ref = f32[16,8,128]{2,1,0:T(8,128)S(1)} async-done(((f32[16,8,128]{2,1,0:T(8,128)}), f32[16,8,128]{2,1,0:T(8,128)S(1)}, u32[]{:S(2)}, u32[]{:S(2)}) %all-to-all-start.2) | async-done | bytes 65568 | tf_op jit(solution)/shard_map/all_to_all | solution.py:328
  55.6 0.0 copy-done
  55.6 0.0 copy-done.2
  55.6 0.9 shard_map.127
  56.5 13.4 %all_to_all.71.recv_ref = f32[32,16,128]{2,1,0:T(8,128)S(1)} all-to-all(f32[32,16,128]{2,1,0:T(8,128)S(1)} %get-tuple-element.34), channel_id=1, replica_groups={{0,4,8,12,16,20,24,28,1,5,9,13,17,21,25,29,2,6,10,14,18,22,26,30,3,7,11..., dimensions={0} | all-to-all | bytes 524288 | tf_op jit(solution)/shard_map/all_to_all | solution.py:328
  69.8 1.3 shard_map.128
  71.1 13.2 %all_to_all.72.recv_ref = f32[16,8,128]{2,1,0:T(8,128)S(1)} all-to-all(f32[16,8,128]{2,1,0:T(8,128)S(1)} %get-tuple-element.37), channel_id=1, replica_groups=mesh['group'=16,'sub'=32] {'group'}, dimensions={0} | all-to-all | bytes 131072 | tf_op jit(solution)/shard_map/all_to_all | solution.py:328
  84.4 13.4 %all_to_all.73.recv_ref = f32[32,8,128]{2,1,0:T(8,128)S(1)} all-to-all(f32[32,8,128]{2,1,0:T(8,128)S(1)} %shard_map.129), channel_id=1, replica_groups={{0,4,8,12,16,20,24,28,1,5,9,13,17,21,25,29,2,6,10,14,18,22,26,30,3,7,11..., dimensions={0} | all-to-all | bytes 262144 | tf_op jit(solution)/shard_map/all_to_all | solution.py:328
  97.8 0.5 shard_map.130
  98.2 12.3 %all_to_all.74.recv_ref = f32[16,8,128]{2,1,0:T(8,128)S(1)} all-to-all(f32[16,8,128]{2,1,0:T(8,128)S(1)} %shard_map.130), channel_id=1, replica_groups=mesh['group'=16,'sub'=32] {'group'}, dimensions={0} | all-to-all | bytes 131072 | tf_op jit(solution)/shard_map/all_to_all | solution.py:328
  110.6 0.9 shard_map.131
  111.5 13.4 %all_to_all.75.recv_ref = f32[32,16,128]{2,1,0:T(8,128)S(1)} all-to-all(f32[32,16,128]{2,1,0:T(8,128)S(1)} %get-tuple-element.39), channel_id=1, replica_groups={{0,4,8,12,16,20,24,28,1,5,9,13,17,21,25,29,2,6,10,14,18,22,26,30,3,7,11..., dimensions={0} | all-to-all | bytes 524288 | tf_op jit(solution)/shard_map/all_to_all | solution.py:328
  124.9 1.3 shard_map.132
  126.2 13.2 %all_to_all.76.recv_ref = f32[16,8,128]{2,1,0:T(8,128)S(1)} all-to-all(f32[16,8,128]{2,1,0:T(8,128)S(1)} %get-tuple-element.42), channel_id=1, replica_groups=mesh['group'=16,'sub'=32] {'group'}, dimensions={0} | all-to-all | bytes 131072 | tf_op jit(solution)/shard_map/all_to_all | solution.py:328
  139.4 13.4 %all_to_all.77.recv_ref = f32[32,8,128]{2,1,0:T(8,128)S(1)} all-to-all(f32[32,8,128]{2,1,0:T(8,128)S(1)} %shard_map.133), channel_id=1, replica_groups={{0,4,8,12,16,20,24,28,1,5,9,13,17,21,25,29,2,6,10,14,18,22,26,30,3,7,11..., dimensions={0} | all-to-all | bytes 262144 | tf_op jit(solution)/shard_map/all_to_all | solution.py:328
  152.8 0.5 shard_map.134
  153.3 12.3 %all_to_all.78.recv_ref = f32[16,8,128]{2,1,0:T(8,128)S(1)} all-to-all(f32[16,8,128]{2,1,0:T(8,128)S(1)} %shard_map.134), channel_id=1, replica_groups=mesh['group'=16,'sub'=32] {'group'}, dimensions={0} | all-to-all | bytes 131072 | tf_op jit(solution)/shard_map/all_to_all | solution.py:328
  165.6 0.9 shard_map.135
  166.5 13.4 %all_to_all.79.recv_ref = f32[32,16,128]{2,1,0:T(8,128)S(1)} all-to-all(f32[32,16,128]{2,1,0:T(8,128)S(1)} %get-tuple-element.45), channel_id=1, replica_groups={{0,4,8,12,16,20,24,28,1,5,9,13,17,21,25,29,2,6,10,14,18,22,26,30,3,7,11..., dimensions={0} | all-to-all | bytes 524288 | tf_op jit(solution)/shard_map/all_to_all | solution.py:328
  179.9 1.0 shard_map.136
  180.9 12.9 %all_to_all.80.recv_ref = f32[16,4,128]{2,1,0:T(4,128)S(1)} all-to-all(f32[16,4,128]{2,1,0:T(4,128)S(1)} %get-tuple-element.48), channel_id=1, replica_groups=mesh['group'=16,'sub'=32] {'group'}, dimensions={0} | all-to-all | bytes 65536 | tf_op jit(solution)/shard_map/all_to_all | solution.py:328
  193.8 13.1 %all_to_all.81.recv_ref = f32[32,4,128]{2,1,0:T(4,128)S(1)} all-to-all(f32[32,4,128]{2,1,0:T(4,128)S(1)} %shard_map.137), channel_id=1, replica_groups={{0,4,8,12,16,20,24,28,1,5,9,13,17,21,25,29,2,6,10,14,18,22,26,30,3,7,11..., dimensions={0} | all-to-all | bytes 131072 | tf_op jit(solution)/shard_map/all_to_all | solution.py:328
  206.9 0.9 shard_map.138
  (3 shorter events, 0.1 us)
Async XLA Ops:
  19.9 12.1 %copy-start.3 = (s32[8,8]{1,0:T(8,128)S(1)}, s32[8,8]{1,0:T(8,128)}, u32[]{:S(2)}) copy-start(s32[8,8]{1,0:T(8,128)} %cols_ref.1) | copy-start | bytes 772
  19.9 21.3 %all-to-all-start.1 = ((f32[32,8,128]{2,1,0:T(8,128)}), f32[32,8,128]{2,1,0:T(8,128)S(1)}, u32[]{:S(2)}, u32[]{:S(2)}) async-start(f32[32,8,128]{2,1,0:T(8,128)} %shard_map.123), calls=%async_computation.1 | async-start | bytes 262144 | tf_op jit(solution)/shard_map/all_to_all | solution.py:328
  32.1 9.1 %copy-start.1 = (f32[64,2048]{1,0:T(8,128)S(1)}, f32[64,2048]{1,0:T(8,128)}, u32[]{:S(2)}) copy-start(f32[64,2048]{1,0:T(8,128)} %inverse_ref.4) | copy-start | bytes 1572868
  42.3 13.2 %all-to-all-start.2 = ((f32[16,8,128]{2,1,0:T(8,128)}), f32[16,8,128]{2,1,0:T(8,128)S(1)}, u32[]{:S(2)}, u32[]{:S(2)}) async-start(f32[16,8,128]{2,1,0:T(8,128)} %shard_map.125), calls=%async_computation.2 | async-start | bytes 131072 | tf_op jit(solution)/shard_map/all_to_all | solution.py:328
  47.7 7.8 %copy-start = (f32[512,128]{1,0:T(8,128)S(1)}, f32[512,128]{1,0:T(8,128)}, u32[]{:S(2)}) copy-start(f32[512,128]{1,0:T(8,128)} %right_ref.11) | copy-start | bytes 786436
  47.7 7.8 %copy-start.2 = (f32[64,512]{1,0:T(8,128)S(1)}, f32[64,512]{1,0:T(8,128)}, u32[]{:S(2)}) copy-start(f32[64,512]{1,0:T(8,128)} %basis_ref.11) | copy-start | bytes 393220

commit v6 on v5

--- a/solution.py
+++ b/solution.py
@@ -94,10 +94,10 @@
         msg_ref[at, 8:, :] = lands[peer * 8 : (peer + 1) * 8]
 
 
-def coupled_of(recv_ref, rows_ref, columns_ref):
+def arrived(recv_ref, columns_ref):
     out = jnp.concatenate([recv_ref[at, :8, :] for at in PLACE], axis=0)
     back = jnp.concatenate([recv_ref[at, 8:, :] for at in PLACE], axis=0) * columns_ref[:, 2:3]
-    return exact(place_of(rows_ref[...]), jnp.concatenate([out, back], axis=0))
+    return jnp.concatenate([out, back], axis=0)
 
 
 def coarse_of(recv_ref, basis_ref):
@@ -213,7 +213,17 @@
 
 
 def image_of(recv_ref, z_ref, matrix_ref, rows_ref, columns_ref):
-    return times(matrix_ref[...], z_ref[...]) - coupled_of(recv_ref, rows_ref, columns_ref)
+    high, mid, low = split(matrix_ref[...])
+    z = split(z_ref[...])
+    got = split(-arrived(recv_ref, columns_ref))
+    place = place_of(rows_ref[...])
+    pair = jnp.concatenate(z[:2], axis=1)
+    right = jnp.concatenate([pair, jnp.concatenate(got[:2], axis=1)], axis=0)
+    first = dot(jnp.concatenate([high, place], axis=1), right)
+    second = dot(mid, pair)
+    left = jnp.concatenate([high, low, place], axis=1)
+    third = dot(left, jnp.concatenate([z[2], z[0], got[2]], axis=0))
+    return first[:, :RHS] + (first[:, RHS:] + second[:, :RHS] + (second[:, RHS:] + third))
 
 
 def k_image0(

time: 209 us -> 209 us (level)
  no operation moved by 1% of the time
where the time goes in v6:
time: 209 us; the launch traced here: 208 us
  blocking collectives  161 us (77%)
  starting transfers between devices  17.5 us (8%)
  Pallas kernels  17.4 us (8%)
  waiting for transfers between devices  11.4 us (5%)
    all_to_all x12, blocking collectives, swap(): lax.all_to_all(x, axis, split_axis=0, concat_axis=0, tiled=True, axis_ind...  161 us
    all_to_all x2, starting transfers between devices, swap(): lax.all_to_all(x, axis, split_axis=0, concat_axis=0, tiled=True, axis_ind...  17.5 us
    pallas_call x17, Pallas kernels, call(): pl.pallas_call(kernel, out_shape=shapes, in_specs=specs, out_specs=[pl.Bl...  17.4 us
    all_to_all x2, waiting for transfers between devices, swap(): lax.all_to_all(x, axis, split_axis=0, concat_axis=0, tiled=True, axis_ind...  11.4 us
  transfers between devices with their start and end apart: 2, of which 2 were waited for; matrix products, arithmetic and copies ran while one was open for 0% of the time, Pallas kernels for 3%

profile of v6, /device:TPU:1, one launch (start us, length us, event | category | flops | bytes accessed | tf_op | source)
XLA Modules:
  0.0 208.1 jit_solution(12358774793357008864)
XLA Ops:
  0.6 1.4 shard_map.122
  2.1 17.1 %all_to_all.70.recv_ref = f32[16,8,128]{2,1,0:T(8,128)S(1)} all-to-all(f32[16,8,128]{2,1,0:T(8,128)S(1)} %get-tuple-element.26), channel_id=1, replica_groups=mesh['group'=16,'sub'=32] {'group'}, dimensions={0} | all-to-all | bytes 131072 | tf_op jit(solution)/shard_map/all_to_all | solution.py:338
  19.2 0.8 shard_map.123
  19.9 0.0 copy-start.3
  19.9 12.1 %all-to-all-start.1 = ((f32[32,8,128]{2,1,0:T(8,128)}), f32[32,8,128]{2,1,0:T(8,128)S(1)}, u32[]{:S(2)}, u32[]{:S(2)}) async-start(f32[32,8,128]{2,1,0:T(8,128)} %shard_map.123), calls=%async_computation.1 | async-start | bytes 262144 | tf_op jit(solution)/shard_map/all_to_all | solution.py:338
  32.1 0.0 copy-done.3
  32.1 0.0 copy-start.1
  32.1 3.2 %shard_map.124 = (f32[512,512]{1,0:T(8,128)}, f32[512,128]{1,0:T(8,128)}) custom-call(s32[8,8]{1,0:T(8,128)S(1)} %copy-done.3, f32[512,512]{1,0:T(8,128)} %values_ref.1, f32[1,512]{1,0:T(1,128)} %mass_ref.1), custom_call_target="tpu_custom_call" | custom-call | flops 1000000 | bytes 2361600 | tf_op jit(solution)/shard_map/pallas_call | solution.py:324
  35.3 6.0 %all-to-all-done.1.recv_ref = f32[32,8,128]{2,1,0:T(8,128)S(1)} async-done(((f32[32,8,128]{2,1,0:T(8,128)}), f32[32,8,128]{2,1,0:T(8,128)S(1)}, u32[]{:S(2)}, u32[]{:S(2)}) %all-to-all-start.1) | async-done | bytes 131104 | tf_op jit(solution)/shard_map/all_to_all | solution.py:338
  41.2 0.0 copy-done.1
  41.2 1.1 shard_map.125
  42.3 5.4 %all-to-all-start.2 = ((f32[16,8,128]{2,1,0:T(8,128)}), f32[16,8,128]{2,1,0:T(8,128)S(1)}, u32[]{:S(2)}, u32[]{:S(2)}) async-start(f32[16,8,128]{2,1,0:T(8,128)} %shard_map.125), calls=%async_computation.2 | async-start | bytes 131072 | tf_op jit(solution)/shard_map/all_to_all | solution.py:338
  47.7 0.0 copy-start
  47.7 0.0 copy-start.2
  47.7 2.4 %shard_map.126 = (f32[512,512]{1,0:T(8,128)S(1)}, f32[512,128]{1,0:T(8,128)S(1)}) custom-call(f32[32,8,128]{2,1,0:T(8,128)S(1)} %all-to-all-done.1.recv_ref, f32[8,256]{1,0:T(8,128)S(1)} %get-tuple-element.30.rows_ref, f32[256,128]{1,0:T(8,128)S(1)} %get-tuple-element.27.columns_ref, f32[512,128]{1,0:T(8,128)} %get-tuple-element.31.base_ref, ...), custom_call_target="tpu_custom_call" | custom-call | flops 1000000 | bytes 3153920 | tf_op jit(solution)/shard_map/pallas_call | solution.py:324
  50.1 5.4 %all-to-all-done.2.recv_ref = f32[16,8,128]{2,1,0:T(8,128)S(1)} async-done(((f32[16,8,128]{2,1,0:T(8,128)}), f32[16,8,128]{2,1,0:T(8,128)S(1)}, u32[]{:S(2)}, u32[]{:S(2)}) %all-to-all-start.2) | async-done | bytes 65568 | tf_op jit(solution)/shard_map/all_to_all | solution.py:338
  55.6 0.0 copy-done
  55.6 0.0 copy-done.2
  55.6 0.9 shard_map.127
  56.5 13.4 %all_to_all.71.recv_ref = f32[32,16,128]{2,1,0:T(8,128)S(1)} all-to-all(f32[32,16,128]{2,1,0:T(8,128)S(1)} %get-tuple-element.34), channel_id=1, replica_groups={{0,4,8,12,16,20,24,28,1,5,9,13,17,21,25,29,2,6,10,14,18,22,26,30,3,7,11..., dimensions={0} | all-to-all | bytes 524288 | tf_op jit(solution)/shard_map/all_to_all | solution.py:338
  69.8 1.5 shard_map.128
  71.3 13.2 %all_to_all.72.recv_ref = f32[16,8,128]{2,1,0:T(8,128)S(1)} all-to-all(f32[16,8,128]{2,1,0:T(8,128)S(1)} %get-tuple-element.37), channel_id=1, replica_groups=mesh['group'=16,'sub'=32] {'group'}, dimensions={0} | all-to-all | bytes 131072 | tf_op jit(solution)/shard_map/all_to_all | solution.py:338
  84.6 13.4 %all_to_all.73.recv_ref = f32[32,8,128]{2,1,0:T(8,128)S(1)} all-to-all(f32[32,8,128]{2,1,0:T(8,128)S(1)} %shard_map.129), channel_id=1, replica_groups={{0,4,8,12,16,20,24,28,1,5,9,13,17,21,25,29,2,6,10,14,18,22,26,30,3,7,11..., dimensions={0} | all-to-all | bytes 262144 | tf_op jit(solution)/shard_map/all_to_all | solution.py:338
  97.9 0.5 shard_map.130
  98.4 12.3 %all_to_all.74.recv_ref = f32[16,8,128]{2,1,0:T(8,128)S(1)} all-to-all(f32[16,8,128]{2,1,0:T(8,128)S(1)} %shard_map.130), channel_id=1, replica_groups=mesh['group'=16,'sub'=32] {'group'}, dimensions={0} | all-to-all | bytes 131072 | tf_op jit(solution)/shard_map/all_to_all | solution.py:338
  110.7 0.9 shard_map.131
  111.6 13.4 %all_to_all.75.recv_ref = f32[32,16,128]{2,1,0:T(8,128)S(1)} all-to-all(f32[32,16,128]{2,1,0:T(8,128)S(1)} %get-tuple-element.39), channel_id=1, replica_groups={{0,4,8,12,16,20,24,28,1,5,9,13,17,21,25,29,2,6,10,14,18,22,26,30,3,7,11..., dimensions={0} | all-to-all | bytes 524288 | tf_op jit(solution)/shard_map/all_to_all | solution.py:338
  125.0 1.5 shard_map.132
  126.5 13.2 %all_to_all.76.recv_ref = f32[16,8,128]{2,1,0:T(8,128)S(1)} all-to-all(f32[16,8,128]{2,1,0:T(8,128)S(1)} %get-tuple-element.42), channel_id=1, replica_groups=mesh['group'=16,'sub'=32] {'group'}, dimensions={0} | all-to-all | bytes 131072 | tf_op jit(solution)/shard_map/all_to_all | solution.py:338
  139.7 13.4 %all_to_all.77.recv_ref = f32[32,8,128]{2,1,0:T(8,128)S(1)} all-to-all(f32[32,8,128]{2,1,0:T(8,128)S(1)} %shard_map.133), channel_id=1, replica_groups={{0,4,8,12,16,20,24,28,1,5,9,13,17,21,25,29,2,6,10,14,18,22,26,30,3,7,11..., dimensions={0} | all-to-all | bytes 262144 | tf_op jit(solution)/shard_map/all_to_all | solution.py:338
  153.1 0.5 shard_map.134
  153.6 12.3 %all_to_all.78.recv_ref = f32[16,8,128]{2,1,0:T(8,128)S(1)} all-to-all(f32[16,8,128]{2,1,0:T(8,128)S(1)} %shard_map.134), channel_id=1, replica_groups=mesh['group'=16,'sub'=32] {'group'}, dimensions={0} | all-to-all | bytes 131072 | tf_op jit(solution)/shard_map/all_to_all | solution.py:338
  165.9 0.9 shard_map.135
  166.8 13.4 %all_to_all.79.recv_ref = f32[32,16,128]{2,1,0:T(8,128)S(1)} all-to-all(f32[32,16,128]{2,1,0:T(8,128)S(1)} %get-tuple-element.45), channel_id=1, replica_groups={{0,4,8,12,16,20,24,28,1,5,9,13,17,21,25,29,2,6,10,14,18,22,26,30,3,7,11..., dimensions={0} | all-to-all | bytes 524288 | tf_op jit(solution)/shard_map/all_to_all | solution.py:338
  180.2 1.0 shard_map.136
  181.2 12.9 %all_to_all.80.recv_ref = f32[16,4,128]{2,1,0:T(4,128)S(1)} all-to-all(f32[16,4,128]{2,1,0:T(4,128)S(1)} %get-tuple-element.48), channel_id=1, replica_groups=mesh['group'=16,'sub'=32] {'group'}, dimensions={0} | all-to-all | bytes 65536 | tf_op jit(solution)/shard_map/all_to_all | solution.py:338
  194.1 13.1 %all_to_all.81.recv_ref = f32[32,4,128]{2,1,0:T(4,128)S(1)} all-to-all(f32[32,4,128]{2,1,0:T(4,128)S(1)} %shard_map.137), channel_id=1, replica_groups={{0,4,8,12,16,20,24,28,1,5,9,13,17,21,25,29,2,6,10,14,18,22,26,30,3,7,11..., dimensions={0} | all-to-all | bytes 131072 | tf_op jit(solution)/shard_map/all_to_all | solution.py:338
  207.2 0.9 shard_map.138
  (3 shorter events, 0.1 us)
Async XLA Ops:
  19.9 12.1 %copy-start.3 = (s32[8,8]{1,0:T(8,128)S(1)}, s32[8,8]{1,0:T(8,128)}, u32[]{:S(2)}) copy-start(s32[8,8]{1,0:T(8,128)} %cols_ref.1) | copy-start | bytes 772
  19.9 21.3 %all-to-all-start.1 = ((f32[32,8,128]{2,1,0:T(8,128)}), f32[32,8,128]{2,1,0:T(8,128)S(1)}, u32[]{:S(2)}, u32[]{:S(2)}) async-start(f32[32,8,128]{2,1,0:T(8,128)} %shard_map.123), calls=%async_computation.1 | async-start | bytes 262144 | tf_op jit(solution)/shard_map/all_to_all | solution.py:338
  32.1 9.1 %copy-start.1 = (f32[64,2048]{1,0:T(8,128)S(1)}, f32[64,2048]{1,0:T(8,128)}, u32[]{:S(2)}) copy-start(f32[64,2048]{1,0:T(8,128)} %inverse_ref.4) | copy-start | bytes 1572868
  42.3 13.2 %all-to-all-start.2 = ((f32[16,8,128]{2,1,0:T(8,128)}), f32[16,8,128]{2,1,0:T(8,128)S(1)}, u32[]{:S(2)}, u32[]{:S(2)}) async-start(f32[16,8,128]{2,1,0:T(8,128)} %shard_map.125), calls=%async_computation.2 | async-start | bytes 131072 | tf_op jit(solution)/shard_map/all_to_all | solution.py:338
  47.7 7.8 %copy-start = (f32[512,128]{1,0:T(8,128)S(1)}, f32[512,128]{1,0:T(8,128)}, u32[]{:S(2)}) copy-start(f32[512,128]{1,0:T(8,128)} %right_ref.11) | copy-start | bytes 786436
  47.7 7.8 %copy-start.2 = (f32[64,512]{1,0:T(8,128)S(1)}, f32[64,512]{1,0:T(8,128)}, u32[]{:S(2)}) copy-start(f32[64,512]{1,0:T(8,128)} %basis_ref.11) | copy-start | bytes 393220
